TPU v7x, 32 devices: a whole 2x2x4 slice. The times are simulated.
32 devices in a mesh: section: 2 (over x), dp: 16 (over z, y, core).
Axes of the slice: x: 2, y: 2, z: 4, core: 2. Of those that a mesh axis runs over, the one named last changes fastest.
Arguments:
- tokens: bfloat16 [2, 3584, 768], P(None, 'dp'), may hold values from -6 to 6
- cotangent: bfloat16 [2, 3584, 768], P(None, 'dp'), may hold values from -6 to 6
- crop_ids: int32 [2, 3584], P(None, 'dp'), may hold values from 0 to 6, as said below
- attn_weights: float32 [2, 768, 3072], P('section', 'dp')
- up_weights: float32 [2, 768, 3072], P('section', 'dp'), may hold values from -0.21875 to 0.21875
- down_weights: float32 [2, 3072, 768], P('section', 'dp'), may hold values from -0.109375 to 0.109375
- vectors: float32 [2, 12, 768], P('section', None, 'dp')
- first_attn: float32 [2, 768, 3072], P('section', 'dp'), may hold values from -0.0004272461 to 0.0004272461
- first_up: float32 [2, 768, 3072], P('section', 'dp'), may hold values from -0.0004272461 to 0.0004272461
- first_down: float32 [2, 3072, 768], P('section', 'dp'), may hold values from -0.0004272461 to 0.0004272461
- first_vectors: float32 [2, 12, 768], P('section', None, 'dp'), may hold values from -0.0012207031 to 0.0012207031
- second_attn: float32 [2, 768, 3072], P('section', 'dp'), may hold values from 7.064254e-11 to 2.8257016e-10
- second_up: float32 [2, 768, 3072], P('section', 'dp'), may hold values from 7.064254e-11 to 2.8257016e-10
- second_down: float32 [2, 3072, 768], P('section', 'dp'), may hold values from 7.064254e-11 to 2.8257016e-10
- second_vectors: float32 [2, 12, 768], P('section', None, 'dp'), may hold values from 6.3578287e-10 to 2.5431315e-09
Outputs:
- boundary: bfloat16 [2, 2, 3584, 768], P('section', None, 'dp')
- input_grads: bfloat16 [2, 2, 3584, 768], P('section', None, 'dp')
- grad_norm: float32 [], replicated
- new_attn: float32 [2, 768, 3072], P('section', 'dp')
- new_up: float32 [2, 768, 3072], P('section', 'dp')
- new_down: float32 [2, 3072, 768], P('section', 'dp')
- new_vectors: float32 [2, 12, 768], P('section', None, 'dp')
- new_first_attn: float32 [2, 768, 3072], P('section', 'dp')
- new_first_up: float32 [2, 768, 3072], P('section', 'dp')
- new_first_down: float32 [2, 3072, 768], P('section', 'dp')
- new_first_vectors: float32 [2, 12, 768], P('section', None, 'dp')
- new_second_attn: float32 [2, 768, 3072], P('section', 'dp')
- new_second_up: float32 [2, 768, 3072], P('section', 'dp')
- new_second_down: float32 [2, 3072, 768], P('section', 'dp')
- new_second_vectors: float32 [2, 12, 768], P('section', None, 'dp')
Inputs may be any that keep to these rules, and one draw needn't show every extreme that they name: `crop_ids`: within each aligned block of 224 tokens of one micro-batch, ids start at 0 and never fall; a crop is a run of equal ids, of 197 or 37 tokens, except that the last run of a block may be shorter; equal ids in different blocks are different crops.
All inputs are finite; a program needn't handle non-finite values.
Results may differ from a plain program's by a relative error of at most 0.024.
The roundings to bfloat16 on the way count: a program that leaves them out, or rounds other values in their place, can miss the bound.
Values may be sent and summed in bfloat16 or wider, within the bound.
A program may use at most 384 MiB of HBM per device.

v0:
```python
from functools import partial

import jax
import jax.numpy as jnp
from jax import lax
from jax.sharding import PartitionSpec as P

HEADS = 12
STEP = 10


LN_EPS = 1e-06
NEG_BIG = -1e30
BETA_ONE = 0.9
BETA_TWO = 0.999
RATE = 0.1
VECTOR_RATE = 0.5
DECAY_RATE = 0.01
ADAM_EPS = 1e-08
MAX_NORM = 1.0


def from_behind(block, axis, distance):
    devices = range(lax.axis_size(axis))
    route = [(i - distance, i) for i in devices if i - distance in devices]
    return lax.ppermute(block, axis, route)


def layer_norm(features, gain_row, shift_row):
    center = jnp.mean(features, axis=-1, keepdims=True)
    centered = features - center
    spread = jnp.mean(centered * centered, axis=-1, keepdims=True)
    return centered * lax.rsqrt(spread + LN_EPS) * gain_row + shift_row


def split_heads(packed, model_width):
    shaped = packed.reshape(packed.shape[0], 3, HEADS, model_width // HEADS)
    return (shaped[:, 0], shaped[:, 1], shaped[:, 2])


def attention_scores(queries, keys_block, crop_row):
    head_scale = queries.shape[-1] ** (-0.5)
    scores = (
        jnp.einsum("qhd,khd->hqk", queries, keys_block, preferred_element_type=jnp.float32)
        * head_scale
    )
    same_crop = crop_row[:, None] == crop_row[None, :]
    return jnp.where(same_crop[None], scores, NEG_BIG)


def forward_layer(inputs, crop_row, weights):
    attn, upward_w, downward_w, vectors_b = weights
    model_width = attn.shape[0]
    pack_rows = inputs.shape[0]
    params = vectors_b.astype(jnp.float32)
    hidden = layer_norm(inputs, params[0], params[1]).astype(jnp.bfloat16)
    qkv_bias = jnp.concatenate([params[2], jnp.zeros_like(params[2]), params[3]])
    packed = (
        jnp.dot(hidden, attn[:, : 3 * model_width], preferred_element_type=jnp.float32) + qkv_bias
    ).astype(jnp.bfloat16)
    queries, keys_block, values_block = split_heads(packed, model_width)
    scores = attention_scores(queries, keys_block, crop_row)
    row_peak = jnp.max(scores, axis=-1, keepdims=True)
    exponent = jnp.exp(scores - row_peak)
    totals = jnp.sum(exponent, axis=-1, keepdims=True)
    soft_weights = (exponent / totals).astype(jnp.bfloat16)
    log_total = row_peak + jnp.log(totals)
    mixed = jnp.einsum(
        "hqk,khd->qhd", soft_weights, values_block, preferred_element_type=jnp.float32
    )
    mixed = mixed.reshape(pack_rows, model_width).astype(jnp.bfloat16)
    middle = inputs + (
        jnp.dot(mixed, attn[:, 3 * model_width :], preferred_element_type=jnp.float32) + params[4]
    )
    hidden_two = layer_norm(middle, params[5], params[6]).astype(jnp.bfloat16)
    upward = jnp.dot(hidden_two, upward_w, preferred_element_type=jnp.float32) + params[8:].reshape(
        -1
    )
    active = jax.nn.gelu(upward, approximate=False).astype(jnp.bfloat16)
    output = middle + (jnp.dot(active, downward_w, preferred_element_type=jnp.float32) + params[7])
    return (output, (inputs, hidden, packed, log_total, mixed, middle, hidden_two, upward, active))


def blank_kept(pack_rows, model_width, hidden_units):
    return (
        jnp.zeros((pack_rows, model_width), jnp.float32),
        jnp.zeros((pack_rows, model_width), jnp.bfloat16),
        jnp.zeros((pack_rows, 3 * model_width), jnp.bfloat16),
        jnp.zeros((HEADS, pack_rows, 1), jnp.float32),
        jnp.zeros((pack_rows, model_width), jnp.bfloat16),
        jnp.zeros((pack_rows, model_width), jnp.float32),
        jnp.zeros((pack_rows, model_width), jnp.bfloat16),
        jnp.zeros((pack_rows, hidden_units), jnp.float32),
        jnp.zeros((pack_rows, hidden_units), jnp.bfloat16),
    )


def backward_layer(kept, crop_row, grad_out, weights):
    attn, upward_w, downward_w, vectors_b = weights
    inputs, hidden, packed, log_total, mixed, middle, hidden_two, upward, active = kept
    model_width = attn.shape[0]
    pack_rows = inputs.shape[0]
    params = vectors_b.astype(jnp.float32)
    grad_down = grad_out.astype(jnp.bfloat16)
    grad_w_down = jnp.einsum("pi,pj->ij", active, grad_down, preferred_element_type=jnp.float32)
    grad_active = jnp.einsum("pj,ij->pi", grad_down, downward_w, preferred_element_type=jnp.float32)
    gelu_back = jax.vjp(partial(jax.nn.gelu, approximate=False), upward)[1]
    grad_up = gelu_back(grad_active)[0].astype(jnp.bfloat16)
    grad_w_up = jnp.einsum("pi,pj->ij", hidden_two, grad_up, preferred_element_type=jnp.float32)
    grad_hidden_two = jnp.einsum("pj,ij->pi", grad_up, upward_w, preferred_element_type=jnp.float32)
    norm_back_two = jax.vjp(layer_norm, middle, params[5], params[6])[1]
    grad_middle_part, grad_gain_two, grad_shift_two = norm_back_two(grad_hidden_two)
    grad_middle = grad_out + grad_middle_part
    grad_branch = grad_middle.astype(jnp.bfloat16)
    grad_w_out = jnp.einsum("pi,pj->ij", mixed, grad_branch, preferred_element_type=jnp.float32)
    grad_mixed = jnp.einsum(
        "pj,ij->pi", grad_branch, attn[:, 3 * model_width :], preferred_element_type=jnp.float32
    ).astype(jnp.bfloat16)
    queries, keys_block, values_block = split_heads(packed, model_width)
    scores = attention_scores(queries, keys_block, crop_row)
    probs = jnp.exp(scores - log_total)
    grad_heads = grad_mixed.reshape(pack_rows, HEADS, model_width // HEADS)
    grad_probs = jnp.einsum(
        "qhd,khd->hqk", grad_heads, values_block, preferred_element_type=jnp.float32
    )
    grad_values = jnp.einsum(
        "hqk,qhd->khd", probs.astype(jnp.bfloat16), grad_heads, preferred_element_type=jnp.float32
    )
    grad_scores = (
        probs * (grad_probs - jnp.sum(grad_probs * probs, axis=-1, keepdims=True))
    ).astype(jnp.bfloat16)
    head_scale = queries.shape[-1] ** (-0.5)
    grad_queries = (
        jnp.einsum("hqk,khd->qhd", grad_scores, keys_block, preferred_element_type=jnp.float32)
        * head_scale
    )
    grad_keys = (
        jnp.einsum("hqk,qhd->khd", grad_scores, queries, preferred_element_type=jnp.float32)
        * head_scale
    )
    grad_packed = jnp.concatenate(
        [
            grad_queries.reshape(pack_rows, model_width),
            grad_keys.reshape(pack_rows, model_width),
            grad_values.reshape(pack_rows, model_width),
        ],
        axis=1,
    ).astype(jnp.bfloat16)
    grad_w_qkv = jnp.einsum("pi,pj->ij", hidden, grad_packed, preferred_element_type=jnp.float32)
    grad_hidden = jnp.einsum(
        "pj,ij->pi", grad_packed, attn[:, : 3 * model_width], preferred_element_type=jnp.float32
    )
    norm_back_one = jax.vjp(layer_norm, inputs, params[0], params[1])[1]
    grad_in_part, grad_gain_one, grad_shift_one = norm_back_one(grad_hidden)
    grad_inputs = grad_middle + grad_in_part
    packed_sums = jnp.sum(grad_packed, axis=0, dtype=jnp.float32)
    vector_rows = jnp.stack(
        [
            grad_gain_one,
            grad_shift_one,
            packed_sums[:model_width],
            packed_sums[2 * model_width :],
            jnp.sum(grad_branch, axis=0, dtype=jnp.float32),
            grad_gain_two,
            grad_shift_two,
            jnp.sum(grad_down, axis=0, dtype=jnp.float32),
        ]
    )
    up_bias_rows = jnp.sum(grad_up, axis=0, dtype=jnp.float32).reshape(-1, model_width)
    grad_vectors = jnp.concatenate([vector_rows, up_bias_rows], axis=0)
    grad_attn = jnp.concatenate([grad_w_qkv, grad_w_out], axis=1)
    return (grad_inputs, (grad_attn, grad_w_up, grad_w_down, grad_vectors))


def place(whole, piece, micro_slot, is_valid):
    former = lax.dynamic_index_in_dim(whole, micro_slot, 0, keepdims=False)
    return lax.dynamic_update_index_in_dim(whole, jnp.where(is_valid, piece, former), micro_slot, 0)


def adam_update(master, gradient, moment_one, moment_two, decay_rate, step_rate):
    new_one = BETA_ONE * moment_one + (1.0 - BETA_ONE) * gradient
    new_two = BETA_TWO * moment_two + (1.0 - BETA_TWO) * gradient * gradient
    ratio = (
        new_one / (1.0 - BETA_ONE**STEP) / (jnp.sqrt(new_two / (1.0 - BETA_TWO**STEP)) + ADAM_EPS)
    )
    return (master - step_rate * (ratio + decay_rate * master), new_one, new_two)


def shards(
    tokens,
    cotangent,
    crop_ids,
    attn_weights,
    up_weights,
    down_weights,
    vectors,
    first_attn,
    first_up,
    first_down,
    first_vectors,
    second_attn,
    second_up,
    second_down,
    second_vectors,
):
    section_index = lax.axis_index("section")
    micro_count = tokens.shape[0]
    pack_rows = tokens.shape[1]
    model_width = tokens.shape[2]
    weights = (
        lax.all_gather(attn_weights[0].astype(jnp.bfloat16), "dp", axis=0, tiled=True),
        lax.all_gather(up_weights[0].astype(jnp.bfloat16), "dp", axis=0, tiled=True),
        lax.all_gather(down_weights[0].astype(jnp.bfloat16), "dp", axis=0, tiled=True),
        lax.all_gather(vectors[0].astype(jnp.bfloat16), "dp", axis=1, tiled=True),
    )
    hidden_units = weights[1].shape[1]
    received = jnp.zeros((pack_rows, model_width), jnp.bfloat16)
    saved_inputs = jnp.zeros((micro_count, pack_rows, model_width), jnp.bfloat16)
    boundary = jnp.zeros((micro_count, pack_rows, model_width), jnp.bfloat16)
    for tick_number in range(micro_count + 1):
        position = tick_number - section_index
        is_valid = (position >= 0) & (position < micro_count)
        micro_slot = jnp.clip(position, 0, micro_count - 1)
        own_tokens = lax.dynamic_index_in_dim(tokens, micro_slot, 0, keepdims=False)
        layer_input = jnp.where(section_index == 0, own_tokens, received)
        crop_row = lax.dynamic_index_in_dim(crop_ids, micro_slot, 0, keepdims=False)

        def run_layer():
            return forward_layer(layer_input.astype(jnp.float32), crop_row, weights)

        def skip_layer():
            return (
                jnp.zeros((pack_rows, model_width), jnp.float32),
                blank_kept(pack_rows, model_width, hidden_units),
            )

        output, kept = lax.cond(is_valid, run_layer, skip_layer)
        sent = output.astype(jnp.bfloat16)
        saved_inputs = place(saved_inputs, layer_input, micro_slot, is_valid)
        boundary = place(boundary, sent, micro_slot, is_valid)
        if tick_number < micro_count:
            received = from_behind(sent, "section", 1)
    zero_grads = tuple((jnp.zeros(piece.shape, jnp.float32) for piece in weights))
    totals = zero_grads
    reduced = None
    back_received = jnp.zeros((pack_rows, model_width), jnp.bfloat16)
    input_grads = jnp.zeros((micro_count, pack_rows, model_width), jnp.bfloat16)
    for tick_number in range(micro_count + 1):
        position = tick_number - (1 - section_index)
        is_valid = (position >= 0) & (position < micro_count)
        micro_slot = jnp.clip(position, 0, micro_count - 1)
        own_grad = lax.dynamic_index_in_dim(cotangent, micro_slot, 0, keepdims=False)
        grad_out = jnp.where(section_index == 1, own_grad, back_received).astype(jnp.float32)
        crop_row = lax.dynamic_index_in_dim(crop_ids, micro_slot, 0, keepdims=False)

        def run_back():
            layer_input = lax.dynamic_index_in_dim(saved_inputs, micro_slot, 0, keepdims=False)
            kept = forward_layer(layer_input.astype(jnp.float32), crop_row, weights)[1]
            return backward_layer(kept, crop_row, grad_out, weights)

        def skip_back():
            return (jnp.zeros((pack_rows, model_width), jnp.float32), zero_grads)

        grad_inputs, grads = lax.cond(is_valid, run_back, skip_back)
        sent = grad_inputs.astype(jnp.bfloat16)
        input_grads = place(input_grads, sent, micro_slot, is_valid)
        if tick_number < micro_count:
            back_received = from_behind(sent, "section", -1)
        totals = jax.tree.map(jnp.add, totals, grads)
    reduced = (
        lax.psum_scatter(totals[0], "dp", scatter_dimension=0, tiled=True),
        lax.psum_scatter(totals[1], "dp", scatter_dimension=0, tiled=True),
        lax.psum_scatter(totals[2], "dp", scatter_dimension=0, tiled=True),
        lax.psum_scatter(totals[3], "dp", scatter_dimension=1, tiled=True),
    )
    squares = sum_squares(reduced)
    grad_norm = jnp.sqrt(lax.psum(squares, ("section", "dp")))
    clip_factor = jnp.minimum(1.0, MAX_NORM / (grad_norm + 1e-06))
    masters = (attn_weights, up_weights, down_weights, vectors)
    firsts = (first_attn, first_up, first_down, first_vectors)
    seconds = (second_attn, second_up, second_down, second_vectors)
    decays = (DECAY_RATE, DECAY_RATE, DECAY_RATE, 0.0)
    rates = (RATE, RATE, RATE, VECTOR_RATE)
    updated = [
        adam_update(
            master[0], gradient * clip_factor, moment_one[0], moment_two[0], decay_rate, step_rate
        )
        for master, gradient, moment_one, moment_two, decay_rate, step_rate in zip(
            masters, reduced, firsts, seconds, decays, rates
        )
    ]
    new_masters = tuple((entry[0][None] for entry in updated))
    new_firsts = tuple((entry[1][None] for entry in updated))
    new_seconds = tuple((entry[2][None] for entry in updated))
    return (boundary[None], input_grads[None], grad_norm) + new_masters + new_firsts + new_seconds


def sum_squares(arrays):
    running = jnp.zeros((), jnp.float32)
    for member in arrays:
        running = running + jnp.sum(member * member)
    return running


def solution(mesh):
    return jax.shard_map(
        shards,
        mesh=mesh,
        in_specs=(
            P(None, "dp", None),
            P(None, "dp", None),
            P(None, "dp"),
            P("section", "dp", None),
            P("section", "dp", None),
            P("section", "dp", None),
            P("section", None, "dp"),
            P("section", "dp", None),
            P("section", "dp", None),
            P("section", "dp", None),
            P("section", None, "dp"),
            P("section", "dp", None),
            P("section", "dp", None),
            P("section", "dp", None),
            P("section", None, "dp"),
        ),
        out_specs=(
            P("section", None, "dp", None),
            P("section", None, "dp", None),
            P(),
            P("section", "dp", None),
            P("section", "dp", None),
            P("section", "dp", None),
            P("section", None, "dp"),
            P("section", "dp", None),
            P("section", "dp", None),
            P("section", "dp", None),
            P("section", None, "dp"),
            P("section", "dp", None),
            P("section", "dp", None),
            P("section", "dp", None),
            P("section", None, "dp"),
        ),
        check_vma=False,
    )
```

profile of v0, /device:TPU:0, one launch (start us, length us, event | category | flops | bytes accessed | tf_op | source)
XLA Modules:
  0.0 971.1 jit_solution(582120427396488637)
XLA Ops:
  12.0 23.6 %all-gather = bf16[16,48,12]{1,2,0:T(8,128)(2,1)S(1)} all-gather(bf16[1,48,12]{1,2,0:T(8,128)(2,1)S(1)} %bitcast.656), channel_id=1, replica_groups=mesh['section'=2,'dp'=16] {'dp'}, dimensions={0}, use_global_device_ids=true | all-gather | bytes 19584 | tf_op jit(solution)/shard_map/all_gather | solution.py:214
  35.8 31.3 %all-gather.5.cloned.1.call-done = bf16[768,3072]{1,0:T(8,128)(2,1)} async-done(((bf16[48,3072]{1,0:T(8,128)(2,1)}), bf16[768,3072]{1,0:T(8,128)(2,1)}) %all-gather.5.cloned.1.call-update) | async-done | bytes 4718608 | tf_op jit(solution)/shard_map/all_gather | solution.py:211
  67.1 54.8 %all-gather.7.cloned.1.call-done = bf16[768,3072]{1,0:T(8,128)(2,1)} async-done(((bf16[48,3072]{1,0:T(8,128)(2,1)}), bf16[768,3072]{1,0:T(8,128)(2,1)}) %all-gather.7.cloned.1.call-update) | async-done | bytes 4718608 | tf_op jit(solution)/shard_map/all_gather | solution.py:212
  121.9 54.8 %all-gather.9.cloned.1.call-done = bf16[3072,768]{1,0:T(8,128)(2,1)} async-done(((bf16[192,768]{1,0:T(8,128)(2,1)}), bf16[3072,768]{1,0:T(8,128)(2,1)}) %all-gather.9.cloned.1.call-update) | async-done | bytes 4718608 | tf_op jit(solution)/shard_map/all_gather | solution.py:213
  176.9 25.5 %conditional.6 = (bf16[224,768]{1,0:T(8,128)(2,1)S(1)}) conditional(s32[]{:T(128)} %convert_element_type.510, () %tuple.80, (bf16[1,224,768]{2,1,0:T(8,128)(2,1)S(1)}, pred[224,768]{1,0:T(8,128)(4,1)S(1)}, bf16[224,768]{1,0:T(8,128)(2,1)S(1)}, bf16[12,768]{1,0:T(8,128)(2,1)S(1)}, bf16[768,3072]{1,0:T(8,128)(2,1)}, /*index=5*/s32[2,224]{1,0:T(2,128)S(1)}, ...), branch_computations={%region_0.1_spmd, %region_1.8_spmd} | conditional | flops 3459028992 | bytes 24859024 | solution.py:237
  190.3 11.9 %fusion.28 = bf16[224,768]{1,0:T(8,128)(2,1)S(1)} fusion(f32[224,768]{1,0:T(8,128)S(1)} %get-tuple-element.530, bf16[3072,768]{1,0:T(8,128)(2,1)} %get-tuple-element.291, f32[3072]{0:T(1024)S(1)} %add.702, bf16[768,3072]{1,0:T(8,128)(2,1)} %get-tuple-element.290, f32[768]{0:T(1024)S(1)} %get-tuple-element.443, f32[768]{0:T(1024)S(1)} %get-tuple-element.444, ...), kind=kOutput, calls=%fused_computation.38 | convolution fusion | flops 2160721920 | bytes 10492672 | tf_op jit(solution)/shard_map/cond/branch_1_fun/dot_general | solution.py:80
  211.9 24.6 %conditional.7 = (bf16[224,768]{1,0:T(8,128)(2,1)S(1)}) conditional(s32[]{:T(128)} %convert_element_type.515, () %tuple.82, (bf16[224,768]{1,0:T(8,128)(2,1)S(1)}, bf16[12,768]{1,0:T(8,128)(2,1)S(1)}, bf16[768,3072]{1,0:T(8,128)(2,1)}, s32[2,224]{1,0:T(2,128)S(1)}, s32[]{:T(128)}, /*index=5*/bf16[768,3072]{1,0:T(8,128)(2,1)}, ...), branch_computations={%region_8.9_spmd, %region_9.16_spmd} | conditional | flops 3458856960 | bytes 28078508 | solution.py:237
  224.6 11.9 %fusion.117 = bf16[224,768]{1,0:T(8,128)(2,1)S(1)} fusion(f32[224,768]{1,0:T(8,128)S(1)} %get-tuple-element.526, bf16[3072,768]{1,0:T(8,128)(2,1)} %get-tuple-element.298, f32[3072]{0:T(1024)S(1)} %add.723, bf16[768,3072]{1,0:T(8,128)(2,1)} %get-tuple-element.297, f32[768]{0:T(1024)S(1)} %get-tuple-element.451, f32[768]{0:T(1024)S(1)} %get-tuple-element.452, ...), kind=kOutput, calls=%fused_computation.151 | convolution fusion | flops 2160721920 | bytes 10492672 | tf_op jit(solution)/shard_map/cond/branch_1_fun/dot_general | solution.py:80
  249.2 31.4 %conditional.9 = (f32[768,3072]{1,0:T(8,128)}, f32[768,3072]{1,0:T(8,128)}, f32[3072,768]{1,0:T(8,128)}, f32[12,768]{1,0:T(8,128)S(1)}, bf16[224,768]{1,0:T(8,128)(2,1)}) conditional(s32[]{:T(128)} %convert_element_type.517, () %tuple.86, (s32[]{:T(128)}, bf16[2,224,768]{2,1,0:T(8,128)(2,1)S(1)}, bf16[12,768]{1,0:T(8,128)(2,1)S(1)}, ...), branch_computations={%region_24.25_spmd, %region_25.45_spmd.clone.clone} | conditional | flops 9054476288 | bytes 222168480 | solution.py:264
  281.9 53.9 %collective-permute-done.2 = bf16[224,768]{1,0:T(8,128)(2,1)S(1)} collective-permute-done((bf16[224,768]{1,0:T(8,128)(2,1)}, bf16[224,768]{1,0:T(8,128)(2,1)S(1)}, u32[]{:S(2)}, u32[]{:S(2)}) %collective-permute-start.2) | collective-permute-done | bytes 344096 | tf_op jit(solution)/shard_map/ppermute | solution.py:26
  337.7 75.7 %conditional.10 = (f32[768,3072]{1,0:T(8,128)}, f32[768,3072]{1,0:T(8,128)}, f32[3072,768]{1,0:T(8,128)}, f32[12,768]{1,0:T(8,128)S(1)}, bf16[224,768]{1,0:T(8,128)(2,1)}) conditional(s32[]{:T(128)} %convert_element_type.520, () %tuple.88, (s32[]{:T(128)}, bf16[2,224,768]{2,1,0:T(8,128)(2,1)S(1)}, bf16[12,768]{1,0:T(8,128)(2,1)S(1)}, ...), branch_computations={%region_45.46_spmd, %region_46.66_spmd} | conditional | flops 9054476288 | bytes 219760000 | solution.py:264
  354.9 11.1 %convert_reduce_fusion.3 = (f32[3072]{0:T(1024)}, bf16[224,3072]{1,0:T(8,128)(2,1)S(1)}) fusion(f32[224,3072]{1,0:T(8,128)S(1)} %convolution_add_fusion.10, bf16[3072,768]{1,0:T(8,128)(2,1)} %get-tuple-element.321, f32[224,768]{1,0:T(8,128)S(1)} %copy-done.2), kind=kOutput, calls=%fused_computation.346 | convolution fusion | flops 1108055040 | bytes 9547776 | tf_op jit(solution)/shard_map/cond/branch_1_fun/pj,ij->pi/dot_general | solution.py:106
  402.4 10.9 %fusion.281 = f32[3072,768]{1,0:T(8,128)} fusion(f32[224,3072]{1,0:T(8,128)} %copy-done.113, f32[224,768]{1,0:T(8,128)S(1)} %copy-done.3), kind=kOutput, calls=%fused_computation.372 | convolution fusion | flops 1101864960 | bytes 12877824 | tf_op jit(solution)/shard_map/cond/branch_1_fun/pi,pj->ij/dot_general | solution.py:105
  414.6 9.0 collective-permute-done.3
  425.5 80.7 %conditional.11 = (f32[768,3072]{1,0:T(8,128)}, f32[768,3072]{1,0:T(8,128)}, f32[3072,768]{1,0:T(8,128)}, f32[12,768]{1,0:T(8,128)S(1)}, bf16[224,768]{1,0:T(8,128)(2,1)}) conditional(s32[]{:T(128)} %convert_element_type.522, () %tuple.90, (s32[]{:T(128)}, bf16[2,224,768]{2,1,0:T(8,128)(2,1)S(1)}, bf16[12,768]{1,0:T(8,128)(2,1)S(1)}, ...), branch_computations={%region_66.67_spmd, %region_67.87_spmd} | conditional | flops 9054476288 | bytes 219991744 | solution.py:264
  444.9 11.0 %convert_reduce_fusion.8 = (f32[3072]{0:T(1024)}, bf16[224,3072]{1,0:T(8,128)(2,1)S(1)}) fusion(f32[224,3072]{1,0:T(8,128)S(1)} %convolution_add_fusion.13, bf16[3072,768]{1,0:T(8,128)(2,1)} %get-tuple-element.329, f32[224,768]{1,0:T(8,128)S(1)} %copy-done), kind=kOutput, calls=%fused_computation.454 | convolution fusion | flops 1108055040 | bytes 9547776 | tf_op jit(solution)/shard_map/cond/branch_1_fun/pj,ij->pi/dot_general | solution.py:106
  494.5 11.2 %fusion.336 = f32[3072,768]{1,0:T(8,128)} fusion(f32[224,3072]{1,0:T(8,128)} %copy-done.114, f32[224,768]{1,0:T(8,128)S(1)} %copy-done.1), kind=kOutput, calls=%fused_computation.480 | convolution fusion | flops 1101864960 | bytes 12877824 | tf_op jit(solution)/shard_map/cond/branch_1_fun/pi,pj->ij/dot_general | solution.py:105
  508.7 15.0 %add_add_fusion.9 = f32[768,3072]{1,0:T(8,128)} fusion(f32[768,3072]{1,0:T(8,128)} %get-tuple-element.368, f32[768,3072]{1,0:T(8,128)} %get-tuple-element.366, f32[768,3072]{1,0:T(8,128)} %get-tuple-element.367), kind=kLoop, calls=%fused_computation.663 | loop fusion | flops 4718592 | bytes 37748736 | tf_op jit(solution)/shard_map/add | solution.py:269
  523.7 14.8 %add_add_fusion.10 = f32[768,3072]{1,0:T(8,128)} fusion(f32[768,3072]{1,0:T(8,128)} %get-tuple-element.365, f32[768,3072]{1,0:T(8,128)} %get-tuple-element.363, f32[768,3072]{1,0:T(8,128)} %get-tuple-element.364), kind=kLoop, calls=%fused_computation.664 | loop fusion | flops 4718592 | bytes 37748736 | tf_op jit(solution)/shard_map/add | solution.py:269
  538.6 13.9 %add_add_fusion.8 = f32[3072,768]{1,0:T(8,128)} fusion(f32[3072,768]{1,0:T(8,128)} %get-tuple-element.371, f32[3072,768]{1,0:T(8,128)} %get-tuple-element.369, f32[3072,768]{1,0:T(8,128)} %get-tuple-element.370), kind=kLoop, calls=%fused_computation.662 | loop fusion | flops 4718592 | bytes 37748736 | tf_op jit(solution)/shard_map/add | solution.py:269
  563.5 113.5 %reduce-scatter.9.cloned.1.call-done = f32[48,3072]{1,0:T(8,128)} async-done(((f32[768,3072]{1,0:T(8,128)}), f32[48,3072]{1,0:T(8,128)}) %reduce-scatter.9.cloned.1.call-update) | async-done | bytes 589840 | tf_op jit(solution)/shard_map/reduce_scatter | solution.py:272
  678.8 113.3 %reduce-scatter.7.cloned.1.call-done = f32[48,3072]{1,0:T(8,128)} async-done(((f32[768,3072]{1,0:T(8,128)}), f32[48,3072]{1,0:T(8,128)}) %reduce-scatter.7.cloned.1.call-update) | async-done | bytes 589840 | tf_op jit(solution)/shard_map/reduce_scatter | solution.py:271
  795.2 112.7 %reduce-scatter.11.cloned.1.call-done = f32[192,768]{1,0:T(8,128)} async-done(((f32[3072,768]{1,0:T(8,128)}), f32[192,768]{1,0:T(8,128)}) %reduce-scatter.11.cloned.1.call-update) | async-done | bytes 589840 | tf_op jit(solution)/shard_map/reduce_scatter | solution.py:273
  912.1 41.3 %psum.7 = f32[]{:T(128)} all-reduce(f32[]{:T(128)S(6)} %add.854), channel_id=1, replica_groups=mesh['section'=2,'dp'=16] {'section','dp'}, use_global_device_ids=true, to_apply=%region_95.96 | all-reduce | flops 1 | bytes 8 | tf_op jit(solution)/shard_map/psum | solution.py:277
  (419 shorter events, 213.0 us)
Async XLA Ops:
  7.2 28.5 %copy-start.52 = (bf16[2,224,768]{2,1,0:T(8,128)(2,1)S(1)}, bf16[2,224,768]{2,1,0:T(8,128)(2,1)}, u32[]{:S(2)}) copy-start(bf16[2,224,768]{2,1,0:T(8,128)(2,1)} %param.27) | copy-start | bytes 2064388
  7.2 59.9 %all-gather.5.cloned.1.call-start = ((), (), s32[]{:S(2)}) async-start(), calls=%async_computation.4 | async-start | bytes 5013504 | tf_op jit(solution)/shard_map/all_gather | solution.py:211
  9.2 167.7 %copy-start.87 = (s32[2,224]{1,0:T(2,128)S(1)}, s32[2,224]{1,0:T(2,128)}, u32[]{:S(2)}) copy-start(s32[2,224]{1,0:T(2,128)} %param.29) | copy-start | bytes 5380
  9.2 112.8 %all-gather.7.cloned.1.call-start = ((), (), s32[]{:S(2)}) async-start(), calls=%async_computation.5 | async-start | bytes 5013504 | tf_op jit(solution)/shard_map/all_gather | solution.py:212
  11.1 165.7 %all-gather.9.cloned.1.call-start = ((), (), s32[]{:S(2)}) async-start(), calls=%async_computation.6 | async-start | bytes 5013504 | tf_op jit(solution)/shard_map/all_gather | solution.py:213
  11.9 550.2 %reduce-scatter.13.cloned.1.call-start = ((), (), s32[]{:S(2)}) async-start(), calls=%async_computation.10 | async-start | bytes 417792
  202.4 9.3 collective-permute-start
  236.6 11.8 %collective-permute-start.1 = (bf16[224,768]{1,0:T(8,128)(2,1)S(1)}, bf16[224,768]{1,0:T(8,128)(2,1)S(1)}, u32[]{:S(2)}, u32[]{:S(2)}) collective-permute-start(bf16[224,768]{1,0:T(8,128)(2,1)S(1)} %get-tuple-element.625), channel_id=1, source_target_pairs={{0,16},{1,17},{2,18},{3,19},{4,20},{5,21},{6,22},{7,23},{8,24},{9,... | collective-permute-start | bytes 1032200 | tf_op jit(solution)/shard_map/ppermute | solution.py:26
  280.6 57.0 %copy-start.77 = (f32[12,768]{1,0:T(8,128)}, f32[12,768]{1,0:T(8,128)S(1)}, u32[]{:S(2)}) copy-start(f32[12,768]{1,0:T(8,128)S(1)} %get-tuple-element.372) | copy-start | bytes 110596
  280.6 55.2 %collective-permute-start.2 = (bf16[224,768]{1,0:T(8,128)(2,1)}, bf16[224,768]{1,0:T(8,128)(2,1)S(1)}, u32[]{:S(2)}, u32[]{:S(2)}) collective-permute-start(bf16[224,768]{1,0:T(8,128)(2,1)} %get-tuple-element.360), channel_id=1, source_target_pairs={{16,0},{17,1},{18,2},{19,3},{20,4},{21,5},{22,6},{23,7},{24,8},{25... | collective-permute-start | bytes 1032200 | tf_op jit(solution)/shard_map/ppermute | solution.py:26
  413.3 10.3 %collective-permute-start.3 = (bf16[224,768]{1,0:T(8,128)(2,1)}, bf16[224,768]{1,0:T(8,128)(2,1)S(1)}, u32[]{:S(2)}, u32[]{:S(2)}) collective-permute-start(bf16[224,768]{1,0:T(8,128)(2,1)} %get-tuple-element.361), channel_id=1, source_target_pairs={{16,0},{17,1},{18,2},{19,3},{20,4},{21,5},{22,6},{23,7},{24,8},{25... | collective-permute-start | bytes 1032200 | tf_op jit(solution)/shard_map/ppermute | solution.py:26
  425.5 81.4 %copy-start.78 = (f32[12,768]{1,0:T(8,128)S(1)}, f32[12,768]{1,0:T(8,128)}, u32[]{:S(2)}) copy-start(f32[12,768]{1,0:T(8,128)} %copy-done.77) | copy-start | bytes 110596
  508.6 168.3 %reduce-scatter.9.cloned.1.call-start = ((), (), s32[]{:S(2)}) async-start(), calls=%async_computation.8 | async-start | bytes 10027008 | tf_op jit(solution)/shard_map/reduce_scatter | solution.py:272
  523.7 268.4 %reduce-scatter.7.cloned.1.call-start = ((), (), s32[]{:S(2)}) async-start(), calls=%async_computation.7 | async-start | bytes 10027008 | tf_op jit(solution)/shard_map/reduce_scatter | solution.py:271
  538.5 369.4 %reduce-scatter.11.cloned.1.call-start = ((), (), s32[]{:S(2)}) async-start(), calls=%async_computation.9 | async-start | bytes 10027008 | tf_op jit(solution)/shard_map/reduce_scatter | solution.py:273
  558.5 352.5 %copy-start.60 = (bf16[224,768]{1,0:T(8,128)(2,1)S(1)}, bf16[224,768]{1,0:T(8,128)(2,1)}, u32[]{:S(2)}) copy-start(bf16[224,768]{1,0:T(8,128)(2,1)} %get-tuple-element.362) | copy-start | bytes 1032196
  559.7 394.4 %copy-start.86 = (f32[1,12,48]{2,0,1:T(1,128)S(1)}, f32[1,12,48]{2,0,1:T(1,128)}, u32[]{:S(2)}) copy-start(f32[1,12,48]{2,0,1:T(1,128)} %param.33) | copy-start | bytes 6916
  559.7 394.3 %copy-start.105 = (f32[1,12,48]{2,0,1:T(1,128)S(1)}, f32[1,12,48]{2,0,1:T(1,128)}, u32[]{:S(2)}) copy-start(f32[1,12,48]{2,0,1:T(1,128)} %param.41) | copy-start | bytes 6916
  559.7 394.3 %copy-start.106 = (f32[1,12,48]{2,0,1:T(1,128)S(1)}, f32[1,12,48]{2,0,1:T(1,128)}, u32[]{:S(2)}) copy-start(f32[1,12,48]{2,0,1:T(1,128)} %param.37) | copy-start | bytes 6916
  559.8 396.2 %copy-start.47 = (f32[1,192,768]{2,1,0:T(8,128)S(1)}, f32[1,192,768]{2,1,0:T(8,128)}, u32[]{:S(2)}) copy-start(f32[1,192,768]{2,1,0:T(8,128)} %param.32) | copy-start | bytes 1769476
  911.0 48.0 %copy-start.48 = (f32[1,48,3072]{2,1,0:T(8,128)S(1)}, f32[1,48,3072]{2,1,0:T(8,128)}, u32[]{:S(2)}) copy-start(f32[1,48,3072]{2,1,0:T(8,128)} %param.30) | copy-start | bytes 1769476
  911.0 48.0 %copy-start.49 = (f32[1,48,3072]{2,1,0:T(8,128)S(1)}, f32[1,48,3072]{2,1,0:T(8,128)}, u32[]{:S(2)}) copy-start(f32[1,48,3072]{2,1,0:T(8,128)} %param.31) | copy-start | bytes 1769476
  912.1 47.0 %copy-start.50 = (f32[48,3072]{1,0:T(8,128)S(1)}, f32[48,3072]{1,0:T(8,128)}, u32[]{:S(2)}) copy-start(f32[48,3072]{1,0:T(8,128)} %reduce-scatter.9.cloned.1.call-done) | copy-start | bytes 1769476
  912.1 47.0 %copy-start.51 = (f32[48,3072]{1,0:T(8,128)S(1)}, f32[48,3072]{1,0:T(8,128)}, u32[]{:S(2)}) copy-start(f32[48,3072]{1,0:T(8,128)} %reduce-scatter.7.cloned.1.call-done) | copy-start | bytes 1769476
  (84 other events, 355.0 us)
Sparse Core Ops, SparseCore 0:
  10.9 56.1 all-gather.4
  70.0 51.9 all-gather.6
  124.8 51.9 all-gather.8
  508.8 53.2 reduce-scatter.12
  566.6 110.3 reduce-scatter.8
  680.9 111.1 reduce-scatter.6
  796.7 111.1 reduce-scatter.10
where the time goes:
time: 975 us; the launch traced here: 971 us
  waiting for transfers between devices  560 us (57%)
  matrix products  155 us (16%)
  other arithmetic  96.8 us (10%)
  blocking collectives  64.8 us (7%)
  local copies, waits for them, and re-layouts  44.7 us (5%)
  loops' own time  22.2 us (2%)
  between operations  19.3 us (2%)
    reduce_scatter x1, waiting for transfers between devices, shards(): lax.psum_scatter(totals[1], 'dp', scatter_dimension=0, tiled=True)  113 us
    reduce_scatter x1, waiting for transfers between devices, shards(): lax.psum_scatter(totals[0], 'dp', scatter_dimension=0, tiled=True)  113 us
    reduce_scatter x1, waiting for transfers between devices, shards(): lax.psum_scatter(totals[2], 'dp', scatter_dimension=0, tiled=True)  113 us
    ppermute x4, waiting for transfers between devices, from_behind(): return lax.ppermute(block, axis, route)  77.9 us
    all_gather x1, waiting for transfers between devices, shards(): lax.all_gather(down_weights[0].astype(jnp.bfloat16), 'dp', axis=0, tiled=...  54.8 us
    all_gather x1, waiting for transfers between devices, shards(): lax.all_gather(up_weights[0].astype(jnp.bfloat16), 'dp', axis=0, tiled=True)  54.8 us
    add x4, other arithmetic, shards(): totals = jax.tree.map(jnp.add, totals, grads)  44.5 us
    psum x1, blocking collectives, shards(): grad_norm = jnp.sqrt(lax.psum(squares, ('section', 'dp')))  41.3 us
  transfers between devices with their start and end apart: 11, of which 11 were waited for; matrix products, arithmetic and copies ran while one was open for 6% of the time, Pallas kernels for 0%

commit v1 on v0

v1 whole, which is shorter than its diff:
```python
from functools import partial

import jax
import jax.numpy as jnp
from jax import lax
from jax.experimental import pallas as pl
from jax.experimental.pallas import tpu as pltpu
from jax.sharding import PartitionSpec as P

HEADS = 12
STEP = 10
LN_EPS = 1e-06
NEG_BIG = -1e30
BETA_ONE = 0.9
BETA_TWO = 0.999
RATE = 0.1
VECTOR_RATE = 0.5
DECAY_RATE = 0.01
ADAM_EPS = 1e-08
MAX_NORM = 1.0
MESH = pl.DeviceIdType.MESH
VMEM_LIMIT = 60 * 2**20
F32 = jnp.float32
BF16 = jnp.bfloat16


class Ring:
    def __init__(self, devices):
        self.devices = devices
        self.chips = devices // 2
        self.reach = self.chips // 2
        self.me = lax.axis_index("dp")
        self.core = self.me % 2
        chip = self.me // 2
        row, column = chip // 2, chip % 2
        self.place = row * (1 - column) + (self.chips - 1 - row) * column

    def device(self, place, core):
        place = (place + 2 * self.chips) % self.chips
        column = place // self.reach
        row = place * (1 - column) + (self.chips - 1 - place) * column
        return (row * 2 + column) * 2 + core

    def target(self, device):
        return (lax.axis_index("section"), device)

    def right(self):
        return self.target(self.device(self.place + 1, self.core))

    def left(self):
        return self.target(self.device(self.place - 1, self.core))

    def sibling(self):
        return self.target(self.device(self.place, 1 - self.core))

    def greet(self):
        barrier = pltpu.get_barrier_semaphore()
        for device in (self.right(), self.left(), self.sibling()):
            pl.semaphore_signal(barrier, inc=1, device_id=device, device_id_type=MESH)
        pl.semaphore_wait(barrier, 3)


def shard_view(ref, device, rows, part=None):
    start = pl.multiple_of(device * rows, rows)
    if part is None:
        return ref.at[pl.ds(start, rows), :]
    columns = ref.shape[1] // 2
    return ref.at[pl.ds(start, rows), pl.ds(part * columns, columns)]


def remote(source, target, send, receive, device):
    return pltpu.make_async_remote_copy(
        src_ref=source,
        dst_ref=target,
        send_sem=send,
        recv_sem=receive,
        device_id=device,
        device_id_type=MESH,
    )


class Gather:
    def __init__(self, ring, whole, rows, halves, send, receive):
        self.ring, self.whole, self.rows, self.halves = ring, whole, rows, halves
        self.send, self.receive = send, receive
        self.sent = []

    def view(self, distance, core, part=None):
        device = self.ring.device(self.ring.place + distance, core)
        return shard_view(self.whole, device, self.rows, part)

    def push(self, way, step):
        ring = self.ring
        direction = 1 if way == 0 else -1
        part = None
        if step == ring.reach:
            if self.halves:
                part = way
            elif way == 1:
                return
        view = self.view(-direction * (step - 1), ring.core, part)
        device = ring.right() if way == 0 else ring.left()
        copy = remote(view, view, self.send.at[way, step], self.receive.at[way, step], device)
        copy.start()
        self.sent.append(copy)

    def arrive(self, way, step):
        ring = self.ring
        direction = 1 if way == 0 else -1
        part = None
        if step == ring.reach:
            if self.halves:
                part = way
            elif way == 1:
                return
        view = self.view(-direction * step, ring.core, part)
        device = ring.right() if way == 0 else ring.left()
        remote(view, view, self.send.at[way, step], self.receive.at[way, step], device).wait_recv()

    def share(self, distance, key):
        ring = self.ring
        view = self.view(distance, ring.core)
        copy = remote(view, view, self.send.at[2, key], self.receive.at[2, key], ring.sibling())
        copy.start()
        self.sent.append(copy)

    def shared(self, distance, key):
        ring = self.ring
        view = self.view(distance, 1 - ring.core)
        remote(view, view, self.send.at[2, key], self.receive.at[2, key], ring.sibling()).wait_recv()

    def begin(self):
        self.push(0, 1)
        self.push(1, 1)
        self.share(0, 0)

    def step(self, step):
        reach = self.ring.reach
        self.arrive(0, step)
        if step < reach:
            self.push(0, step + 1)
        self.arrive(1, step)
        if step < reach:
            self.push(1, step + 1)
            self.share(-step, step)
            self.share(step, reach + step)
        else:
            self.share(reach, reach)

    def finish_shares(self):
        reach = self.ring.reach
        self.shared(0, 0)
        for step in range(1, reach):
            self.shared(-step, step)
            self.shared(step, reach + step)
        self.shared(reach, reach)

    def drain(self):
        for copy in self.sent:
            copy.wait_send()


class Reduce:
    def __init__(self, ring, whole, out, other, slots, rows, halves, block, send, receive):
        self.ring, self.whole, self.out, self.other, self.slots = ring, whole, out, other, slots
        self.rows, self.halves, self.block = rows, halves, block
        self.send, self.receive = send, receive
        self.sent = []

    def view(self, distance, core, part=None):
        device = self.ring.device(self.ring.place + distance, core)
        return shard_view(self.whole, device, self.rows, part)

    def keys(self):
        reach = self.ring.reach
        order = [(reach, reach)]
        for distance in range(reach - 1, 0, -1):
            order += [(distance, reach + distance), (-distance, distance)]
        return order + [(0, 0)]

    def exchange(self):
        ring = self.ring
        for distance, key in self.keys():
            copy = remote(
                self.view(distance, 1 - ring.core),
                self.other.at[key],
                self.send.at[2, key],
                self.receive.at[2, key],
                ring.sibling(),
            )
            copy.start()
            self.sent.append(copy)

    def exchanged(self, key):
        ring = self.ring
        slot = self.other.at[key]
        remote(slot, slot, self.send.at[2, key], self.receive.at[2, key], ring.sibling()).wait_recv()

    def slot(self, way, step, part=None):
        ref = self.slots.at[way, step]
        if part is None:
            return ref
        columns = ref.shape[1] // 2
        return ref.at[:, pl.ds(part * columns, columns)]

    def part_of(self, way, distance):
        if distance == self.ring.reach and self.halves:
            return way
        return None

    def push(self, way, distance):
        ring = self.ring
        if distance == ring.reach and not self.halves and way == 1:
            return
        part = self.part_of(way, distance)
        device = ring.right() if way == 0 else ring.left()
        copy = remote(
            self.view(distance if way == 0 else -distance, ring.core, part),
            self.slot(way, distance, part),
            self.send.at[way, distance],
            self.receive.at[way, distance],
            device,
        )
        copy.start()
        self.sent.append(copy)

    def arrive(self, way, distance):
        ring = self.ring
        if distance == ring.reach and not self.halves and way == 1:
            return
        slot = self.slot(way, distance, self.part_of(way, distance))
        device = ring.right() if way == 0 else ring.left()
        remote(slot, slot, self.send.at[way, distance], self.receive.at[way, distance], device).wait_recv()

    def add(self, distance, key, arrivals, target=None):
        ring = self.ring
        base = ring.device(ring.place + distance, ring.core) * self.rows
        block = self.block
        columns = self.whole.shape[1]
        half = columns // 2

        def body(index, _):
            start = pl.multiple_of(index * block, block)
            here = pl.ds(pl.multiple_of(base + index * block, block), block)
            rows = pl.ds(start, block)
            total = self.whole[here, :].astype(F32) + self.other[key, rows, :].astype(F32)
            whole_total = total
            for way, step in arrivals:
                if step == ring.reach:
                    if not self.halves:
                        if way == 0:
                            whole_total = whole_total + self.slots[way, step, rows, :].astype(F32)
                        continue
                    low = whole_total[:, :half]
                    high = whole_total[:, half:]
                    if way == 0:
                        low = low + self.slots[way, step, rows, :half].astype(F32)
                    else:
                        high = high + self.slots[way, step, rows, half:].astype(F32)
                    whole_total = jnp.concatenate([low, high], axis=1)
                else:
                    whole_total = whole_total + self.slots[way, step, rows, :].astype(F32)
            if target is None:
                self.whole[here, :] = whole_total.astype(self.whole.dtype)
            else:
                target[rows, :] = whole_total.astype(target.dtype)
            return 0

        lax.fori_loop(0, self.rows // block, body, 0)

    def first(self):
        reach = self.ring.reach
        self.exchanged(reach)
        self.add(reach, reach, [])
        self.push(0, reach)
        self.push(1, reach)

    def step(self, distance):
        reach = self.ring.reach
        self.exchanged(reach + distance)
        self.arrive(0, distance + 1)
        self.add(distance, reach + distance, [(0, distance + 1)])
        self.push(0, distance)
        self.exchanged(distance)
        self.arrive(1, distance + 1)
        self.add(-distance, distance, [(1, distance + 1)])
        self.push(1, distance)

    def last(self):
        self.exchanged(0)
        self.arrive(0, 1)
        self.arrive(1, 1)
        self.add(0, 0, [(0, 1), (1, 1)], self.out)

    def drain(self):
        for copy in self.sent:
            copy.wait_send()


def ring_semaphores(count, reach):
    shape = (count, 3, 2 * reach)
    return [pltpu.SemaphoreType.DMA(shape), pltpu.SemaphoreType.DMA(shape)]


def gather_kernel(devices, own_qkv, own_out, own_up, own_down, own_vec, qkv, out, up, down, vec, local, send, receive):
    ring = Ring(devices)
    owned = (own_vec, own_qkv, own_out, own_up, own_down)
    wholes = (vec, qkv, out, up, down)
    gathers = []
    copies = []
    for index, (own, whole) in enumerate(zip(owned, wholes)):
        gathers.append(
            Gather(ring, whole, own.shape[0], index > 0, send.at[index], receive.at[index])
        )
        copies.append(
            pltpu.make_async_copy(own, shard_view(whole, ring.me, own.shape[0]), local.at[index])
        )
    for copy in copies:
        copy.start()
    for copy in copies:
        copy.wait()
    ring.greet()
    for gather in gathers:
        gather.begin()
    for step in range(1, ring.reach + 1):
        for gather in gathers:
            gather.step(step)
    for gather in gathers:
        gather.finish_shares()
        gather.drain()


def ring_gather(devices, owned):
    reach = devices // 4
    return pl.pallas_call(
        partial(gather_kernel, devices),
        out_shape=[
            jax.ShapeDtypeStruct((devices * own.shape[0], own.shape[1]), own.dtype) for own in owned
        ],
        in_specs=[pl.BlockSpec(memory_space=pltpu.VMEM)] * 5,
        out_specs=[pl.BlockSpec(memory_space=pltpu.VMEM)] * 5,
        scratch_shapes=[pltpu.SemaphoreType.DMA((5,))] + ring_semaphores(5, reach),
        compiler_params=pltpu.CompilerParams(
            collective_id=0, has_side_effects=True, vmem_limit_bytes=VMEM_LIMIT
        ),
        name="ring_gather",
    )(*owned)


def reduce_kernel(devices, *refs):
    sums, outs, others, slots = refs[:5], refs[5:10], refs[10:15], refs[15:20]
    send, receive = refs[20:]
    ring = Ring(devices)
    reduces = [
        Reduce(
            ring,
            sums[i],
            outs[i],
            others[i],
            slots[i],
            outs[i].shape[0],
            i < 4,
            16,
            send.at[i],
            receive.at[i],
        )
        for i in range(5)
    ]
    ring.greet()
    for reduce in reduces:
        reduce.exchange()
    for reduce in reduces:
        reduce.first()
    for distance in range(ring.reach - 1, 0, -1):
        for reduce in reduces:
            reduce.step(distance)
    for reduce in reduces:
        reduce.last()
    for reduce in reduces:
        reduce.drain()


def ring_reduce(devices, sums):
    reach = devices // 4
    chips = devices // 2
    out_shapes, others, slots = [], [], []
    for member in sums:
        rows, columns = member.shape[0] // devices, member.shape[1]
        out_shapes.append(jax.ShapeDtypeStruct((rows, columns), F32))
        others.append(pltpu.VMEM((chips, rows, columns), member.dtype))
        slots.append(pltpu.VMEM((2, reach + 1, rows, columns), member.dtype))
    return pl.pallas_call(
        partial(reduce_kernel, devices),
        out_shape=out_shapes,
        in_specs=[pl.BlockSpec(memory_space=pltpu.VMEM)] * 5,
        out_specs=[pl.BlockSpec(memory_space=pltpu.VMEM)] * 5,
        scratch_shapes=others + slots + ring_semaphores(5, reach),
        compiler_params=pltpu.CompilerParams(
            collective_id=1, has_side_effects=True, vmem_limit_bytes=VMEM_LIMIT
        ),
        name="ring_reduce",
    )(*sums)


def pad_tile(block):
    return jnp.pad(block, ((0, 16 - block.shape[0]), (0, 128 - block.shape[1])))


def gather_weights(fast, devices, attn, upward_w, downward_w, vectors):
    shards = (attn.astype(BF16), upward_w.astype(BF16), downward_w.astype(BF16))
    if not fast:
        return tuple(lax.all_gather(s, "dp", axis=0, tiled=True) for s in shards) + (
            lax.all_gather(vectors.astype(BF16), "dp", axis=1, tiled=True),
        )
    width = downward_w.shape[1]
    tile = pad_tile(vectors.astype(BF16))
    qkv, out, up, down, tiles = ring_gather(
        devices, (shards[0][:, : 3 * width], shards[0][:, 3 * width :], shards[1], shards[2], tile)
    )
    rows, columns = vectors.shape
    spread = tiles.reshape(devices, 16, 128)[:, :rows, :columns]
    return (jnp.concatenate([qkv, out], axis=1), up, down, spread.transpose(1, 0, 2).reshape(rows, -1))


def reduce_gradients(fast, devices, gradients):
    attn, upward_w, downward_w, vectors = gradients
    if not fast:
        return tuple(
            lax.psum_scatter(g, "dp", scatter_dimension=0, tiled=True)
            for g in (attn, upward_w, downward_w)
        ) + (lax.psum_scatter(vectors, "dp", scatter_dimension=1, tiled=True),)
    width = downward_w.shape[1]
    rows, columns = vectors.shape[0], vectors.shape[1] // devices
    spread = vectors.reshape(rows, devices, columns).transpose(1, 0, 2)
    tiles = jnp.pad(spread, ((0, 0), (0, 16 - rows), (0, 128 - columns))).reshape(-1, 128)
    qkv, out, up, down, tile = ring_reduce(
        devices,
        (
            attn[:, : 3 * width].astype(BF16),
            attn[:, 3 * width :].astype(BF16),
            upward_w.astype(BF16),
            downward_w.astype(BF16),
            tiles,
        ),
    )
    return (jnp.concatenate([qkv, out], axis=1), up, down, tile[:rows, :columns])


def layer_norm(features, gain_row, shift_row):
    center = jnp.mean(features, axis=-1, keepdims=True)
    centered = features - center
    spread = jnp.mean(centered * centered, axis=-1, keepdims=True)
    return centered * lax.rsqrt(spread + LN_EPS) * gain_row + shift_row


def split_heads(packed, micro_count, model_width):
    shaped = packed.reshape(micro_count, -1, 3, HEADS, model_width // HEADS)
    return (shaped[:, :, 0], shaped[:, :, 1], shaped[:, :, 2])


def attention_scores(queries, keys_block, crop_rows):
    head_scale = queries.shape[-1] ** (-0.5)
    scores = (
        jnp.einsum("mqhd,mkhd->mhqk", queries, keys_block, preferred_element_type=F32) * head_scale
    )
    same_crop = crop_rows[:, :, None] == crop_rows[:, None, :]
    return jnp.where(same_crop[:, None], scores, NEG_BIG)


def forward_layer(inputs, crop_rows, weights):
    attn, upward_w, downward_w, vectors_b = weights
    model_width = attn.shape[0]
    rows = inputs.shape[0]
    params = vectors_b.astype(F32)
    hidden = layer_norm(inputs, params[0], params[1]).astype(BF16)
    qkv_bias = jnp.concatenate([params[2], jnp.zeros_like(params[2]), params[3]])
    packed = (
        jnp.dot(hidden, attn[:, : 3 * model_width], preferred_element_type=F32) + qkv_bias
    ).astype(BF16)
    queries, keys_block, values_block = split_heads(packed, crop_rows.shape[0], model_width)
    scores = attention_scores(queries, keys_block, crop_rows)
    row_peak = jnp.max(scores, axis=-1, keepdims=True)
    exponent = jnp.exp(scores - row_peak)
    totals = jnp.sum(exponent, axis=-1, keepdims=True)
    soft_weights = (exponent / totals).astype(BF16)
    log_total = row_peak + jnp.log(totals)
    mixed = jnp.einsum("mhqk,mkhd->mqhd", soft_weights, values_block, preferred_element_type=F32)
    mixed = mixed.reshape(rows, model_width).astype(BF16)
    middle = inputs + (
        jnp.dot(mixed, attn[:, 3 * model_width :], preferred_element_type=F32) + params[4]
    )
    hidden_two = layer_norm(middle, params[5], params[6]).astype(BF16)
    upward = jnp.dot(hidden_two, upward_w, preferred_element_type=F32) + params[8:].reshape(-1)
    active = jax.nn.gelu(upward, approximate=False).astype(BF16)
    output = middle + (jnp.dot(active, downward_w, preferred_element_type=F32) + params[7])
    return (output, (inputs, hidden, packed, log_total, mixed, middle, hidden_two, upward, active))


def backward_layer(kept, crop_rows, grad_out, weights, with_grads):
    attn, upward_w, downward_w, vectors_b = weights
    inputs, hidden, packed, log_total, mixed, middle, hidden_two, upward, active = kept
    model_width = attn.shape[0]
    rows = inputs.shape[0]
    params = vectors_b.astype(F32)
    grad_down = grad_out.astype(BF16)
    grad_active = jnp.einsum("pj,ij->pi", grad_down, downward_w, preferred_element_type=F32)
    gelu_back = jax.vjp(partial(jax.nn.gelu, approximate=False), upward)[1]
    grad_up = gelu_back(grad_active)[0].astype(BF16)
    grad_hidden_two = jnp.einsum("pj,ij->pi", grad_up, upward_w, preferred_element_type=F32)
    norm_back_two = jax.vjp(layer_norm, middle, params[5], params[6])[1]
    grad_middle_part, grad_gain_two, grad_shift_two = norm_back_two(grad_hidden_two)
    grad_middle = grad_out + grad_middle_part
    grad_branch = grad_middle.astype(BF16)
    grad_mixed = jnp.einsum(
        "pj,ij->pi", grad_branch, attn[:, 3 * model_width :], preferred_element_type=F32
    ).astype(BF16)
    micro_count = crop_rows.shape[0]
    queries, keys_block, values_block = split_heads(packed, micro_count, model_width)
    scores = attention_scores(queries, keys_block, crop_rows)
    probs = jnp.exp(scores - log_total)
    grad_heads = grad_mixed.reshape(micro_count, -1, HEADS, model_width // HEADS)
    grad_probs = jnp.einsum("mqhd,mkhd->mhqk", grad_heads, values_block, preferred_element_type=F32)
    grad_values = jnp.einsum(
        "mhqk,mqhd->mkhd", probs.astype(BF16), grad_heads, preferred_element_type=F32
    )
    grad_scores = (
        probs * (grad_probs - jnp.sum(grad_probs * probs, axis=-1, keepdims=True))
    ).astype(BF16)
    head_scale = queries.shape[-1] ** (-0.5)
    grad_queries = (
        jnp.einsum("mhqk,mkhd->mqhd", grad_scores, keys_block, preferred_element_type=F32)
        * head_scale
    )
    grad_keys = (
        jnp.einsum("mhqk,mqhd->mkhd", grad_scores, queries, preferred_element_type=F32) * head_scale
    )
    grad_packed = jnp.concatenate(
        [
            grad_queries.reshape(rows, model_width),
            grad_keys.reshape(rows, model_width),
            grad_values.reshape(rows, model_width),
        ],
        axis=1,
    ).astype(BF16)
    grad_hidden = jnp.einsum(
        "pj,ij->pi", grad_packed, attn[:, : 3 * model_width], preferred_element_type=F32
    )
    norm_back_one = jax.vjp(layer_norm, inputs, params[0], params[1])[1]
    grad_in_part, grad_gain_one, grad_shift_one = norm_back_one(grad_hidden)
    grad_inputs = grad_middle + grad_in_part
    if not with_grads:
        return (grad_inputs, None)
    grad_w_down = jnp.einsum("pi,pj->ij", active, grad_down, preferred_element_type=F32)
    grad_w_up = jnp.einsum("pi,pj->ij", hidden_two, grad_up, preferred_element_type=F32)
    grad_w_out = jnp.einsum("pi,pj->ij", mixed, grad_branch, preferred_element_type=F32)
    grad_w_qkv = jnp.einsum("pi,pj->ij", hidden, grad_packed, preferred_element_type=F32)
    packed_sums = jnp.sum(grad_packed, axis=0, dtype=F32)
    vector_rows = jnp.stack(
        [
            grad_gain_one,
            grad_shift_one,
            packed_sums[:model_width],
            packed_sums[2 * model_width :],
            jnp.sum(grad_branch, axis=0, dtype=F32),
            grad_gain_two,
            grad_shift_two,
            jnp.sum(grad_down, axis=0, dtype=F32),
        ]
    )
    up_bias_rows = jnp.sum(grad_up, axis=0, dtype=F32).reshape(-1, model_width)
    grad_vectors = jnp.concatenate([vector_rows, up_bias_rows], axis=0)
    grad_attn = jnp.concatenate([grad_w_qkv, grad_w_out], axis=1)
    return (grad_inputs, (grad_attn, grad_w_up, grad_w_down, grad_vectors))


def adam_update(master, gradient, moment_one, moment_two, decay_rate, step_rate):
    new_one = BETA_ONE * moment_one + (1.0 - BETA_ONE) * gradient
    new_two = BETA_TWO * moment_two + (1.0 - BETA_TWO) * gradient * gradient
    ratio = (
        new_one / (1.0 - BETA_ONE**STEP) / (jnp.sqrt(new_two / (1.0 - BETA_TWO**STEP)) + ADAM_EPS)
    )
    return (master - step_rate * (ratio + decay_rate * master), new_one, new_two)


def shards(
    devices,
    tokens,
    cotangent,
    crop_ids,
    attn_weights,
    up_weights,
    down_weights,
    vectors,
    first_attn,
    first_up,
    first_down,
    first_vectors,
    second_attn,
    second_up,
    second_down,
    second_vectors,
):
    section_index = lax.axis_index("section")
    micro_count, pack_rows, model_width = tokens.shape
    flat = (micro_count * pack_rows, model_width)
    fast = (
        devices % 8 == 0
        and all(w.shape[1] % 16 == 0 for w in (attn_weights, up_weights, down_weights))
        and vectors.shape[1] <= 16
        and vectors.shape[2] <= 128
    )
    weights = gather_weights(
        fast, devices, attn_weights[0], up_weights[0], down_weights[0], vectors[0]
    )
    own_tokens = tokens.reshape(flat)
    first_output, _ = forward_layer(own_tokens.astype(F32), crop_ids, weights)
    received = lax.ppermute(first_output.astype(BF16), "section", [(0, 1)])
    layer_input = jnp.where(section_index == 0, own_tokens, received)
    output, kept = forward_layer(layer_input.astype(F32), crop_ids, weights)
    boundary = output.astype(BF16).reshape(tokens.shape)
    own_grad = cotangent.reshape(flat)
    first_back, _ = backward_layer(kept, crop_ids, own_grad.astype(F32), weights, False)
    back_received = lax.ppermute(first_back.astype(BF16), "section", [(1, 0)])
    grad_out = jnp.where(section_index == 1, own_grad, back_received).astype(F32)
    grad_inputs, gradients = backward_layer(kept, crop_ids, grad_out, weights, True)
    input_grads = grad_inputs.astype(BF16).reshape(tokens.shape)
    reduced = reduce_gradients(fast, devices, gradients)
    squares = sum_squares(reduced)
    grad_norm = jnp.sqrt(lax.psum(squares, ("section", "dp")))
    clip_factor = jnp.minimum(1.0, MAX_NORM / (grad_norm + 1e-06))
    masters = (attn_weights, up_weights, down_weights, vectors)
    firsts = (first_attn, first_up, first_down, first_vectors)
    seconds = (second_attn, second_up, second_down, second_vectors)
    decays = (DECAY_RATE, DECAY_RATE, DECAY_RATE, 0.0)
    rates = (RATE, RATE, RATE, VECTOR_RATE)
    updated = [
        adam_update(
            master[0], gradient * clip_factor, moment_one[0], moment_two[0], decay_rate, step_rate
        )
        for master, gradient, moment_one, moment_two, decay_rate, step_rate in zip(
            masters, reduced, firsts, seconds, decays, rates
        )
    ]
    new_masters = tuple((entry[0][None] for entry in updated))
    new_firsts = tuple((entry[1][None] for entry in updated))
    new_seconds = tuple((entry[2][None] for entry in updated))
    return (boundary[None], input_grads[None], grad_norm) + new_masters + new_firsts + new_seconds


def sum_squares(arrays):
    running = jnp.zeros((), F32)
    for member in arrays:
        running = running + jnp.sum(member * member)
    return running


def solution(mesh):
    token_spec = P(None, "dp", None)
    row_spec = P("section", "dp", None)
    column_spec = P("section", None, "dp")
    state = (row_spec, row_spec, row_spec, column_spec)
    micro_spec = P("section", None, "dp", None)
    return jax.shard_map(
        partial(shards, mesh.shape["dp"]),
        mesh=mesh,
        in_specs=(token_spec, token_spec, P(None, "dp")) + 3 * state,
        out_specs=(micro_spec, micro_spec, P()) + 3 * state,
        check_vma=False,
    )
```

time: 975 us -> 529 us (0.54)
  waiting for transfers between devices: 560 us -> 33 us
  Pallas kernels: 0 us -> 163 us
  other arithmetic: 96.8 us -> 36.3 us
  local copies, waits for them, and re-layouts: 44.7 us -> 94.3 us
  blocking collectives: 64.8 us -> 39.2 us
  loops' own time: 22.2 us -> 0 us
  between operations: 19.3 us -> 6.39 us
  matrix products: 155 us -> 145 us
    reduce_scatter x3 -> x0, waiting for transfers between devices: 339 us -> none  [the longest x1 113 us: shards(): lax.psum_scatter(totals[1], 'dp', scatter_dimension=0, tiled=True)]
    pallas_call x0 -> x2, Pallas kernels: none -> 163 us  [the longest x1 81.9 us: ring_gather(): pl.pallas_call(partial(gather_kernel, devices), out_shape=[jax.ShapeDtype...]
    all_gather x3 -> x0, waiting for transfers between devices: 141 us -> none  [the longest x1 54.8 us: shards(): lax.all_gather(down_weights[0].astype(jnp.bfloat16), 'dp', axis=0, tiled=...]
    ppermute x4 -> x2, waiting for transfers between devices: 77.9 us -> 33 us  [the longest x1 17.6 us: shards(): back_received = lax.ppermute(first_back.astype(BF16), 'section', [(1, 0)])]
    add x4 -> x0, other arithmetic: 44.5 us -> none  [shards(): totals = jax.tree.map(jnp.add, totals, grads)]
    reshape x10 -> x12, local copies, waits for them, and re-layouts: 0.05 us -> 36.8 us  [the longest x2 14.7 us: split_heads(): shaped = packed.reshape(micro_count, -1, 3, HEADS, model_width // HEADS)]
    all_gather x1 -> x0, blocking collectives: 23.6 us -> none  [shards(): lax.all_gather(vectors[0].astype(jnp.bfloat16), 'dp', axis=1, tiled=True)]
    another operation x6 -> x0, loops' own time: 22.2 us -> none  [the longest x3 18.7 us: shards(): grad_inputs, grads = lax.cond(is_valid, run_back, skip_back)]
  transfers between devices with their start and end apart: 11 -> 2, of which waited for: 11 -> 2; matrix products, arithmetic and copies ran while one was open for 6% -> 0% of each run, Pallas kernels for 0% -> 0%
where the time goes in v1:
time: 529 us; the launch traced here: 521 us
  Pallas kernels  163 us (31%)
  matrix products  145 us (27%)
  local copies, waits for them, and re-layouts  94.3 us (18%)
  blocking collectives  39.2 us (7%)
  other arithmetic  36.3 us (7%)
  waiting for transfers between devices  33 us (6%)
  between operations  6.39 us (1%)
    pallas_call x1, Pallas kernels, ring_gather(): pl.pallas_call(partial(gather_kernel, devices), out_shape=[jax.ShapeDtype...  81.9 us
    pallas_call x1, Pallas kernels, ring_reduce(): pl.pallas_call(partial(reduce_kernel, devices), out_shape=out_shapes, in_...  80.8 us
    psum x1, blocking collectives, shards(): grad_norm = jnp.sqrt(lax.psum(squares, ('section', 'dp')))  39.2 us
    dot_general x2, matrix products, forward_layer(): jnp.dot(active, downward_w, preferred_element_type=F32) + params[7]  27 us
    unnamed x147, local copies, waits for them, and re-layouts  24.6 us
    dot_general x1, matrix products, forward_layer(): jnp.dot(hidden_two, upward_w, preferred_element_type=F32)  18 us
    ppermute x1, waiting for transfers between devices, shards(): back_received = lax.ppermute(first_back.astype(BF16), 'section', [(1, 0)])  17.6 us
    dot_general x2, matrix products, backward_layer(): jnp.einsum('pj,ij->pi', grad_up, upward_w, preferred_element_type=F32)  15.9 us
  transfers between devices with their start and end apart: 2, of which 2 were waited for; matrix products, arithmetic and copies ran while one was open for 0% of the time, Pallas kernels for 0%

profile of v1, /device:TPU:0, one launch (start us, length us, event | category | flops | bytes accessed | tf_op | source)
XLA Modules:
  0.0 521.2 jit_solution(14750551961052978682)
XLA Ops:
  10.9 81.9 %ring_gather.1 = (bf16[768,2304]{1,0:T(8,128)(2,1)}, bf16[768,768]{1,0:T(8,128)(2,1)}, bf16[768,3072]{1,0:T(8,128)(2,1)}, bf16[3072,768]{1,0:T(8,128)(2,1)}, bf16[256,128]{1,0:T(8,128)(2,1)}) custom-call(bf16[48,2304]{1,0:T(8,128)(2,1)} %slice.124.own_qkv, bf16[48,768]{1,0:T(8,128)(2,1)} %slice.125.own_out, bf16[48,3072]{1,0:T(8,128)(2,1)} %bitcast_convert_fusion.1.own_up, ...), custom_call_target="tpu_custom_call" | custom-call | tf_op jit(solution)/shard_map/ring_gather/pallas_call | solution.py:335
  94.1 5.2 %fusion.26 = bf16[448,2304]{1,0:T(8,128)(2,1)} fusion(bf16[768,2304]{1,0:T(8,128)(2,1)} %get-tuple-element.26, f32[2304]{0:T(1024)S(1)} %pad_maximum_fusion, bf16[448,768]{1,0:T(8,128)(2,1)S(1)} %bitcast.246, f32[768]{0:T(1024)S(1)} %add.250, f32[768]{0:T(1024)S(1)} %mul.528, f32[448]{0:T(512)S(1)} %rsqrt.48, f32[448]{0:T(512)S(1)} %div.145), kind=kOutput, calls=%fused_computation.67 | convolution fusion | flops 1589575680 | bytes 6310400 | tf_op jit(solution)/shard_map/dot_general | solution.py:478
  99.3 7.3 %reshape.354 = bf16[2,224,3,12,64]{4,3,2,1,0:T(8,128)(2,1)} reshape(bf16[448,2304]{1,0:T(8,128)(2,1)} %fusion.26) | data formatting | bytes 4128768 | tf_op jit(solution)/shard_map/reshape | solution.py:457
  106.6 5.4 %fusion.191 = (bf16[2,224,1,12,64]{4,3,2,1,0:T(8,128)(2,1)S(1)}, bf16[2,224,1,12,64]{4,3,2,1,0:T(8,128)(2,1)}, bf16[2,224,1,12,64]{4,3,2,1,0:T(8,128)(2,1)}) fusion(bf16[2,224,3,12,64]{4,3,2,1,0:T(8,128)(2,1)} %reshape.354), kind=kLoop, calls=%fused_computation.313 | loop fusion | bytes 4128768 | tf_op jit(solution)/shard_map/slice | solution.py:458
  130.6 20.2 %fusion.73 = bf16[448,768]{1,0:T(8,128)(2,1)} fusion(f32[448,768]{1,0:T(8,128)S(1)} %get-tuple-element.115, bf16[3072,768]{1,0:T(8,128)(2,1)} %get-tuple-element.29, bf16[768,3072]{1,0:T(8,128)(2,1)} %get-tuple-element.28, f32[3072]{0:T(1024)S(1)} %add.263, f32[768]{0:T(1024)S(1)} %add.266, f32[768]{0:T(1024)S(1)} %add.260, f32[768]{0:T(1024)S(1)} %mul.535, ...), kind=kOutput, calls=%fused_computation.148 | convolution fusion | flops 4321443840 | bytes 11526656 | tf_op jit(solution)/shard_map/dot_general | solution.py:495
  154.3 15.5 %collective-permute-done = bf16[448,768]{1,0:T(8,128)(2,1)S(1)} collective-permute-done((bf16[448,768]{1,0:T(8,128)(2,1)}, bf16[448,768]{1,0:T(8,128)(2,1)S(1)}, u32[]{:S(2)}, u32[]{:S(2)}) %collective-permute-start) | collective-permute-done | bytes 688160 | tf_op jit(solution)/shard_map/ppermute | solution.py:617
  170.4 5.2 %fusion.27 = bf16[448,2304]{1,0:T(8,128)(2,1)} fusion(bf16[768,2304]{1,0:T(8,128)(2,1)} %get-tuple-element.26, f32[2304]{0:T(1024)S(1)} %pad_maximum_fusion, bf16[448,768]{1,0:T(8,128)(2,1)S(1)} %broadcast_select_fusion.1, f32[448]{0:T(512)S(1)} %fusion.138, f32[448]{0:T(512)S(1)} %broadcast_multiply_fusion.1, f32[768]{0:T(1024)S(1)} %add.250, ...), kind=kOutput, calls=%fused_computation.68 | convolution fusion | flops 1589575680 | bytes 6310400 | tf_op jit(solution)/shard_map/dot_general | solution.py:478
  175.6 7.4 %reshape.355 = bf16[2,224,3,12,64]{4,3,2,1,0:T(8,128)(2,1)} reshape(bf16[448,2304]{1,0:T(8,128)(2,1)} %fusion.27) | data formatting | bytes 4128768 | tf_op jit(solution)/shard_map/reshape | solution.py:457
  183.1 5.5 %fusion.190 = (bf16[2,224,1,12,64]{4,3,2,1,0:T(8,128)(2,1)}, bf16[2,224,1,12,64]{4,3,2,1,0:T(8,128)(2,1)}, bf16[2,224,1,12,64]{4,3,2,1,0:T(8,128)(2,1)}) fusion(bf16[2,224,3,12,64]{4,3,2,1,0:T(8,128)(2,1)} %reshape.355), kind=kLoop, calls=%fused_computation.312 | loop fusion | bytes 4128768 | tf_op jit(solution)/shard_map/slice | solution.py:458
  200.3 4.4 fusion.75
  211.8 18.0 %multiply_convert_fusion.2 = (bf16[448,3072]{1,0:T(8,128)(2,1)}, f32[448,3072]{1,0:T(8,128)}, f32[448,3072]{1,0:T(8,128)}) fusion(f32[3072]{0:T(1024)S(1)} %add.263, bf16[768,3072]{1,0:T(8,128)(2,1)} %get-tuple-element.28, f32[448,768]{1,0:T(8,128)S(1)} %get-tuple-element.119, f32[448]{0:T(512)S(1)} %fusion.139, f32[448]{0:T(512)S(1)} %broadcast_multiply_fusion, ...), kind=kOutput, calls=%fused_computation.23 | convolution fusion | flops 2206482432 | bytes 19879424 | tf_op jit(solution)/shard_map/dot_general | solution.py:493
  229.8 13.1 %multiply_reduce_fusion.4 = (f32[448]{0:T(512)S(1)}, f32[448,768]{1,0:T(8,128)}) fusion(f32[448,768]{1,0:T(8,128)} %copy-done.6, f32[448]{0:T(512)S(1)} %broadcast_multiply_fusion, f32[768]{0:T(1024)S(1)} %mul.535, bf16[768,3072]{1,0:T(8,128)(2,1)} %get-tuple-element.28, f32[448,3072]{1,0:T(8,128)} %get-tuple-element.86, ...), kind=kOutput, calls=%fused_computation.140 | convolution fusion | flops 4249878016 | bytes 23906816 | tf_op jit(solution)/shard_map/pj,ij->pi/dot_general | solution.py:509
  256.0 5.1 multiply_reduce_fusion.1
  276.3 5.1 fusion.69
  284.1 17.6 %collective-permute-done.1 = bf16[448,768]{1,0:T(8,128)(2,1)} collective-permute-done((bf16[448,768]{1,0:T(8,128)(2,1)S(1)}, bf16[448,768]{1,0:T(8,128)(2,1)}, u32[]{:S(2)}, u32[]{:S(2)}) %collective-permute-start.1) | collective-permute-done | bytes 688160 | tf_op jit(solution)/shard_map/ppermute | solution.py:623
  303.0 9.1 %convert_reduce_fusion = (f32[3072]{0:T(1024)}, bf16[448,3072]{1,0:T(8,128)(2,1)S(1)}) fusion(f32[448,3072]{1,0:T(8,128)} %get-tuple-element.86, f32[448,3072]{1,0:T(8,128)} %get-tuple-element.120, f32[3072]{0:T(1024)S(1)} %add.263, bf16[448,768]{1,0:T(8,128)(2,1)S(1)} %get-tuple-element.78, bf16[3072,768]{1,0:T(8,128)(2,1)} %get-tuple-element.29), kind=kOutput, calls=%fused_computation.16 | convolution fusion | flops 2137322496 | bytes 19193856 | tf_op jit(solution)/shard_map/pj,ij->pi/dot_general | solution.py:506
  323.7 4.3 fusion.83
  349.6 4.5 fusion.184
  354.5 5.3 %convolution_convert_fusion.1.refs_2_ = bf16[768,3072]{1,0:T(8,128)(2,1)} fusion(bf16[448,3072]{1,0:T(8,128)(2,1)S(1)} %copy-done.56, f32[448,768]{1,0:T(8,128)S(1)} %copy-done.8, f32[448]{0:T(512)S(1)} %fusion.139, f32[448]{0:T(512)S(1)} %broadcast_multiply_fusion, f32[768]{0:T(1024)S(1)} %copy-done.53, f32[768]{0:T(1024)S(1)} %mul.535), kind=kOutput, calls=%fused_computation.60 | convolution fusion | flops 2118008832 | bytes 8857088 | tf_op jit(solution)/shard_map/pi,pj->ij/dot_general | solution.py:554
  361.6 4.1 convolution_convert_fusion.2.refs_0_
  368.0 6.7 %convolution_convert_fusion.refs_3_ = bf16[3072,768]{1,0:T(8,128)(2,1)} fusion(bf16[448,3072]{1,0:T(8,128)(2,1)} %get-tuple-element.85, bf16[448,768]{1,0:T(8,128)(2,1)S(1)} %get-tuple-element.78), kind=kOutput, calls=%fused_computation.59 | convolution fusion | flops 2116288512 | bytes 8159232 | tf_op jit(solution)/shard_map/pi,pj->ij/dot_general | solution.py:553
  374.7 80.8 %ring_reduce.1 = (f32[48,2304]{1,0:T(8,128)}, f32[48,768]{1,0:T(8,128)}, f32[48,3072]{1,0:T(8,128)}, f32[192,768]{1,0:T(8,128)}, f32[16,128]{1,0:T(8,128)}) custom-call(bf16[768,2304]{1,0:T(8,128)(2,1)} %convolution_convert_fusion.2.refs_0_, bf16[768,768]{1,0:T(8,128)(2,1)} %convolution_convert_fusion.3.refs_1_, ...), custom_call_target="tpu_custom_call" | custom-call | tf_op jit(solution)/shard_map/ring_reduce/pallas_call | solution.py:392
  463.3 6.8 %add_convert_fusion.3 = bf16[448,768]{1,0:T(8,128)(2,1)} fusion(f32[448,768]{1,0:T(8,128)} %copy-done.6, bf16[448,3072]{1,0:T(8,128)(2,1)} %get-tuple-element.85, bf16[3072,768]{1,0:T(8,128)(2,1)} %get-tuple-element.29, f32[768]{0:T(1024)S(1)} %copy-done.49), kind=kOutput, calls=%fused_computation.141 | convolution fusion | flops 2114961408 | bytes 9538560 | tf_op jit(solution)/shard_map/dot_general | solution.py:495
  470.2 39.2 %psum.7 = f32[]{:T(128)} all-reduce(f32[]{:T(128)S(6)} %add.287), channel_id=1, replica_groups=mesh['section'=2,'dp'=16] {'section','dp'}, use_global_device_ids=true, to_apply=%region_34.35 | all-reduce | flops 1 | bytes 8 | tf_op jit(solution)/shard_map/psum | solution.py:629
  (268 shorter events, 137.1 us)
Async XLA Ops:
  0.6 93.4 %copy-start.13 = (bf16[2,224,768]{2,1,0:T(8,128)(2,1)S(1)}, bf16[2,224,768]{2,1,0:T(8,128)(2,1)}, u32[]{:S(2)}) copy-start(bf16[2,224,768]{2,1,0:T(8,128)(2,1)} %param.15) | copy-start | bytes 2064388
  94.0 76.4 %copy-start.50 = (f32[768]{0:T(1024)}, f32[768]{0:T(1024)S(1)}, u32[]{:S(2)}) copy-start(f32[768]{0:T(1024)S(1)} %add.250) | copy-start | bytes 9220
  118.2 147.2 %copy-start.14 = (pred[2,224,224]{1,2,0:T(8,128)(4,1)}, pred[2,224,224]{1,2,0:T(8,128)(4,1)S(1)}, u32[]{:S(2)}) copy-start(pred[2,224,224]{1,2,0:T(8,128)(4,1)S(1)} %broadcast_compare_fusion) | copy-start | bytes 301060
  130.4 81.4 %copy-start.52 = (f32[768]{0:T(1024)}, f32[768]{0:T(1024)S(1)}, u32[]{:S(2)}) copy-start(f32[768]{0:T(1024)S(1)} %add.260) | copy-start | bytes 9220
  130.5 20.3 %copy-start.48 = (f32[768]{0:T(1024)}, f32[768]{0:T(1024)S(1)}, u32[]{:S(2)}) copy-start(f32[768]{0:T(1024)S(1)} %add.266) | copy-start | bytes 9220
  150.8 18.9 %collective-permute-start = (bf16[448,768]{1,0:T(8,128)(2,1)}, bf16[448,768]{1,0:T(8,128)(2,1)S(1)}, u32[]{:S(2)}, u32[]{:S(2)}) collective-permute-start(bf16[448,768]{1,0:T(8,128)(2,1)} %fusion.73), channel_id=1, source_target_pairs={{0,16},{1,17},{2,18},{3,19},{4,20},{5,21},{6,22},{7,23},{8,24},{9,... | collective-permute-start | bytes 2064392 | tf_op jit(solution)/shard_map/ppermute | solution.py:617
  211.5 18.3 %copy-start.6 = (f32[448,768]{1,0:T(8,128)}, f32[448,768]{1,0:T(8,128)S(1)}, u32[]{:S(2)}) copy-start(f32[448,768]{1,0:T(8,128)S(1)} %get-tuple-element.119) | copy-start | bytes 4128772
  211.8 18.0 %copy-start.21 = (bf16[2,224,768]{2,1,0:T(8,128)(2,1)S(1)}, bf16[2,224,768]{2,1,0:T(8,128)(2,1)}, u32[]{:S(2)}) copy-start(bf16[2,224,768]{2,1,0:T(8,128)(2,1)} %param.16) | copy-start | bytes 2064388
  249.2 11.9 %slice-start = ((s8[5505024]{0:T(1024)(128)(4,1)}), s8[1310720]{0:T(1024)(128)(4,1)S(1)}, s32[]{:S(2)}) async-start(s8[5505024]{0:T(1024)(128)(4,1)} %bitcast.242), calls=%async_computation | async-start | bytes 2621440
  282.2 30.0 %slice-start.5 = ((s8[4718592]{0:T(1024)(128)(4,1)}), s8[524288]{0:T(1024)(128)(4,1)S(1)}, s32[]{:S(2)}) async-start(s8[4718592]{0:T(1024)(128)(4,1)} %bitcast.257), calls=%async_computation.5 | async-start | bytes 1048576
  282.8 18.9 %collective-permute-start.1 = (bf16[448,768]{1,0:T(8,128)(2,1)S(1)}, bf16[448,768]{1,0:T(8,128)(2,1)}, u32[]{:S(2)}, u32[]{:S(2)}) collective-permute-start(bf16[448,768]{1,0:T(8,128)(2,1)S(1)} %add_convert_fusion.2), channel_id=1, source_target_pairs={{16,0},{17,1},{18,2},{19,3},{20,4},{21,5},{22,6},{23,7},{24,8},{25... | collective-permute-start | bytes 2064392 | tf_op jit(solution)/shard_map/ppermute | solution.py:623
  303.0 65.0 %copy-start.11 = (bf16[448,768]{1,0:T(8,128)(2,1)}, bf16[448,768]{1,0:T(8,128)(2,1)S(1)}, u32[]{:S(2)}) copy-start(bf16[448,768]{1,0:T(8,128)(2,1)S(1)} %get-tuple-element.78) | copy-start | bytes 2064388
  303.0 9.2 %copy-start.7 = (f32[448,768]{1,0:T(8,128)S(1)}, f32[448,768]{1,0:T(8,128)}, u32[]{:S(2)}) copy-start(f32[448,768]{1,0:T(8,128)} %copy-done.6) | copy-start | bytes 4128772
  303.0 9.2 %slice-start.6 = ((s8[4718592]{0:T(1024)(128)(4,1)}), s8[4194304]{0:T(1024)(128)(4,1)S(1)}, s32[]{:S(2)}) async-start(s8[4718592]{0:T(1024)(128)(4,1)} %bitcast.257), calls=%async_computation.6 | async-start | bytes 8388608
  320.6 7.4 %slice-start.2 = ((s8[5505024]{0:T(1024)(128)(4,1)}), s8[1310720]{0:T(1024)(128)(4,1)S(1)}, s32[]{:S(2)}) async-start(s8[5505024]{0:T(1024)(128)(4,1)} %bitcast.244), calls=%async_computation.2 | async-start | bytes 2621440
  354.0 11.7 %copy-start.16 = (f32[448,768]{1,0:T(8,128)}, f32[448,768]{1,0:T(8,128)S(1)}, u32[]{:S(2)}) copy-start(f32[448,768]{1,0:T(8,128)S(1)} %get-tuple-element.130) | copy-start | bytes 4128772
  374.7 88.6 %copy-start.49 = (f32[768]{0:T(1024)S(1)}, f32[768]{0:T(1024)}, u32[]{:S(2)}) copy-start(f32[768]{0:T(1024)} %copy-done.48) | copy-start | bytes 9220
  463.3 46.8 %copy-start.42 = (f32[16,128]{1,0:T(8,128)S(1)}, f32[16,128]{1,0:T(8,128)}, u32[]{:S(2)}) copy-start(f32[16,128]{1,0:T(8,128)} %get-tuple-element.34) | copy-start | bytes 24580
  463.3 46.8 %copy-start.43 = (f32[1,12,48]{2,0,1:T(1,128)S(1)}, f32[1,12,48]{2,0,1:T(1,128)}, u32[]{:S(2)}) copy-start(f32[1,12,48]{2,0,1:T(1,128)} %param.21) | copy-start | bytes 6916
  463.3 46.8 %copy-start.46 = (f32[1,12,48]{2,0,1:T(1,128)S(1)}, f32[1,12,48]{2,0,1:T(1,128)}, u32[]{:S(2)}) copy-start(f32[1,12,48]{2,0,1:T(1,128)} %param.29) | copy-start | bytes 6916
  463.3 46.8 %copy-start.47 = (f32[1,12,48]{2,0,1:T(1,128)S(1)}, f32[1,12,48]{2,0,1:T(1,128)}, u32[]{:S(2)}) copy-start(f32[1,12,48]{2,0,1:T(1,128)} %param.25) | copy-start | bytes 6916
  463.3 48.7 %copy-start.5 = (f32[448,768]{1,0:T(8,128)S(1)}, f32[448,768]{1,0:T(8,128)}, u32[]{:S(2)}) copy-start(f32[448,768]{1,0:T(8,128)} %copy-done.4) | copy-start | bytes 4128772
  463.3 48.7 %copy-start.12 = (bf16[448,768]{1,0:T(8,128)(2,1)S(1)}, bf16[448,768]{1,0:T(8,128)(2,1)}, u32[]{:S(2)}) copy-start(bf16[448,768]{1,0:T(8,128)(2,1)} %copy-done.11) | copy-start | bytes 2064388
  470.2 44.7 %copy-start.23 = (f32[1,192,768]{2,1,0:T(8,128)S(1)}, f32[1,192,768]{2,1,0:T(8,128)}, u32[]{:S(2)}) copy-start(f32[1,192,768]{2,1,0:T(8,128)} %param.20) | copy-start | bytes 1769476
  (42 other events, 177.4 us)

commit v2 on v1

v2 whole, which is shorter than its diff:
```python
from functools import partial

import jax
import jax.numpy as jnp
from jax import lax
from jax.experimental import pallas as pl
from jax.experimental.pallas import tpu as pltpu
from jax.sharding import PartitionSpec as P

HEADS = 12
STEP = 10
LN_EPS = 1e-06
NEG_BIG = -1e30
BETA_ONE = 0.9
BETA_TWO = 0.999
RATE = 0.1
VECTOR_RATE = 0.5
DECAY_RATE = 0.01
ADAM_EPS = 1e-08
MAX_NORM = 1.0
MESH = pl.DeviceIdType.MESH
VMEM_LIMIT = 60 * 2**20
F32 = jnp.float32
BF16 = jnp.bfloat16


class Ring:
    def __init__(self, devices):
        self.devices = devices
        self.chips = devices // 2
        self.reach = self.chips // 2
        self.me = lax.axis_index("dp")
        self.core = self.me % 2
        chip = self.me // 2
        row, column = chip // 2, chip % 2
        self.place = row * (1 - column) + (self.chips - 1 - row) * column

    def device(self, place, core):
        place = (place + 2 * self.chips) % self.chips
        column = place // self.reach
        row = place * (1 - column) + (self.chips - 1 - place) * column
        return (row * 2 + column) * 2 + core

    def target(self, device):
        return (lax.axis_index("section"), device)

    def right(self):
        return self.target(self.device(self.place + 1, self.core))

    def left(self):
        return self.target(self.device(self.place - 1, self.core))

    def sibling(self):
        return self.target(self.device(self.place, 1 - self.core))

    def greet(self):
        barrier = pltpu.get_barrier_semaphore()
        for device in (self.right(), self.left(), self.sibling()):
            pl.semaphore_signal(barrier, inc=1, device_id=device, device_id_type=MESH)
        pl.semaphore_wait(barrier, 3)


def shard_view(ref, device, rows, part=None):
    start = pl.multiple_of(device * rows, rows)
    if part is None:
        return ref.at[pl.ds(start, rows), :]
    columns = ref.shape[1] // 2
    return ref.at[pl.ds(start, rows), pl.ds(part * columns, columns)]


def remote(source, target, send, receive, device):
    return pltpu.make_async_remote_copy(
        src_ref=source,
        dst_ref=target,
        send_sem=send,
        recv_sem=receive,
        device_id=device,
        device_id_type=MESH,
    )


class Gather:
    def __init__(self, ring, whole, rows, halves, send, receive):
        self.ring, self.whole, self.rows, self.halves = ring, whole, rows, halves
        self.send, self.receive = send, receive

    def view(self, distance, core, part=None):
        device = self.ring.device(self.ring.place + distance, core)
        return shard_view(self.whole, device, self.rows, part)

    def hop(self, way, step, came):
        ring = self.ring
        direction = 1 if way == 0 else -1
        part = None
        if step == ring.reach:
            if self.halves:
                part = way
            elif way == 1:
                return None
        view = self.view(-direction * (step if came else step - 1), ring.core, part)
        device = ring.right() if way == 0 else ring.left()
        return remote(view, view, self.send.at[way, step], self.receive.at[way, step], device)

    def push(self, way, step):
        copy = self.hop(way, step, False)
        if copy is not None:
            copy.start()

    def arrive(self, way, step):
        copy = self.hop(way, step, True)
        if copy is not None:
            copy.wait_recv()

    def share(self, distance, key, core):
        view = self.view(distance, core)
        return remote(view, view, self.send.at[2, key], self.receive.at[2, key], self.ring.sibling())

    def shares(self):
        reach = self.ring.reach
        keys = [(0, 0), (reach, reach)]
        for step in range(1, reach):
            keys += [(-step, step), (step, reach + step)]
        return keys

    def begin(self):
        self.push(0, 1)
        self.push(1, 1)
        self.share(0, 0, self.ring.core).start()

    def step(self, step):
        reach, core = self.ring.reach, self.ring.core
        self.arrive(0, step)
        if step < reach:
            self.push(0, step + 1)
        self.arrive(1, step)
        if step < reach:
            self.push(1, step + 1)
            self.share(-step, step, core).start()
            self.share(step, reach + step, core).start()
        else:
            self.share(reach, reach, core).start()

    def finish(self):
        for distance, key in self.shares():
            self.share(distance, key, 1 - self.ring.core).wait_recv()

    def drain(self):
        for distance, key in self.shares():
            self.share(distance, key, self.ring.core).wait_send()
        for step in range(1, self.ring.reach + 1):
            for way in (0, 1):
                copy = self.hop(way, step, False)
                if copy is not None:
                    copy.wait_send()


class Reduce:
    def __init__(self, ring, whole, base, put, other, slots, halves, block, send, receive):
        self.ring, self.whole, self.base, self.put, self.other, self.slots = ring, whole, base, put, other, slots
        self.rows, self.halves, self.block = other.shape[1], halves, block
        self.send, self.receive = send, receive

    def row(self, distance, core):
        device = self.ring.device(self.ring.place + distance, core)
        return pl.multiple_of(self.base + device * self.rows, 16)

    def view(self, distance, core, part=None):
        rows = pl.ds(self.row(distance, core), self.rows)
        if part is None:
            return self.whole.at[rows, :]
        columns = self.whole.shape[1] // 2
        return self.whole.at[rows, pl.ds(part * columns, columns)]

    def keys(self):
        reach = self.ring.reach
        order = [(reach, reach)]
        for distance in range(reach - 1, 0, -1):
            order += [(distance, reach + distance), (-distance, distance)]
        return order + [(0, 0)]

    def swap(self, distance, key):
        return remote(
            self.view(distance, 1 - self.ring.core),
            self.other.at[key],
            self.send.at[2, key],
            self.receive.at[2, key],
            self.ring.sibling(),
        )

    def exchange(self):
        for distance, key in self.keys():
            self.swap(distance, key).start()

    def exchanged(self, key):
        slot = self.other.at[key]
        remote(
            slot, slot, self.send.at[2, key], self.receive.at[2, key], self.ring.sibling()
        ).wait_recv()

    def slot(self, way, distance):
        ref = self.slots.at[way, distance - 1]
        if distance == self.ring.reach and self.halves:
            columns = ref.shape[1] // 2
            return ref.at[:, pl.ds(way * columns, columns)]
        return ref

    def hop(self, way, distance, came):
        ring = self.ring
        if distance == ring.reach and not self.halves and way == 1:
            return None
        slot = self.slot(way, distance)
        source = slot
        if not came:
            part = way if distance == ring.reach and self.halves else None
            source = self.view(distance if way == 0 else -distance, ring.core, part)
        device = ring.right() if way == 0 else ring.left()
        return remote(
            source, slot, self.send.at[way, distance], self.receive.at[way, distance], device
        )

    def push(self, way, distance):
        copy = self.hop(way, distance, False)
        if copy is not None:
            copy.start()

    def arrive(self, way, distance):
        copy = self.hop(way, distance, True)
        if copy is not None:
            copy.wait_recv()

    def add(self, distance, key, arrivals, final=False):
        ring = self.ring
        base = self.row(distance, ring.core)
        block = self.block
        half = self.whole.shape[1] // 2

        def body(index, _):
            here = pl.ds(pl.multiple_of(base + index * block, 16), block)
            rows = pl.ds(pl.multiple_of(index * block, block), block)
            total = self.whole[here, :].astype(F32) + self.other[key, rows, :].astype(F32)
            for way, far in arrivals:
                if far == ring.reach and self.halves:
                    low, high = total[:, :half], total[:, half:]
                    if way == 0:
                        low = low + self.slots[way, far - 1, rows, :half].astype(F32)
                    else:
                        high = high + self.slots[way, far - 1, rows, half:].astype(F32)
                    total = jnp.concatenate([low, high], axis=1)
                elif far < ring.reach or way == 0:
                    total = total + self.slots[way, far - 1, rows, :].astype(F32)
            if final:
                self.put(rows, total)
            else:
                self.whole[here, :] = total.astype(self.whole.dtype)
            return 0

        lax.fori_loop(0, self.rows // block, body, 0)

    def first(self):
        reach = self.ring.reach
        self.exchanged(reach)
        self.add(reach, reach, [])
        self.push(0, reach)
        self.push(1, reach)

    def step(self, distance):
        reach = self.ring.reach
        self.exchanged(reach + distance)
        self.arrive(0, distance + 1)
        self.add(distance, reach + distance, [(0, distance + 1)])
        self.push(0, distance)
        self.exchanged(distance)
        self.arrive(1, distance + 1)
        self.add(-distance, distance, [(1, distance + 1)])
        self.push(1, distance)

    def last(self):
        self.exchanged(0)
        self.arrive(0, 1)
        self.arrive(1, 1)
        self.add(0, 0, [(0, 1), (1, 1)], True)

    def drain(self):
        for distance, key in self.keys():
            self.swap(distance, key).wait_send()
        for distance in range(1, self.ring.reach + 1):
            for way in (0, 1):
                copy = self.hop(way, distance, False)
                if copy is not None:
                    copy.wait_send()


def dot_nn(a, b):
    return lax.dot_general(a, b, (((1,), (0,)), ((), ())), preferred_element_type=F32)


def dot_nt(a, b):
    return lax.dot_general(a, b, (((1,), (1,)), ((), ())), preferred_element_type=F32)


def dot_tn(a, b):
    return lax.dot_general(a, b, (((0,), (0,)), ((), ())), preferred_element_type=F32)


def erf(value):
    bound = 3.832506856900711
    value = jnp.clip(value, -bound, bound)
    square = value * value
    top = 0.00022905065861350646
    for factor in (
        0.0034082910107109506,
        0.050955695062380861,
        0.18520832239976145,
        1.128379143519084,
    ):
        top = top * square + factor
    bottom = -1.1791602954361697e-7
    for factor in (
        0.000023547966471313185,
        0.0010179625278914885,
        0.014070470171167667,
        0.11098505178285362,
        0.49746925110067538,
        1.0,
    ):
        bottom = bottom * square + factor
    return value * top / bottom


def norm_parts(features):
    center = jnp.mean(features, axis=-1, keepdims=True)
    centered = features - center
    spread = jnp.mean(centered * centered, axis=-1, keepdims=True)
    scale = lax.rsqrt(spread + LN_EPS)
    return centered * scale, scale


def norm_back(z, scale, e, gain):
    t = e * gain
    return (
        t - jnp.mean(t, axis=-1, keepdims=True) - z * jnp.mean(t * z, axis=-1, keepdims=True)
    ) * scale


def column_sum(value):
    return jnp.sum(value, axis=0, keepdims=True)


def layer_kernel(
    devices,
    sections,
    tokens,
    cotangent,
    crops,
    own_attn,
    own_up,
    own_down,
    own_vec,
    boundary,
    input_grads,
    sum_attn,
    sum_up,
    sum_down,
    sum_vec,
    norm,
    w_qkv,
    w_out,
    w_up,
    w_down,
    tiles,
    params,
    x_in,
    hidden,
    qkv,
    log_total,
    mixed,
    middle,
    hidden_two,
    slope,
    active,
    mask,
    dy_in,
    grad_up,
    grad_branch,
    grad_heads,
    grad_qkv,
    flow,
    flow_two,
    vec_sums,
    vec_tiles,
    g_down,
    other_down,
    other_up,
    other_attn,
    other_vec,
    slots_down,
    slots_up,
    slots_attn,
    slots_vec,
    norm_slots,
    local,
    send,
    receive,
    across,
    norm_sem,
):
    section = lax.axis_index("section")
    first_section = section == 0
    last_section = section == 1
    ring = Ring(devices)
    me = ring.me
    micro_count, pack = tokens.shape[0], tokens.shape[1]
    width = tokens.shape[2]
    hidden_units = w_up.shape[1]
    tiles_up = hidden_units // width
    head_width = width // HEADS
    pairs = HEADS // 2
    pair_width = 2 * head_width
    head_scale = head_width ** (-0.5)
    vec_rows, vec_columns = own_vec.shape[1], own_vec.shape[2]

    def rows_of(micro):
        return pl.ds(pl.multiple_of(micro * pack, 16), pack)

    def lanes(start, count):
        return pl.ds(pl.multiple_of(start, 128), count)


    stage_attn = slope.at[pl.ds(0, own_attn.shape[1]), :]
    stage_up = slope.at[pl.ds(own_attn.shape[1], own_up.shape[1]), :]
    stage_down = middle.at[pl.ds(0, own_down.shape[1]), :]
    loads = [
        pltpu.make_async_copy(own_attn.at[0], stage_attn, local.at[0]),
        pltpu.make_async_copy(own_up.at[0], stage_up, local.at[1]),
        pltpu.make_async_copy(own_down.at[0], stage_down, local.at[2]),
    ]
    for load in loads:
        load.start()

    def load_tokens(micro):
        return pltpu.make_async_copy(tokens.at[micro], x_in.at[rows_of(micro), :], local.at[3 + micro])

    def load_cotangent(micro):
        return pltpu.make_async_copy(
            cotangent.at[micro], dy_in.at[rows_of(micro), :], local.at[3 + micro]
        )

    @pl.when(first_section)
    def _():
        for micro in range(micro_count):
            load_tokens(micro).start()

    @pl.when(last_section)
    def _():
        for micro in range(micro_count):
            load_cotangent(micro).start()

    total_devices = sections * devices
    flat = section * devices + me

    def other_device(distance):
        other = (flat + distance) % total_devices
        return (other // devices, other % devices)

    barrier = pltpu.get_barrier_semaphore()

    def greet(distance, _):
        pl.semaphore_signal(
            barrier, inc=1, device_id=other_device(distance), device_id_type=MESH
        )
        return 0

    lax.fori_loop(1, total_devices, greet, 0)

    vec_tiles[...] = jnp.zeros_like(vec_tiles)
    vec_tiles[0:vec_rows, 0:vec_columns] = own_vec[0]
    tiles[pl.ds(pl.multiple_of(me * 16, 16), 16), :] = vec_tiles[0:16, :].astype(BF16)
    vec_sums[...] = jnp.zeros_like(vec_sums)
    log_total[...] = jnp.zeros_like(log_total)
    for load in loads:
        load.wait()
    count = own_attn.shape[1]
    here = pl.ds(pl.multiple_of(me * count, 16), count)
    w_qkv[here, :] = stage_attn[:, : 3 * width].astype(BF16)
    w_out[here, :] = stage_attn[:, 3 * width :].astype(BF16)
    count = own_up.shape[1]
    w_up[pl.ds(pl.multiple_of(me * count, 16), count), :] = stage_up[...].astype(BF16)
    count = own_down.shape[1]
    w_down[pl.ds(pl.multiple_of(me * count, 16), count), :] = stage_down[...].astype(BF16)

    pl.semaphore_wait(barrier, total_devices - 1)


    def gather_of(index, whole, rows, halves=True):
        return Gather(ring, whole, rows, halves, send.at[index], receive.at[index])

    get_vec = gather_of(0, tiles, 16, False)
    get_qkv = gather_of(1, w_qkv, own_attn.shape[1])
    get_out = gather_of(2, w_out, own_attn.shape[1])
    get_up = gather_of(3, w_up, own_up.shape[1])
    get_down = gather_of(4, w_down, own_down.shape[1])

    reach = ring.reach
    for gather in (get_vec, get_qkv, get_out):
        gather.begin()
    for step in range(1, reach + 1):
        for gather in (get_vec, get_qkv, get_out):
            gather.step(step)
        if step == reach // 2:
            get_up.begin()
    get_up.step(1)
    get_down.begin()
    for gather in (get_vec, get_qkv, get_out):
        gather.finish()

    late = []
    for step in range(2, reach + 1):
        late.append(partial(get_up.step, step))
        late.append(partial(get_down.step, step - 1))
    late.append(get_up.finish)
    late_down = [partial(get_down.step, reach), get_down.finish]

    @pl.when(last_section)
    def _():
        for call in late + late_down:
            call()

    for device in range(devices):
        params[:, device * vec_columns : (device + 1) * vec_columns] = tiles[
            device * 16 : (device + 1) * 16, 0:vec_columns
        ].astype(F32)


    for micro in range(micro_count):
        row = crops[micro : micro + 1, :].astype(F32)
        square = jnp.broadcast_to(row, (pack, pack))
        mask[micro] = jnp.where(square == square.T, 1.0, 0.0)

    lane = lax.broadcasted_iota(jnp.int32, (1, pair_width), 1)
    in_low = lane < head_width

    def of_head(value, sub):
        return jnp.where(in_low if sub == 0 else ~in_low, value, jnp.zeros_like(value))

    def forward_micro(micro, serve):
        here = rows_of(micro)
        inputs = x_in[here, :].astype(F32)
        z, _ = norm_parts(inputs)
        hidden[here, :] = (z * params[0:1, :] + params[1:2, :]).astype(BF16)
        for part in range(3):
            value = dot_nn(hidden[here, :], w_qkv[:, part * width : (part + 1) * width])
            if part == 0:
                value = value + params[2:3, :]
            if part == 2:
                value = value + params[3:4, :]
            qkv[here, part * width : (part + 1) * width] = value.astype(BF16)
        serve(0)

        def pair(index, _):
            at = index * pair_width
            queries = qkv[here, lanes(at, pair_width)]
            keys = qkv[here, lanes(width + at, pair_width)]
            values = qkv[here, lanes(2 * width + at, pair_width)]
            outs = []
            logs = log_total[here, :]
            head_lane = lax.broadcasted_iota(jnp.int32, (1, 128), 1)
            for sub in range(2):
                scores = dot_nt(of_head(queries, sub), keys) * head_scale
                scores = jnp.where(mask[micro] > 0.5, scores, NEG_BIG)
                peak = jnp.max(scores, axis=-1, keepdims=True)
                exponent = jnp.exp(scores - peak)
                totals = jnp.sum(exponent, axis=-1, keepdims=True)
                probs = (exponent * (1.0 / totals)).astype(BF16)
                logs = jnp.where(head_lane == 2 * index + sub, peak + jnp.log(totals), logs)
                outs.append(dot_nn(probs, values))
            log_total[here, :] = logs
            mixed[here, lanes(at, pair_width)] = jnp.where(in_low, outs[0], outs[1]).astype(BF16)
            return 0

        lax.fori_loop(0, pairs, pair, 0)
        serve(1)
        middle_value = x_in[here, :].astype(F32) + (
            dot_nn(mixed[here, :], w_out[...]) + params[4:5, :]
        )
        middle[here, :] = middle_value
        z, _ = norm_parts(middle_value)
        hidden_two[here, :] = (z * params[5:6, :] + params[6:7, :]).astype(BF16)
        serve(2)
        for part in range(tiles_up):
            columns = slice(part * width, (part + 1) * width)
            upward = dot_nn(hidden_two[here, :], w_up[:, columns]) + params[8 + part : 9 + part, :]
            half = 0.5 + 0.5 * erf(upward * 0.7071067811865476)
            active[here, columns] = (upward * half).astype(BF16)
            slope[here, columns] = half + upward * (
                jnp.exp(-0.5 * upward * upward) * 0.3989422804014327
            )
        serve(3)

    def hand_over(source, target, micro):
        here = rows_of(micro)
        return remote(
            source.at[micro],
            target.at[here, :],
            across.at[0, micro],
            across.at[1, micro],
            (1 - section, me),
        )

    def forward_step(micro, _):
        @pl.when(last_section)
        def _():
            hand_over(boundary, x_in, micro).wait_recv()

        @pl.when(first_section)
        def _():
            load_tokens(micro).wait()

        def serve(point):
            @pl.when(first_section & (micro == 0))
            def _():
                split = [late[0:2], late[2:4], late[4:], []]
                for call in split[point]:
                    call()

        forward_micro(micro, serve)
        return 0

    lax.fori_loop(0, micro_count, forward_step, 0)

    @pl.when(first_section)
    def _():
        for call in late_down:
            call()

    def finish_step(micro, _):
        here = rows_of(micro)
        output = middle[here, :] + (dot_nn(active[here, :], w_down[...]) + params[7:8, :])
        boundary[micro] = output.astype(BF16)

        @pl.when(first_section)
        def _():
            hand_over(boundary, x_in, micro).start()

        return 0

    lax.fori_loop(0, micro_count, finish_step, 0)
    for gather in (get_vec, get_qkv, get_out, get_up, get_down):
        gather.drain()


    def into(ref, first):
        def put(rows, value):
            ref[rows, pl.ds(first, value.shape[1])] = value

        return put

    def reduce_of(index, whole, base, put, other, slots, halves=True, block=16):
        return Reduce(
            ring, whole, base, put, other, slots, halves, block, send.at[index], receive.at[index]
        )

    put_down = reduce_of(5, g_down, 0, into(sum_down, 0), other_down, slots_down, block=64)
    put_up = reduce_of(6, w_up, 0, into(sum_up, 0), other_up, slots_up)
    put_attn = [
        reduce_of(
            7 + part,
            w_down,
            part * width,
            into(sum_attn, part * width),
            other_attn.at[part],
            slots_attn.at[part],
            block=other_attn.shape[2],
        )
        for part in range(4)
    ]
    put_vec = reduce_of(11, vec_tiles, 0, into(sum_vec, 0), other_vec, slots_vec, False)

    def weigh_down():
        chunk = 2 * own_down.shape[1]

        def body(index, _):
            columns = lanes(index * chunk, chunk)
            g_down[pl.ds(pl.multiple_of(index * chunk, 16), chunk), :] = dot_tn(
                active[:, columns], dy_in[...]
            ).astype(BF16)
            return 0

        lax.fori_loop(0, hidden_units // chunk, body, 0)

    def add_vec(row, value):
        vec_sums[row : row + 1, :] += value

    def backward_micro(micro, serve):
        here = rows_of(micro)
        add_vec(7, column_sum(dy_in[here, :].astype(F32)))
        for part in range(tiles_up):
            columns = slice(part * width, (part + 1) * width)
            back = dot_nt(dy_in[here, :], w_down[columns, :]) * slope[here, columns]
            back = back.astype(BF16)
            grad_up[here, columns] = back
            add_vec(8 + part, column_sum(back.astype(F32)))
            more = dot_nt(back, w_up[:, columns])
            if part == 0:
                flow[...] = more
            else:
                flow[...] += more
        serve(0)
        e = flow[...]
        z, scale = norm_parts(middle[here, :])
        add_vec(5, column_sum(e * z))
        add_vec(6, column_sum(e))
        back = dy_in[here, :].astype(F32) + norm_back(z, scale, e, params[5:6, :])
        flow_two[...] = back
        back = back.astype(BF16)
        grad_branch[here, :] = back
        add_vec(4, column_sum(back.astype(F32)))
        grad_heads[...] = dot_nt(back, w_out[...]).astype(BF16)
        serve(1)

        def pair(index, _):
            at = index * pair_width
            queries = qkv[here, lanes(at, pair_width)]
            keys = qkv[here, lanes(width + at, pair_width)]
            values = qkv[here, lanes(2 * width + at, pair_width)]
            back_out = grad_heads[:, lanes(at, pair_width)]
            head_lane = lax.broadcasted_iota(jnp.int32, (1, 128), 1)
            results = []
            for sub in range(2):
                scores = dot_nt(of_head(queries, sub), keys) * head_scale
                scores = jnp.where(mask[micro] > 0.5, scores, NEG_BIG)
                logs = jnp.sum(
                    jnp.where(head_lane == 2 * index + sub, log_total[here, :], 0.0),
                    axis=-1,
                    keepdims=True,
                )
                probs = jnp.exp(scores - logs)
                back_probs = dot_nt(of_head(back_out, sub), values)
                inner = jnp.sum(back_probs * probs, axis=-1, keepdims=True)
                back_scores = (probs * (back_probs - inner)).astype(BF16)
                results.append(
                    (
                        dot_nn(back_scores, keys) * head_scale,
                        dot_tn(back_scores, queries) * head_scale,
                        dot_tn(probs.astype(BF16), back_out),
                    )
                )
            for part in range(3):
                grad_qkv[here, lanes(part * width + at, pair_width)] = jnp.where(
                    in_low, results[0][part], results[1][part]
                ).astype(BF16)
            return 0

        lax.fori_loop(0, pairs, pair, 0)
        serve(2)
        e = dot_nt(grad_qkv[here, :], w_qkv[...])
        z, scale = norm_parts(x_in[here, :].astype(F32))
        add_vec(0, column_sum(e * z))
        add_vec(1, column_sum(e))
        add_vec(2, column_sum(grad_qkv[here, 0:width].astype(F32)))
        add_vec(3, column_sum(grad_qkv[here, 2 * width : 3 * width].astype(F32)))
        back = flow_two[...] + norm_back(z, scale, e, params[0:1, :])
        input_grads[micro] = back.astype(BF16)
        serve(3)

    def backward_step(micro, _):
        @pl.when(first_section)
        def _():
            hand_over(input_grads, dy_in, micro).wait_recv()

        @pl.when(last_section)
        def _():
            load_cotangent(micro).wait()

        is_last = micro == micro_count - 1

        def serve(point):
            @pl.when(first_section & is_last)
            def _():
                if point == 0:
                    put_down.step(reach - 1)
                if point == 2:
                    put_down.step(reach - 2)

        @pl.when(first_section & is_last)
        def _():
            weigh_down()
            put_down.exchange()
            put_down.first()

        backward_micro(micro, serve)

        @pl.when(last_section)
        def _():
            hand_over(input_grads, dy_in, micro).start()

        return 0

    lax.fori_loop(0, micro_count, backward_step, 0)

    @pl.when(last_section)
    def _():
        weigh_down()
        put_down.exchange()
        put_down.first()

    third = width // 3

    def weigh(source, grad, columns, target, base):
        def body(index, _):
            rows = lanes(index * third, third)
            target[pl.ds(pl.multiple_of(base + index * third, 16), third), :] = dot_tn(
                source[:, rows], grad[:, columns]
            ).astype(BF16)
            return 0

        lax.fori_loop(0, 3, body, 0)

    weigh(hidden_two, grad_up, slice(0, hidden_units), w_up, 0)
    put_up.exchange()

    @pl.when(last_section)
    def _():
        put_down.step(reach - 1)

    put_up.first()
    for part in range(3):
        weigh(hidden, grad_qkv, slice(part * width, (part + 1) * width), w_down, part * width)
        put_attn[part].exchange()
    weigh(mixed, grad_branch, slice(0, width), w_down, 3 * width)
    put_attn[3].exchange()

    vec_tiles[...] = jnp.zeros_like(vec_tiles)
    for device in range(devices):
        vec_tiles[device * 16 : (device + 1) * 16, 0:vec_columns] = vec_sums[
            :, device * vec_columns : (device + 1) * vec_columns
        ]
    put_vec.exchange()

    @pl.when(last_section)
    def _():
        put_down.step(reach - 2)

    put_up.step(reach - 1)
    put_vec.first()
    for part in range(4):
        put_attn[part].first()
    for distance in range(reach - 3, 0, -1):
        put_down.step(distance)
    put_up.step(reach - 2)
    for part in range(4):
        put_attn[part].step(reach - 1)
    put_vec.step(reach - 1)
    put_down.last()
    for distance in range(reach - 3, 0, -1):
        put_up.step(distance)
    for distance in range(reach - 2, 0, -1):
        for part in range(4):
            put_attn[part].step(distance)
        put_vec.step(distance)
        if distance == reach - 2:
            put_up.last()
    for part in range(4):
        put_attn[part].last()
    put_vec.last()


    def squares(ref):
        value = ref[...]
        value = value * value
        while value.shape[1] > 128:
            value = sum(
                value[:, start : start + 128] for start in range(0, value.shape[1], 128)
            )
        return sum(value[start : start + 8, :] for start in range(0, value.shape[0], 8))

    norm_slots[0] = squares(sum_attn) + squares(sum_up) + squares(sum_down) + squares(sum_vec)

    def tell(distance, _):
        remote(
            norm_slots.at[0],
            norm_slots.at[distance],
            norm_sem.at[0],
            norm_sem.at[1],
            other_device(distance),
        ).start()
        return 0

    lax.fori_loop(1, total_devices, tell, 0)
    rest = norm_slots.at[pl.ds(1, total_devices - 1)]
    heard = remote(rest, rest, norm_sem.at[0], norm_sem.at[1], other_device(1))
    heard.wait_recv()
    order = jnp.zeros(norm_slots.shape[1:], F32)

    def gather_up(device, order):
        return order + norm_slots[(flat - device + total_devices) % total_devices]

    order = lax.fori_loop(0, total_devices, gather_up, order)
    total = jnp.sum(jnp.sum(order, axis=0, keepdims=True), axis=1, keepdims=True)
    norm[...] = jnp.broadcast_to(jnp.sqrt(total), norm.shape)
    heard.wait_send()


    put_down.drain()
    put_up.drain()
    for part in range(4):
        put_attn[part].drain()
    put_vec.drain()
    for micro in range(micro_count):

        @pl.when(first_section)
        def _():
            hand_over(boundary, x_in, micro).wait_send()

        @pl.when(last_section)
        def _():
            hand_over(input_grads, dy_in, micro).wait_send()


def run_layers(devices, sections, tokens, cotangent, crop_ids, attn, upward_w, downward_w, vectors):
    micro_count, pack, width = tokens.shape
    rows = micro_count * pack
    chips, reach = devices // 2, devices // 4
    hidden_units = upward_w.shape[2]
    attn_rows, up_rows, down_rows = attn.shape[1], upward_w.shape[1], downward_w.shape[1]
    in_hbm = pl.BlockSpec(memory_space=pl.ANY)
    in_vmem = pl.BlockSpec(memory_space=pltpu.VMEM)

    def other(rows_of_shard, columns, kind=BF16):
        return pltpu.VMEM((chips, rows_of_shard, columns), kind)

    def slots(rows_of_shard, columns, kind=BF16):
        return pltpu.VMEM((2, reach, rows_of_shard, columns), kind)

    scratch = [
        pltpu.VMEM((width, 3 * width), BF16),
        pltpu.VMEM((width, width), BF16),
        pltpu.VMEM((width, hidden_units), BF16),
        pltpu.VMEM((hidden_units, width), BF16),
        pltpu.VMEM((devices * 16, 128), BF16),
        pltpu.VMEM((16, width), F32),
        pltpu.VMEM((rows, width), BF16),
        pltpu.VMEM((rows, width), BF16),
        pltpu.VMEM((rows, 3 * width), BF16),
        pltpu.VMEM((rows, 128), F32),
        pltpu.VMEM((rows, width), BF16),
        pltpu.VMEM((rows, width), F32),
        pltpu.VMEM((rows, width), BF16),
        pltpu.VMEM((rows, hidden_units), F32),
        pltpu.VMEM((rows, hidden_units), BF16),
        pltpu.VMEM((micro_count, pack, pack), F32),
        pltpu.VMEM((rows, width), BF16),
        pltpu.VMEM((rows, hidden_units), BF16),
        pltpu.VMEM((rows, width), BF16),
        pltpu.VMEM((pack, width), BF16),
        pltpu.VMEM((rows, 3 * width), BF16),
        pltpu.VMEM((pack, width), F32),
        pltpu.VMEM((pack, width), F32),
        pltpu.VMEM((16, width), F32),
        pltpu.VMEM((devices * 16, 128), F32),
        pltpu.VMEM((hidden_units, width), BF16),
        other(down_rows, width),
        other(up_rows, hidden_units),
        pltpu.VMEM((4, chips, attn_rows, width), BF16),
        other(16, 128, F32),
        slots(down_rows, width),
        slots(up_rows, hidden_units),
        pltpu.VMEM((4, 2, reach, attn_rows, width), BF16),
        slots(16, 128, F32),
        pltpu.VMEM((sections * devices, 8, 128), F32),
        pltpu.SemaphoreType.DMA((3 + micro_count,)),
        pltpu.SemaphoreType.DMA((12, 3, 2 * reach)),
        pltpu.SemaphoreType.DMA((12, 3, 2 * reach)),
        pltpu.SemaphoreType.DMA((2, micro_count)),
        pltpu.SemaphoreType.DMA((2,)),
    ]
    return pl.pallas_call(
        partial(layer_kernel, devices, sections),
        out_shape=[
            jax.ShapeDtypeStruct(tokens.shape, BF16),
            jax.ShapeDtypeStruct(tokens.shape, BF16),
            jax.ShapeDtypeStruct(attn.shape[1:], F32),
            jax.ShapeDtypeStruct(upward_w.shape[1:], F32),
            jax.ShapeDtypeStruct(downward_w.shape[1:], F32),
            jax.ShapeDtypeStruct((16, 128), F32),
            jax.ShapeDtypeStruct((8, 128), F32),
        ],
        in_specs=[in_hbm, in_hbm, in_vmem, in_hbm, in_hbm, in_hbm, in_vmem],
        out_specs=[in_vmem] * 7,
        scratch_shapes=scratch,
        compiler_params=pltpu.CompilerParams(
            collective_id=0, has_side_effects=True, vmem_limit_bytes=VMEM_LIMIT
        ),
        name="two_layers",
    )(tokens, cotangent, crop_ids, attn, upward_w, downward_w, vectors)


def adam_kernel(norm, *refs):
    grads, states, results = refs[:4], refs[4:16], refs[16:28]
    clip_factor = jnp.minimum(1.0, MAX_NORM / (norm[0:1, 0:1] + 1e-06))
    for index in range(4):
        master, moment_one, moment_two = (states[index + 4 * part] for part in range(3))
        shape = master.shape[1:]
        gradient = grads[index][0 : shape[0], 0 : shape[1]] * clip_factor
        decay, rate = (0.0, VECTOR_RATE) if index == 3 else (DECAY_RATE, RATE)
        updated = adam_update(master[0], gradient, moment_one[0], moment_two[0], decay, rate)
        for part in range(3):
            results[index + 4 * part][0] = updated[part]


def run_adam(norm, grads, states):
    steps = 3

    def cut(shape):
        block = shape[:-2] + (shape[-2] // steps, shape[-1])
        lead = (0,) * (len(shape) - 2)
        return pl.BlockSpec(block, lambda i: lead + (i, 0))

    def keep(shape):
        lead = (0,) * len(shape)
        return pl.BlockSpec(shape, lambda i: lead)

    def spec(index, array):
        return keep(array.shape) if index % 4 == 3 else cut(array.shape)

    state_specs = [spec(i, a) for i, a in enumerate(states)]
    return pl.pallas_call(
        adam_kernel,
        grid=(steps,),
        out_shape=[jax.ShapeDtypeStruct(a.shape, F32) for a in states],
        in_specs=[keep(norm.shape)] + [spec(i, a) for i, a in enumerate(grads)] + state_specs,
        out_specs=state_specs,
        compiler_params=pltpu.CompilerParams(vmem_limit_bytes=VMEM_LIMIT),
        name="adam",
    )(norm, *grads, *states)


def layer_norm(features, gain_row, shift_row):
    center = jnp.mean(features, axis=-1, keepdims=True)
    centered = features - center
    spread = jnp.mean(centered * centered, axis=-1, keepdims=True)
    return centered * lax.rsqrt(spread + LN_EPS) * gain_row + shift_row


def split_heads(packed, micro_count, model_width):
    shaped = packed.reshape(micro_count, -1, 3, HEADS, model_width // HEADS)
    return (shaped[:, :, 0], shaped[:, :, 1], shaped[:, :, 2])


def attention_scores(queries, keys_block, crop_rows):
    head_scale = queries.shape[-1] ** (-0.5)
    scores = (
        jnp.einsum("mqhd,mkhd->mhqk", queries, keys_block, preferred_element_type=F32) * head_scale
    )
    same_crop = crop_rows[:, :, None] == crop_rows[:, None, :]
    return jnp.where(same_crop[:, None], scores, NEG_BIG)


def forward_layer(inputs, crop_rows, weights):
    attn, upward_w, downward_w, vectors_b = weights
    model_width = attn.shape[0]
    rows = inputs.shape[0]
    params = vectors_b.astype(F32)
    hidden = layer_norm(inputs, params[0], params[1]).astype(BF16)
    qkv_bias = jnp.concatenate([params[2], jnp.zeros_like(params[2]), params[3]])
    packed = (
        jnp.dot(hidden, attn[:, : 3 * model_width], preferred_element_type=F32) + qkv_bias
    ).astype(BF16)
    queries, keys_block, values_block = split_heads(packed, crop_rows.shape[0], model_width)
    scores = attention_scores(queries, keys_block, crop_rows)
    row_peak = jnp.max(scores, axis=-1, keepdims=True)
    exponent = jnp.exp(scores - row_peak)
    totals = jnp.sum(exponent, axis=-1, keepdims=True)
    soft_weights = (exponent / totals).astype(BF16)
    log_total = row_peak + jnp.log(totals)
    mixed = jnp.einsum("mhqk,mkhd->mqhd", soft_weights, values_block, preferred_element_type=F32)
    mixed = mixed.reshape(rows, model_width).astype(BF16)
    middle = inputs + (
        jnp.dot(mixed, attn[:, 3 * model_width :], preferred_element_type=F32) + params[4]
    )
    hidden_two = layer_norm(middle, params[5], params[6]).astype(BF16)
    upward = jnp.dot(hidden_two, upward_w, preferred_element_type=F32) + params[8:].reshape(-1)
    active = jax.nn.gelu(upward, approximate=False).astype(BF16)
    output = middle + (jnp.dot(active, downward_w, preferred_element_type=F32) + params[7])
    return (output, (inputs, hidden, packed, log_total, mixed, middle, hidden_two, upward, active))


def backward_layer(kept, crop_rows, grad_out, weights, with_grads):
    attn, upward_w, downward_w, vectors_b = weights
    inputs, hidden, packed, log_total, mixed, middle, hidden_two, upward, active = kept
    model_width = attn.shape[0]
    rows = inputs.shape[0]
    params = vectors_b.astype(F32)
    grad_down = grad_out.astype(BF16)
    grad_active = jnp.einsum("pj,ij->pi", grad_down, downward_w, preferred_element_type=F32)
    gelu_back = jax.vjp(partial(jax.nn.gelu, approximate=False), upward)[1]
    grad_up = gelu_back(grad_active)[0].astype(BF16)
    grad_hidden_two = jnp.einsum("pj,ij->pi", grad_up, upward_w, preferred_element_type=F32)
    norm_back_two = jax.vjp(layer_norm, middle, params[5], params[6])[1]
    grad_middle_part, grad_gain_two, grad_shift_two = norm_back_two(grad_hidden_two)
    grad_middle = grad_out + grad_middle_part
    grad_branch = grad_middle.astype(BF16)
    grad_mixed = jnp.einsum(
        "pj,ij->pi", grad_branch, attn[:, 3 * model_width :], preferred_element_type=F32
    ).astype(BF16)
    micro_count = crop_rows.shape[0]
    queries, keys_block, values_block = split_heads(packed, micro_count, model_width)
    scores = attention_scores(queries, keys_block, crop_rows)
    probs = jnp.exp(scores - log_total)
    grad_heads = grad_mixed.reshape(micro_count, -1, HEADS, model_width // HEADS)
    grad_probs = jnp.einsum("mqhd,mkhd->mhqk", grad_heads, values_block, preferred_element_type=F32)
    grad_values = jnp.einsum(
        "mhqk,mqhd->mkhd", probs.astype(BF16), grad_heads, preferred_element_type=F32
    )
    grad_scores = (
        probs * (grad_probs - jnp.sum(grad_probs * probs, axis=-1, keepdims=True))
    ).astype(BF16)
    head_scale = queries.shape[-1] ** (-0.5)
    grad_queries = (
        jnp.einsum("mhqk,mkhd->mqhd", grad_scores, keys_block, preferred_element_type=F32)
        * head_scale
    )
    grad_keys = (
        jnp.einsum("mhqk,mqhd->mkhd", grad_scores, queries, preferred_element_type=F32) * head_scale
    )
    grad_packed = jnp.concatenate(
        [
            grad_queries.reshape(rows, model_width),
            grad_keys.reshape(rows, model_width),
            grad_values.reshape(rows, model_width),
        ],
        axis=1,
    ).astype(BF16)
    grad_hidden = jnp.einsum(
        "pj,ij->pi", grad_packed, attn[:, : 3 * model_width], preferred_element_type=F32
    )
    norm_back_one = jax.vjp(layer_norm, inputs, params[0], params[1])[1]
    grad_in_part, grad_gain_one, grad_shift_one = norm_back_one(grad_hidden)
    grad_inputs = grad_middle + grad_in_part
    if not with_grads:
        return (grad_inputs, None)
    grad_w_down = jnp.einsum("pi,pj->ij", active, grad_down, preferred_element_type=F32)
    grad_w_up = jnp.einsum("pi,pj->ij", hidden_two, grad_up, preferred_element_type=F32)
    grad_w_out = jnp.einsum("pi,pj->ij", mixed, grad_branch, preferred_element_type=F32)
    grad_w_qkv = jnp.einsum("pi,pj->ij", hidden, grad_packed, preferred_element_type=F32)
    packed_sums = jnp.sum(grad_packed, axis=0, dtype=F32)
    vector_rows = jnp.stack(
        [
            grad_gain_one,
            grad_shift_one,
            packed_sums[:model_width],
            packed_sums[2 * model_width :],
            jnp.sum(grad_branch, axis=0, dtype=F32),
            grad_gain_two,
            grad_shift_two,
            jnp.sum(grad_down, axis=0, dtype=F32),
        ]
    )
    up_bias_rows = jnp.sum(grad_up, axis=0, dtype=F32).reshape(-1, model_width)
    grad_vectors = jnp.concatenate([vector_rows, up_bias_rows], axis=0)
    grad_attn = jnp.concatenate([grad_w_qkv, grad_w_out], axis=1)
    return (grad_inputs, (grad_attn, grad_w_up, grad_w_down, grad_vectors))


def adam_update(master, gradient, moment_one, moment_two, decay_rate, step_rate):
    new_one = BETA_ONE * moment_one + (1.0 - BETA_ONE) * gradient
    new_two = BETA_TWO * moment_two + (1.0 - BETA_TWO) * gradient * gradient
    ratio = (
        new_one / (1.0 - BETA_ONE**STEP) / (jnp.sqrt(new_two / (1.0 - BETA_TWO**STEP)) + ADAM_EPS)
    )
    return (master - step_rate * (ratio + decay_rate * master), new_one, new_two)


def shards_by_kernels(devices, sections, tokens, cotangent, crop_ids, *states):
    boundary, input_grads, attn, upward_w, downward_w, vectors, norm = run_layers(
        devices, sections, tokens, cotangent, crop_ids, *states[:4]
    )
    updated = run_adam(norm, (attn, upward_w, downward_w, vectors), states)
    return (boundary[None], input_grads[None], norm[0, 0]) + tuple(updated)


def shards_by_collectives(devices, sections, tokens, cotangent, crop_ids, *states):
    section_index = lax.axis_index("section")
    flat = (-1, tokens.shape[2])
    masters, firsts, seconds = states[:4], states[4:8], states[8:]
    shards = [master[0].astype(BF16) for master in masters]
    weights = tuple(
        lax.all_gather(shard, "dp", axis=axis, tiled=True) for shard, axis in zip(shards, (0, 0, 0, 1))
    )
    own_tokens = tokens.reshape(flat)
    first_output, _ = forward_layer(own_tokens.astype(F32), crop_ids, weights)
    received = lax.ppermute(first_output.astype(BF16), "section", [(0, 1)])
    layer_input = jnp.where(section_index == 0, own_tokens, received)
    output, kept = forward_layer(layer_input.astype(F32), crop_ids, weights)
    boundary = output.astype(BF16).reshape(tokens.shape)
    own_grad = cotangent.reshape(flat)
    first_back, _ = backward_layer(kept, crop_ids, own_grad.astype(F32), weights, False)
    back_received = lax.ppermute(first_back.astype(BF16), "section", [(1, 0)])
    grad_out = jnp.where(section_index == 1, own_grad, back_received).astype(F32)
    grad_inputs, gradients = backward_layer(kept, crop_ids, grad_out, weights, True)
    input_grads = grad_inputs.astype(BF16).reshape(tokens.shape)
    reduced = tuple(
        lax.psum_scatter(gradient, "dp", scatter_dimension=axis, tiled=True)
        for gradient, axis in zip(gradients, (0, 0, 0, 1))
    )
    squares = sum(jnp.sum(member * member) for member in reduced)
    grad_norm = jnp.sqrt(lax.psum(squares, ("section", "dp")))
    clip_factor = jnp.minimum(1.0, MAX_NORM / (grad_norm + 1e-06))
    decays = (DECAY_RATE, DECAY_RATE, DECAY_RATE, 0.0)
    rates = (RATE, RATE, RATE, VECTOR_RATE)
    updated = [
        adam_update(master[0], gradient * clip_factor, one[0], two[0], decay_rate, step_rate)
        for master, gradient, one, two, decay_rate, step_rate in zip(
            masters, reduced, firsts, seconds, decays, rates
        )
    ]
    new_states = tuple(entry[part][None] for part in range(3) for entry in updated)
    return (boundary[None], input_grads[None], grad_norm) + new_states


def shards(devices, sections, tokens, cotangent, crop_ids, *states):
    whole_tiles = (
        devices % 8 == 0
        and all(state.shape[1] % 16 == 0 for state in states[:3])
        and states[2].shape[1] % 64 == 0
        and states[3].shape[1] <= 16
        and states[3].shape[2] <= 128
    )
    run = shards_by_kernels if whole_tiles else shards_by_collectives
    return run(devices, sections, tokens, cotangent, crop_ids, *states)


def solution(mesh):
    token_spec = P(None, "dp", None)
    row_spec = P("section", "dp", None)
    column_spec = P("section", None, "dp")
    state = (row_spec, row_spec, row_spec, column_spec)
    micro_spec = P("section", None, "dp", None)
    return jax.shard_map(
        partial(shards, mesh.shape["dp"], mesh.shape["section"]),
        mesh=mesh,
        in_specs=(token_spec, token_spec, P(None, "dp")) + 3 * state,
        out_specs=(micro_spec, micro_spec, P()) + 3 * state,
        check_vma=False,
    )
```

time: 529 us -> 269 us (0.51); the launches traced: 521 us -> 268 us
  matrix products: 145 us -> 0 us
  Pallas kernels: 163 us -> 258 us
  local copies, waits for them, and re-layouts: 94.3 us -> 9.26 us
  blocking collectives: 39.2 us -> 0 us
  other arithmetic: 36.3 us -> 0 us
  waiting for transfers between devices: 33 us -> 0 us
  between operations: 6.39 us -> 0.69 us
    dot_general x30 -> x0, matrix products: 145 us -> none  [the longest x2 27 us: forward_layer(): jnp.dot(active, downward_w, preferred_element_type=F32) + params[7]]
    pallas_call x2, Pallas kernels: 163 us -> 258 us  [the longest x1 251 us: run_layers(): pl.pallas_call(partial(layer_kernel, devices, sections), out_shape=[jax.S...]
    psum x1 -> x0, blocking collectives: 39.2 us -> none  [shards(): grad_norm = jnp.sqrt(lax.psum(squares, ('section', 'dp')))]
    reshape x12 -> x0, local copies, waits for them, and re-layouts: 36.8 us -> none  [the longest x2 14.7 us: split_heads(): shaped = packed.reshape(micro_count, -1, 3, HEADS, model_width // HEADS)]
    ppermute x2 -> x0, waiting for transfers between devices: 33 us -> none  [the longest x1 17.6 us: shards(): back_received = lax.ppermute(first_back.astype(BF16), 'section', [(1, 0)])]
    unnamed x147 -> x20, local copies, waits for them, and re-layouts: 24.6 us -> 8.07 us
    reduce_sum x17 -> x0, other arithmetic: 16.5 us -> none  [the longest x3 5.15 us: sum_squares(): running = running + jnp.sum(member * member)]
    convert_element_type x8 -> x0, other arithmetic: 12.4 us -> none  [the longest x3 4.78 us: gather_weights(): shards = (attn.astype(BF16), upward_w.astype(BF16), downward_w.astype(BF16))]
  transfers between devices with their start and end apart: 2 -> 0, of which waited for: 2 -> 0; matrix products, arithmetic and copies ran while one was open for 0% -> 0% of each run, Pallas kernels for 0% -> 0%
where the time goes in v2:
time: 269 us; the launch traced here: 268 us
  Pallas kernels  258 us (96%)
  local copies, waits for them, and re-layouts  9.26 us (3%)
    pallas_call x1, Pallas kernels, run_layers(): pl.pallas_call(partial(layer_kernel, devices, sections), out_shape=[jax.S...  251 us
    unnamed x20, local copies, waits for them, and re-layouts  8.07 us
    pallas_call x1, Pallas kernels, run_adam(): pl.pallas_call(adam_kernel, grid=(steps,), out_shape=[jax.ShapeDtypeStruc...  6.89 us

profile of v2, /device:TPU:0, one launch (start us, length us, event | category | flops | bytes accessed | tf_op | source)
XLA Modules:
  0.0 267.9 jit_solution(12148931025184185947)
XLA Ops:
  0.6 1.3 copy.30.own_vec.refs_7_
  1.9 251.1 %two_layers.1 = (bf16[2,224,768]{2,1,0:T(8,128)(2,1)}, bf16[2,224,768]{2,1,0:T(8,128)(2,1)}, f32[48,3072]{1,0:T(8,128)}, f32[48,3072]{1,0:T(8,128)}, f32[192,768...) custom-call(bf16[2,224,768]{2,1,0:T(8,128)(2,1)} %tokens.1, bf16[2,224,768]{2,1,0:T(8,128)(2,1)} %cotangent.1, ...), custom_call_target="tpu_custom_call" | custom-call | tf_op jit(solution)/shard_map/two_layers/pallas_call | solution.py:976
  253.1 0.0 copy-start.4
  253.1 0.7 copy-done.4
  253.8 0.0 copy-start.5
  253.8 0.6 copy.32.refs_11_
  254.4 0.1 copy-done.5
  254.5 0.6 copy.33.refs_15_
  255.0 0.0 copy-start.1
  255.0 6.9 %adam.1 = (f32[1,48,3072]{2,1,0:T(8,128)}, f32[1,48,3072]{2,1,0:T(8,128)}, f32[1,192,768]{2,1,0:T(8,128)}, f32[1,12,48]{2,1,0:T(8,128)}, f32[1,48,3072]{2,1,0:T(...) custom-call(f32[8,128]{1,0:T(8,128)} %get-tuple-element.36.norm, ...), custom_call_target="tpu_custom_call" | custom-call | tf_op jit(solution)/shard_map/adam/pallas_call | solution.py:1026
  261.9 0.0 copy-start.3
  262.0 1.3 copy.34
  263.3 0.0 copy-done.3
  263.3 0.0 copy-start.2
  263.3 0.6 copy.35
  263.9 0.1 copy-done.2
  264.0 0.6 copy.36
  264.6 1.2 slice.3
  265.7 0.0 copy-done.1
  265.8 0.0 copy-start
  265.8 0.8 copy.39
  266.6 0.5 copy-done
  267.1 0.8 copy.40
Async XLA Ops:
  253.1 0.7 copy-start.4
  253.8 0.7 copy-start.5
  255.0 10.7 %copy-start.1 = (bf16[2,224,768]{2,1,0:T(8,128)(2,1)S(1)}, bf16[2,224,768]{2,1,0:T(8,128)(2,1)}, u32[]{:S(2)}) copy-start(bf16[2,224,768]{2,1,0:T(8,128)(2,1)} %get-tuple-element.34) | copy-start | bytes 2064388
  261.9 1.3 copy-start.3
  263.3 0.7 copy-start.2
  265.8 1.3 copy-start

commit v3 on v2

--- a/solution.py
+++ b/solution.py
@@ -53,20 +53,6 @@
     def sibling(self):
         return self.target(self.device(self.place, 1 - self.core))
 
-    def greet(self):
-        barrier = pltpu.get_barrier_semaphore()
-        for device in (self.right(), self.left(), self.sibling()):
-            pl.semaphore_signal(barrier, inc=1, device_id=device, device_id_type=MESH)
-        pl.semaphore_wait(barrier, 3)
-
-
-def shard_view(ref, device, rows, part=None):
-    start = pl.multiple_of(device * rows, rows)
-    if part is None:
-        return ref.at[pl.ds(start, rows), :]
-    columns = ref.shape[1] // 2
-    return ref.at[pl.ds(start, rows), pl.ds(part * columns, columns)]
-
 
 def remote(source, target, send, receive, device):
     return pltpu.make_async_remote_copy(
@@ -79,14 +65,32 @@
     )
 
 
+class Shards:
+    def __init__(self, ring, whole, rows, stride=None, base=0, first=0, columns=None):
+        self.ring, self.whole, self.rows = ring, whole, rows
+        self.stride = rows if stride is None else stride
+        self.base, self.first = base, first
+        self.columns = whole.shape[1] if columns is None else columns
+
+    def row(self, distance, core):
+        device = self.ring.device(self.ring.place + distance, core)
+        return pl.multiple_of(device * self.stride + self.base, 16)
+
+    def view(self, distance, core, part=None):
+        rows = pl.ds(self.row(distance, core), self.rows)
+        if part is None:
+            return self.whole.at[rows, pl.ds(self.first, self.columns)]
+        columns = self.columns // 2
+        return self.whole.at[rows, pl.ds(self.first + part * columns, columns)]
+
+    def of_bytes(self, count):
+        return self.whole.at[pl.ds(0, count * self.rows), pl.ds(self.first, self.columns)]
+
+
 class Gather:
-    def __init__(self, ring, whole, rows, halves, send, receive):
-        self.ring, self.whole, self.rows, self.halves = ring, whole, rows, halves
-        self.send, self.receive = send, receive
-
-    def view(self, distance, core, part=None):
-        device = self.ring.device(self.ring.place + distance, core)
-        return shard_view(self.whole, device, self.rows, part)
+    def __init__(self, shards, halves, sent, shared, arrived):
+        self.ring, self.shards, self.halves = shards.ring, shards, halves
+        self.sent, self.shared, self.arrived = sent, shared, arrived
 
     def hop(self, way, step, came):
         ring = self.ring
@@ -97,9 +101,9 @@
                 part = way
             elif way == 1:
                 return None
-        view = self.view(-direction * (step if came else step - 1), ring.core, part)
+        view = self.shards.view(-direction * (step if came else step - 1), ring.core, part)
         device = ring.right() if way == 0 else ring.left()
-        return remote(view, view, self.send.at[way, step], self.receive.at[way, step], device)
+        return remote(view, view, self.sent, self.arrived.at[way, step - 1], device)
 
     def push(self, way, step):
         copy = self.hop(way, step, False)
@@ -111,91 +115,73 @@
         if copy is not None:
             copy.wait_recv()
 
-    def share(self, distance, key, core):
-        view = self.view(distance, core)
-        return remote(view, view, self.send.at[2, key], self.receive.at[2, key], self.ring.sibling())
-
-    def shares(self):
-        reach = self.ring.reach
-        keys = [(0, 0), (reach, reach)]
-        for step in range(1, reach):
-            keys += [(-step, step), (step, reach + step)]
-        return keys
+    def share(self, distance):
+        view = self.shards.view(distance, self.ring.core)
+        remote(view, view, self.sent, self.shared, self.ring.sibling()).start()
 
     def begin(self):
         self.push(0, 1)
         self.push(1, 1)
-        self.share(0, 0, self.ring.core).start()
+        self.share(0)
 
     def step(self, step):
-        reach, core = self.ring.reach, self.ring.core
+        reach = self.ring.reach
         self.arrive(0, step)
         if step < reach:
             self.push(0, step + 1)
         self.arrive(1, step)
         if step < reach:
             self.push(1, step + 1)
-            self.share(-step, step, core).start()
-            self.share(step, reach + step, core).start()
+            self.share(-step)
+            self.share(step)
         else:
-            self.share(reach, reach, core).start()
+            self.share(reach)
+
+    def bytes_of(self, count):
+        view = self.shards.of_bytes(count)
+        return remote(view, view, self.sent, self.shared, self.ring.sibling())
 
     def finish(self):
-        for distance, key in self.shares():
-            self.share(distance, key, 1 - self.ring.core).wait_recv()
+        self.bytes_of(self.ring.chips).wait_recv()
 
     def drain(self):
-        for distance, key in self.shares():
-            self.share(distance, key, self.ring.core).wait_send()
-        for step in range(1, self.ring.reach + 1):
-            for way in (0, 1):
-                copy = self.hop(way, step, False)
-                if copy is not None:
-                    copy.wait_send()
+        self.bytes_of(2 * self.ring.chips - 1).wait_send()
 
 
 class Reduce:
-    def __init__(self, ring, whole, base, put, other, slots, halves, block, send, receive):
-        self.ring, self.whole, self.base, self.put, self.other, self.slots = ring, whole, base, put, other, slots
-        self.rows, self.halves, self.block = other.shape[1], halves, block
-        self.send, self.receive = send, receive
-
-    def row(self, distance, core):
-        device = self.ring.device(self.ring.place + distance, core)
-        return pl.multiple_of(self.base + device * self.rows, 16)
-
-    def view(self, distance, core, part=None):
-        rows = pl.ds(self.row(distance, core), self.rows)
-        if part is None:
-            return self.whole.at[rows, :]
-        columns = self.whole.shape[1] // 2
-        return self.whole.at[rows, pl.ds(part * columns, columns)]
+    def __init__(self, shards, put, other, slots, halves, block, sent, swapped, arrived):
+        self.ring, self.shards, self.put = shards.ring, shards, put
+        self.other, self.slots, self.halves, self.block = other, slots, halves, block
+        self.sent, self.swapped, self.arrived = sent, swapped, arrived
 
     def keys(self):
         reach = self.ring.reach
-        order = [(reach, reach)]
+        order = [(reach, 0)]
         for distance in range(reach - 1, 0, -1):
-            order += [(distance, reach + distance), (-distance, distance)]
-        return order + [(0, 0)]
-
-    def swap(self, distance, key):
-        return remote(
-            self.view(distance, 1 - self.ring.core),
+            order += [(distance, 2 * (reach - distance) - 1), (-distance, 2 * (reach - distance))]
+        return order + [(0, 2 * reach - 1)]
+
+    def key(self, distance):
+        return dict(self.keys())[distance]
+
+    def swap(self, distance):
+        key = self.key(distance)
+        remote(
+            self.shards.view(distance, 1 - self.ring.core),
             self.other.at[key],
-            self.send.at[2, key],
-            self.receive.at[2, key],
+            self.sent,
+            self.swapped.at[min(key, 1)],
             self.ring.sibling(),
-        )
+        ).start()
 
     def exchange(self):
-        for distance, key in self.keys():
-            self.swap(distance, key).start()
-
-    def exchanged(self, key):
-        slot = self.other.at[key]
-        remote(
-            slot, slot, self.send.at[2, key], self.receive.at[2, key], self.ring.sibling()
-        ).wait_recv()
+        for distance, _ in self.keys():
+            self.swap(distance)
+
+    def exchanged(self, first):
+        slots = self.other.at[pl.ds(0, 1)] if first else self.other.at[pl.ds(1, self.ring.chips - 1)]
+        semaphore = self.swapped.at[0 if first else 1]
+        remote(slots, slots, self.sent, semaphore, self.ring.sibling()).wait_recv()
 
     def slot(self, way, distance):
         ref = self.slots.at[way, distance - 1]
@@ -212,11 +198,9 @@
         source = slot
         if not came:
             part = way if distance == ring.reach and self.halves else None
-            source = self.view(distance if way == 0 else -distance, ring.core, part)
+            source = self.shards.view(distance if way == 0 else -distance, ring.core, part)
         device = ring.right() if way == 0 else ring.left()
-        return remote(
-            source, slot, self.send.at[way, distance], self.receive.at[way, distance], device
-        )
+        return remote(source, slot, self.sent, self.arrived.at[way, distance - 1], device)
 
     def push(self, way, distance):
         copy = self.hop(way, distance, False)
@@ -228,16 +212,18 @@
         if copy is not None:
             copy.wait_recv()
 
-    def add(self, distance, key, arrivals, final=False):
-        ring = self.ring
-        base = self.row(distance, ring.core)
+    def add(self, distance, arrivals, final=False):
+        ring, shards = self.ring, self.shards
+        key = self.key(distance)
+        base = shards.row(distance, ring.core)
         block = self.block
-        half = self.whole.shape[1] // 2
+        half = shards.columns // 2
+        columns = pl.ds(shards.first, shards.columns)
 
         def body(index, _):
             here = pl.ds(pl.multiple_of(base + index * block, 16), block)
             rows = pl.ds(pl.multiple_of(index * block, block), block)
-            total = self.whole[here, :].astype(F32) + self.other[key, rows, :].astype(F32)
+            total = shards.whole[here, columns].astype(F32) + self.other[key, rows, :].astype(F32)
             for way, far in arrivals:
                 if far == ring.reach and self.halves:
                     low, high = total[:, :half], total[:, half:]
@@ -251,43 +237,36 @@
             if final:
                 self.put(rows, total)
             else:
-                self.whole[here, :] = total.astype(self.whole.dtype)
+                shards.whole[here, columns] = total.astype(shards.whole.dtype)
             return 0
 
-        lax.fori_loop(0, self.rows // block, body, 0)
+        lax.fori_loop(0, shards.rows // block, body, 0)
 
     def first(self):
         reach = self.ring.reach
-        self.exchanged(reach)
-        self.add(reach, reach, [])
+        self.exchanged(True)
+        self.add(reach, [])
         self.push(0, reach)
         self.push(1, reach)
 
     def step(self, distance):
-        reach = self.ring.reach
-        self.exchanged(reach + distance)
+        if distance == self.ring.reach - 1:
+            self.exchanged(False)
         self.arrive(0, distance + 1)
-        self.add(distance, reach + distance, [(0, distance + 1)])
+        self.add(distance, [(0, distance + 1)])
         self.push(0, distance)
-        self.exchanged(distance)
         self.arrive(1, distance + 1)
-        self.add(-distance, distance, [(1, distance + 1)])
+        self.add(-distance, [(1, distance + 1)])
         self.push(1, distance)
 
     def last(self):
-        self.exchanged(0)
         self.arrive(0, 1)
         self.arrive(1, 1)
-        self.add(0, 0, [(0, 1), (1, 1)], True)
+        self.add(0, [(0, 1), (1, 1)], True)
 
     def drain(self):
-        for distance, key in self.keys():
-            self.swap(distance, key).wait_send()
-        for distance in range(1, self.ring.reach + 1):
-            for way in (0, 1):
-                copy = self.hop(way, distance, False)
-                if copy is not None:
-                    copy.wait_send()
+        view = self.shards.of_bytes(2 * self.ring.chips - 1)
+        remote(view, view, self.sent, self.swapped.at[0], self.ring.sibling()).wait_send()
 
 
 def dot_nn(a, b):
@@ -302,29 +281,14 @@
     return lax.dot_general(a, b, (((0,), (0,)), ((), ())), preferred_element_type=F32)
 
 
-def erf(value):
-    bound = 3.832506856900711
-    value = jnp.clip(value, -bound, bound)
-    square = value * value
-    top = 0.00022905065861350646
-    for factor in (
-        0.0034082910107109506,
-        0.050955695062380861,
-        0.18520832239976145,
-        1.128379143519084,
-    ):
-        top = top * square + factor
-    bottom = -1.1791602954361697e-7
-    for factor in (
-        0.000023547966471313185,
-        0.0010179625278914885,
-        0.014070470171167667,
-        0.11098505178285362,
-        0.49746925110067538,
-        1.0,
-    ):
-        bottom = bottom * square + factor
-    return value * top / bottom
+def gelu_parts(value):
+    bell = jnp.exp(-0.5 * value * value)
+    t = 1.0 / (1.0 + (0.3275911 * 0.7071067811865476) * jnp.abs(value))
+    tail = 0.5 * 1.061405429
+    for factor in (-1.453152027, 1.421413741, -0.284496736, 0.254829592):
+        tail = tail * t + 0.5 * factor
+    tail = tail * t * bell
+    return jnp.where(value >= 0.0, 1.0 - tail, tail), bell * 0.3989422804014327
 
 
 def norm_parts(features):
@@ -351,20 +315,23 @@
     sections,
     tokens,
     cotangent,
-    crops,
+    crops_in,
     own_attn,
     own_up,
     own_down,
-    own_vec,
-    boundary,
-    input_grads,
+    own_vec_in,
+    boundary_out,
+    input_grads_out,
     sum_attn,
     sum_up,
     sum_down,
     sum_vec,
     norm,
-    w_qkv,
-    w_out,
+    crops,
+    own_vec,
+    boundary,
+    input_grads,
+    w_attn,
     w_up,
     w_down,
     tiles,
@@ -399,8 +366,10 @@
     slots_vec,
     norm_slots,
     local,
-    send,
-    receive,
+    gather_sems,
+    gather_ways,
+    reduce_sems,
+    reduce_ways,
     across,
     norm_sem,
 ):
@@ -415,9 +384,10 @@
     tiles_up = hidden_units // width
     head_width = width // HEADS
     pairs = HEADS // 2
+    unroll = 3
     pair_width = 2 * head_width
     head_scale = head_width ** (-0.5)
-    vec_rows, vec_columns = own_vec.shape[1], own_vec.shape[2]
+    vec_rows, vec_columns = own_vec.shape[0], own_vec.shape[2]
 
     def rows_of(micro):
         return pl.ds(pl.multiple_of(micro * pack, 16), pack)
@@ -433,16 +403,18 @@
         pltpu.make_async_copy(own_attn.at[0], stage_attn, local.at[0]),
         pltpu.make_async_copy(own_up.at[0], stage_up, local.at[1]),
         pltpu.make_async_copy(own_down.at[0], stage_down, local.at[2]),
+        pltpu.make_async_copy(own_vec_in, own_vec, local.at[3]),
+        pltpu.make_async_copy(crops_in, crops, local.at[4]),
     ]
     for load in loads:
         load.start()
 
     def load_tokens(micro):
-        return pltpu.make_async_copy(tokens.at[micro], x_in.at[rows_of(micro), :], local.at[3 + micro])
+        return pltpu.make_async_copy(tokens.at[micro], x_in.at[rows_of(micro), :], local.at[5 + micro])
 
     def load_cotangent(micro):
         return pltpu.make_async_copy(
-            cotangent.at[micro], dy_in.at[rows_of(micro), :], local.at[3 + micro]
+            cotangent.at[micro], dy_in.at[rows_of(micro), :], local.at[5 + micro]
         )
 
     @pl.when(first_section)
@@ -455,70 +427,74 @@
         for micro in range(micro_count):
             load_cotangent(micro).start()
 
-    total_devices = sections * devices
-    flat = section * devices + me
-
-    def other_device(distance):
-        other = (flat + distance) % total_devices
-        return (other // devices, other % devices)
-
     barrier = pltpu.get_barrier_semaphore()
-
-    def greet(distance, _):
-        pl.semaphore_signal(
-            barrier, inc=1, device_id=other_device(distance), device_id_type=MESH
-        )
-        return 0
-
-    lax.fori_loop(1, total_devices, greet, 0)
+    neighbours = (ring.right(), ring.left(), ring.sibling(), (1 - section, me))
+    for device in neighbours:
+        pl.semaphore_signal(barrier, inc=1, device_id=device, device_id_type=MESH)
 
     vec_tiles[...] = jnp.zeros_like(vec_tiles)
-    vec_tiles[0:vec_rows, 0:vec_columns] = own_vec[0]
-    tiles[pl.ds(pl.multiple_of(me * 16, 16), 16), :] = vec_tiles[0:16, :].astype(BF16)
     vec_sums[...] = jnp.zeros_like(vec_sums)
-    log_total[...] = jnp.zeros_like(log_total)
     for load in loads:
         load.wait()
+    vec_tiles[0:vec_rows, 0:vec_columns] = own_vec[:, 0, :]
+    tiles[pl.ds(pl.multiple_of(me * 16, 16), 16), :] = vec_tiles[0:16, :].astype(BF16)
     count = own_attn.shape[1]
     here = pl.ds(pl.multiple_of(me * count, 16), count)
-    w_qkv[here, :] = stage_attn[:, : 3 * width].astype(BF16)
-    w_out[here, :] = stage_attn[:, 3 * width :].astype(BF16)
+    w_attn[here, :] = stage_attn[...].astype(BF16)
     count = own_up.shape[1]
     w_up[pl.ds(pl.multiple_of(me * count, 16), count), :] = stage_up[...].astype(BF16)
     count = own_down.shape[1]
     w_down[pl.ds(pl.multiple_of(me * count, 16), count), :] = stage_down[...].astype(BF16)
 
-    pl.semaphore_wait(barrier, total_devices - 1)
-
-
-    def gather_of(index, whole, rows, halves=True):
-        return Gather(ring, whole, rows, halves, send.at[index], receive.at[index])
-
-    get_vec = gather_of(0, tiles, 16, False)
-    get_qkv = gather_of(1, w_qkv, own_attn.shape[1])
-    get_out = gather_of(2, w_out, own_attn.shape[1])
-    get_up = gather_of(3, w_up, own_up.shape[1])
-    get_down = gather_of(4, w_down, own_down.shape[1])
+    pl.semaphore_wait(barrier, len(neighbours))
+
+
+    def gather_of(index, shards, halves=True):
+        return Gather(
+            shards,
+            halves,
+            gather_sems.at[index, 0],
+            gather_sems.at[index, 1],
+            gather_ways.at[index],
+        )
+
+    down_rows = own_down.shape[1]
+    get_vec = gather_of(0, Shards(ring, tiles, 16), False)
+    get_attn = gather_of(1, Shards(ring, w_attn, own_attn.shape[1]))
+    get_up = gather_of(2, Shards(ring, w_up, own_up.shape[1]))
+    get_down = [
+        gather_of(3 + part, Shards(ring, w_down, down_rows // 2, down_rows, part * down_rows // 2))
+        for part in range(2)
+    ]
+
+    def down_step(step):
+        for gather in get_down:
+            gather.step(step)
+
+    def down_finish():
+        for gather in get_down:
+            gather.finish()
 
     reach = ring.reach
-    for gather in (get_vec, get_qkv, get_out):
-        gather.begin()
+    get_vec.begin()
+    get_attn.begin()
     for step in range(1, reach + 1):
-        for gather in (get_vec, get_qkv, get_out):
-            gather.step(step)
+        get_vec.step(step)
+        get_attn.step(step)
         if step == reach // 2:
             get_up.begin()
     get_up.step(1)
-    get_down.begin()
-    for gather in (get_vec, get_qkv, get_out):
-        gather.finish()
+    for gather in get_down:
+        gather.begin()
+    get_vec.finish()
+    get_attn.finish()
 
     late = []
     for step in range(2, reach + 1):
         late.append(partial(get_up.step, step))
-        late.append(partial(get_down.step, step - 1))
+        late.append(partial(down_step, step - 1))
     late.append(get_up.finish)
-    late_down = [partial(get_down.step, reach), get_down.finish]
+    late_down = [partial(down_step, reach), down_finish]
 
     @pl.when(last_section)
     def _():
@@ -548,7 +524,7 @@
         z, _ = norm_parts(inputs)
         hidden[here, :] = (z * params[0:1, :] + params[1:2, :]).astype(BF16)
         for part in range(3):
-            value = dot_nn(hidden[here, :], w_qkv[:, part * width : (part + 1) * width])
+            value = dot_nn(hidden[here, :], w_attn[:, part * width : (part + 1) * width])
             if part == 0:
                 value = value + params[2:3, :]
             if part == 2:
@@ -561,26 +537,23 @@
             queries = qkv[here, lanes(at, pair_width)]
             keys = qkv[here, lanes(width + at, pair_width)]
             values = qkv[here, lanes(2 * width + at, pair_width)]
+            scores = [dot_nt(keys, of_head(queries, sub)) for sub in range(2)]
             outs = []
-            logs = log_total[here, :]
-            head_lane = lax.broadcasted_iota(jnp.int32, (1, 128), 1)
             for sub in range(2):
-                scores = dot_nt(of_head(queries, sub), keys) * head_scale
-                scores = jnp.where(mask[micro] > 0.5, scores, NEG_BIG)
-                peak = jnp.max(scores, axis=-1, keepdims=True)
-                exponent = jnp.exp(scores - peak)
-                totals = jnp.sum(exponent, axis=-1, keepdims=True)
+                value = jnp.where(mask[micro] > 0.5, scores[sub] * head_scale, NEG_BIG)
+                peak = jnp.max(value, axis=0, keepdims=True)
+                exponent = jnp.exp(value - peak)
+                totals = jnp.sum(exponent, axis=0, keepdims=True)
                 probs = (exponent * (1.0 / totals)).astype(BF16)
-                logs = jnp.where(head_lane == 2 * index + sub, peak + jnp.log(totals), logs)
-                outs.append(dot_nn(probs, values))
-            log_total[here, :] = logs
+                log_total[pl.ds(micro * HEADS + 2 * index + sub, 1), :] = peak + jnp.log(totals)
+                outs.append(dot_tn(probs, values))
             mixed[here, lanes(at, pair_width)] = jnp.where(in_low, outs[0], outs[1]).astype(BF16)
             return 0
 
-        lax.fori_loop(0, pairs, pair, 0)
+        lax.fori_loop(0, pairs, pair, 0, unroll=unroll)
         serve(1)
         middle_value = x_in[here, :].astype(F32) + (
-            dot_nn(mixed[here, :], w_out[...]) + params[4:5, :]
+            dot_nn(mixed[here, :], w_attn[:, 3 * width :]) + params[4:5, :]
         )
         middle[here, :] = middle_value
         z, _ = norm_parts(middle_value)
@@ -589,11 +562,9 @@
         for part in range(tiles_up):
             columns = slice(part * width, (part + 1) * width)
             upward = dot_nn(hidden_two[here, :], w_up[:, columns]) + params[8 + part : 9 + part, :]
-            half = 0.5 + 0.5 * erf(upward * 0.7071067811865476)
-            active[here, columns] = (upward * half).astype(BF16)
-            slope[here, columns] = half + upward * (
-                jnp.exp(-0.5 * upward * upward) * 0.3989422804014327
-            )
+            area, density = gelu_parts(upward)
+            active[here, columns] = (upward * area).astype(BF16)
+            slope[here, columns] = area + upward * density
         serve(3)
 
     def hand_over(source, target, micro):
@@ -644,8 +615,9 @@
         return 0
 
     lax.fori_loop(0, micro_count, finish_step, 0)
-    for gather in (get_vec, get_qkv, get_out, get_up, get_down):
+    for gather in (get_vec, get_attn, get_up, *get_down):
         gather.drain()
+    pltpu.make_async_copy(boundary, boundary_out, local.at[0]).start()
 
 
     def into(ref, first):
@@ -654,38 +626,56 @@
 
         return put
 
-    def reduce_of(index, whole, base, put, other, slots, halves=True, block=16):
+    def reduce_of(index, shards, put, other, slots, halves=True, block=16):
         return Reduce(
-            ring, whole, base, put, other, slots, halves, block, send.at[index], receive.at[index]
+            shards,
+            put,
+            other,
+            slots,
+            halves,
+            block,
+            reduce_sems.at[index, 0],
+            reduce_sems.at[index, pl.ds(1, 2)],
+            reduce_ways.at[index],
         )
 
-    put_down = reduce_of(5, g_down, 0, into(sum_down, 0), other_down, slots_down, block=64)
-    put_up = reduce_of(6, w_up, 0, into(sum_up, 0), other_up, slots_up)
+    put_down = reduce_of(
+        0, Shards(ring, g_down, down_rows), into(sum_down, 0), other_down, slots_down, block=64
+    )
+    put_up = reduce_of(
+        1, Shards(ring, w_up, own_up.shape[1]), into(sum_up, 0), other_up, slots_up
+    )
+    half_attn = w_attn.shape[1] // 2
     put_attn = [
         reduce_of(
-            7 + part,
-            w_down,
-            part * width,
-            into(sum_attn, part * width),
+            2 + part,
+            Shards(ring, w_attn, own_attn.shape[1], first=part * half_attn, columns=half_attn),
+            into(sum_attn, part * half_attn),
             other_attn.at[part],
             slots_attn.at[part],
-            block=other_attn.shape[2],
         )
-        for part in range(4)
+        for part in range(2)
     ]
-    put_vec = reduce_of(11, vec_tiles, 0, into(sum_vec, 0), other_vec, slots_vec, False)
-
-    def weigh_down():
-        chunk = 2 * own_down.shape[1]
-
-        def body(index, _):
-            columns = lanes(index * chunk, chunk)
-            g_down[pl.ds(pl.multiple_of(index * chunk, 16), chunk), :] = dot_tn(
-                active[:, columns], dy_in[...]
-            ).astype(BF16)
-            return 0
-
-        lax.fori_loop(0, hidden_units // chunk, body, 0)
+    put_vec = reduce_of(
+        4, Shards(ring, vec_tiles, 16), into(sum_vec, 0), other_vec, slots_vec, False
+    )
+
+    chunk = 2 * down_rows
+
+    def weigh_down(distance):
+        start = ring.device(ring.place + distance, 0) * down_rows
+        columns = lanes(start, chunk)
+        g_down[pl.ds(pl.multiple_of(start, 16), chunk), :] = dot_tn(
+            active[:, columns], dy_in[...]
+        ).astype(BF16)
+        put_down.swap(distance)
+
+    def start_down():
+        for index, (distance, _) in enumerate(put_down.keys()):
+            weigh_down(distance)
+            if index == 1:
+                put_down.first()
+        put_down.step(reach - 1)
 
     def add_vec(row, value):
         vec_sums[row : row + 1, :] += value
@@ -714,7 +704,7 @@
         back = back.astype(BF16)
         grad_branch[here, :] = back
         add_vec(4, column_sum(back.astype(F32)))
-        grad_heads[...] = dot_nt(back, w_out[...]).astype(BF16)
+        grad_heads[...] = dot_nt(back, w_attn[:, 3 * width :]).astype(BF16)
         serve(1)
 
         def pair(index, _):
@@ -723,25 +713,21 @@
             keys = qkv[here, lanes(width + at, pair_width)]
             values = qkv[here, lanes(2 * width + at, pair_width)]
             back_out = grad_heads[:, lanes(at, pair_width)]
-            head_lane = lax.broadcasted_iota(jnp.int32, (1, 128), 1)
+            scores = [dot_nt(keys, of_head(queries, sub)) for sub in range(2)]
+            back_probs = [dot_nt(values, of_head(back_out, sub)) for sub in range(2)]
             results = []
             for sub in range(2):
-                scores = dot_nt(of_head(queries, sub), keys) * head_scale
-                scores = jnp.where(mask[micro] > 0.5, scores, NEG_BIG)
-                logs = jnp.sum(
-                    jnp.where(head_lane == 2 * index + sub, log_total[here, :], 0.0),
-                    axis=-1,
-                    keepdims=True,
+                value = jnp.where(mask[micro] > 0.5, scores[sub] * head_scale, NEG_BIG)
+                probs = jnp.exp(
+                    value - log_total[pl.ds(micro * HEADS + 2 * index + sub, 1), :]
                 )
-                probs = jnp.exp(scores - logs)
-                back_probs = dot_nt(of_head(back_out, sub), values)
-                inner = jnp.sum(back_probs * probs, axis=-1, keepdims=True)
-                back_scores = (probs * (back_probs - inner)).astype(BF16)
+                inner = jnp.sum(back_probs[sub] * probs, axis=0, keepdims=True)
+                back_scores = (probs * (back_probs[sub] - inner)).astype(BF16)
                 results.append(
                     (
-                        dot_nn(back_scores, keys) * head_scale,
-                        dot_tn(back_scores, queries) * head_scale,
-                        dot_tn(probs.astype(BF16), back_out),
+                        dot_tn(back_scores, keys) * head_scale,
+                        dot_nn(back_scores, queries) * head_scale,
+                        dot_nn(probs.astype(BF16), back_out),
                     )
                 )
             for part in range(3):
@@ -750,9 +736,9 @@
                 ).astype(BF16)
             return 0
 
-        lax.fori_loop(0, pairs, pair, 0)
+        lax.fori_loop(0, pairs, pair, 0, unroll=unroll)
         serve(2)
-        e = dot_nt(grad_qkv[here, :], w_qkv[...])
+        e = dot_nt(grad_qkv[here, :], w_attn[:, : 3 * width])
         z, scale = norm_parts(x_in[here, :].astype(F32))
         add_vec(0, column_sum(e * z))
         add_vec(1, column_sum(e))
@@ -776,16 +762,15 @@
         def serve(point):
             @pl.when(first_section & is_last)
             def _():
-                if point == 0:
-                    put_down.step(reach - 1)
-                if point == 2:
+                if point == 1:
                     put_down.step(reach - 2)
+                if point == 3:
+                    for distance in range(reach - 3, 0, -1):
+                        put_down.step(distance)
 
         @pl.when(first_section & is_last)
         def _():
-            weigh_down()
-            put_down.exchange()
-            put_down.first()
+            start_down()
 
         backward_micro(micro, serve)
 
@@ -797,71 +782,69 @@
 
     lax.fori_loop(0, micro_count, backward_step, 0)
 
+    copy_input_grads = pltpu.make_async_copy(input_grads, input_grads_out, local.at[1])
+    copy_input_grads.start()
+
     @pl.when(last_section)
     def _():
-        weigh_down()
-        put_down.exchange()
-        put_down.first()
+        start_down()
 
     third = width // 3
 
-    def weigh(source, grad, columns, target, base):
+    def weigh(source, grad, target, first):
         def body(index, _):
-            rows = lanes(index * third, third)
-            target[pl.ds(pl.multiple_of(base + index * third, 16), third), :] = dot_tn(
-                source[:, rows], grad[:, columns]
-            ).astype(BF16)
+            target[
+                pl.ds(pl.multiple_of(index * third, 16), third),
+                pl.ds(first, grad.shape[1]),
+            ] = dot_tn(source[:, lanes(index * third, third)], grad[...]).astype(BF16)
             return 0
 
         lax.fori_loop(0, 3, body, 0)
 
-    weigh(hidden_two, grad_up, slice(0, hidden_units), w_up, 0)
+    weigh(hidden_two, grad_up, w_up, 0)
     put_up.exchange()
 
     @pl.when(last_section)
     def _():
-        put_down.step(reach - 1)
+        put_down.step(reach - 2)
 
     put_up.first()
-    for part in range(3):
-        weigh(hidden, grad_qkv, slice(part * width, (part + 1) * width), w_down, part * width)
-        put_attn[part].exchange()
-    weigh(mixed, grad_branch, slice(0, width), w_down, 3 * width)
-    put_attn[3].exchange()
-
     vec_tiles[...] = jnp.zeros_like(vec_tiles)
     for device in range(devices):
         vec_tiles[device * 16 : (device + 1) * 16, 0:vec_columns] = vec_sums[
             :, device * vec_columns : (device + 1) * vec_columns
         ]
     put_vec.exchange()
+    weigh(hidden, grad_qkv, w_attn, 0)
+    put_attn[0].exchange()
+    weigh(mixed, grad_branch, w_attn, 3 * width)
+    put_attn[1].exchange()
 
     @pl.when(last_section)
     def _():
-        put_down.step(reach - 2)
-
+        for distance in range(reach - 3, 0, -1):
+            put_down.step(distance)
+
+    put_vec.first()
     put_up.step(reach - 1)
-    put_vec.first()
-    for part in range(4):
+    put_down.last()
+    for part in range(2):
         put_attn[part].first()
-    for distance in range(reach - 3, 0, -1):
-        put_down.step(distance)
     put_up.step(reach - 2)
-    for part in range(4):
+    put_vec.step(reach - 1)
+    for part in range(2):
         put_attn[part].step(reach - 1)
-    put_vec.step(reach - 1)
-    put_down.last()
-    for distance in range(reach - 3, 0, -1):
-        put_up.step(distance)
     for distance in range(reach - 2, 0, -1):
-        for part in range(4):
+        if distance > 1:
+            put_up.step(distance - 1)
+        else:
+            put_up.last()
+        put_vec.step(distance)
+        for part in range(2):
             put_attn[part].step(distance)
-        put_vec.step(distance)
-        if distance == reach - 2:
-            put_up.last()
-    for part in range(4):
+    put_vec.last()
+    for part in range(2):
         put_attn[part].last()
-    put_vec.last()
 
 
     def squares(ref):
@@ -872,6 +855,13 @@
                 value[:, start : start + 128] for start in range(0, value.shape[1], 128)
             )
         return sum(value[start : start + 8, :] for start in range(0, value.shape[0], 8))
+
+    total_devices = sections * devices
+    flat = section * devices + me
+
+    def other_device(distance):
+        other = (flat + distance) % total_devices
+        return (other // devices, other % devices)
 
     norm_slots[0] = squares(sum_attn) + squares(sum_up) + squares(sum_down) + squares(sum_vec)
 
@@ -889,22 +879,20 @@
     rest = norm_slots.at[pl.ds(1, total_devices - 1)]
     heard = remote(rest, rest, norm_sem.at[0], norm_sem.at[1], other_device(1))
     heard.wait_recv()
-    order = jnp.zeros(norm_slots.shape[1:], F32)
-
-    def gather_up(device, order):
+
+    def collect(device, order):
         return order + norm_slots[(flat - device + total_devices) % total_devices]
 
-    order = lax.fori_loop(0, total_devices, gather_up, order)
+    order = lax.fori_loop(0, total_devices, collect, jnp.zeros(norm_slots.shape[1:], F32))
     total = jnp.sum(jnp.sum(order, axis=0, keepdims=True), axis=1, keepdims=True)
-    norm[...] = jnp.broadcast_to(jnp.sqrt(total), norm.shape)
+    norm[0, 0] = jnp.sqrt(total)[0, 0]
     heard.wait_send()
 
 
-    put_down.drain()
-    put_up.drain()
-    for part in range(4):
-        put_attn[part].drain()
-    put_vec.drain()
+    for reduce in (put_down, put_up, *put_attn, put_vec):
+        reduce.drain()
+    pltpu.make_async_copy(boundary, boundary_out, local.at[0]).wait()
+    copy_input_grads.wait()
     for micro in range(micro_count):
 
         @pl.when(first_section)
@@ -932,8 +920,11 @@
         return pltpu.VMEM((2, reach, rows_of_shard, columns), kind)
 
     scratch = [
-        pltpu.VMEM((width, 3 * width), BF16),
-        pltpu.VMEM((width, width), BF16),
+        pltpu.VMEM(crop_ids.shape, jnp.int32),
+        pltpu.VMEM(vectors.shape, F32),
+        pltpu.VMEM(tokens.shape, BF16),
+        pltpu.VMEM(tokens.shape, BF16),
+        pltpu.VMEM((width, attn.shape[2]), BF16),
         pltpu.VMEM((width, hidden_units), BF16),
         pltpu.VMEM((hidden_units, width), BF16),
         pltpu.VMEM((devices * 16, 128), BF16),
@@ -941,7 +932,7 @@
         pltpu.VMEM((rows, width), BF16),
         pltpu.VMEM((rows, width), BF16),
         pltpu.VMEM((rows, 3 * width), BF16),
-        pltpu.VMEM((rows, 128), F32),
+        pltpu.VMEM((micro_count * HEADS, pack), F32),
         pltpu.VMEM((rows, width), BF16),
         pltpu.VMEM((rows, width), F32),
         pltpu.VMEM((rows, width), BF16),
@@ -960,16 +951,18 @@
         pltpu.VMEM((hidden_units, width), BF16),
         other(down_rows, width),
         other(up_rows, hidden_units),
-        pltpu.VMEM((4, chips, attn_rows, width), BF16),
+        pltpu.VMEM((2, chips, attn_rows, attn.shape[2] // 2), BF16),
         other(16, 128, F32),
         slots(down_rows, width),
         slots(up_rows, hidden_units),
-        pltpu.VMEM((4, 2, reach, attn_rows, width), BF16),
+        pltpu.VMEM((2, 2, reach, attn_rows, attn.shape[2] // 2), BF16),
         slots(16, 128, F32),
         pltpu.VMEM((sections * devices, 8, 128), F32),
-        pltpu.SemaphoreType.DMA((3 + micro_count,)),
-        pltpu.SemaphoreType.DMA((12, 3, 2 * reach)),
-        pltpu.SemaphoreType.DMA((12, 3, 2 * reach)),
+        pltpu.SemaphoreType.DMA((5 + micro_count,)),
+        pltpu.SemaphoreType.DMA((5, 2)),
+        pltpu.SemaphoreType.DMA((5, 2, reach)),
+        pltpu.SemaphoreType.DMA((5, 3)),
+        pltpu.SemaphoreType.DMA((5, 2, reach)),
         pltpu.SemaphoreType.DMA((2, micro_count)),
         pltpu.SemaphoreType.DMA((2,)),
     ]
@@ -982,10 +975,10 @@
             jax.ShapeDtypeStruct(upward_w.shape[1:], F32),
             jax.ShapeDtypeStruct(downward_w.shape[1:], F32),
             jax.ShapeDtypeStruct((16, 128), F32),
-            jax.ShapeDtypeStruct((8, 128), F32),
+            jax.ShapeDtypeStruct((1, 1), F32),
         ],
-        in_specs=[in_hbm, in_hbm, in_vmem, in_hbm, in_hbm, in_hbm, in_vmem],
-        out_specs=[in_vmem] * 7,
+        in_specs=[in_hbm] * 7,
+        out_specs=[in_hbm] * 2 + [in_vmem] * 4 + [pl.BlockSpec(memory_space=pltpu.SMEM)],
         scratch_shapes=scratch,
         compiler_params=pltpu.CompilerParams(
             collective_id=0, has_side_effects=True, vmem_limit_bytes=VMEM_LIMIT
@@ -994,21 +987,55 @@
     )(tokens, cotangent, crop_ids, attn, upward_w, downward_w, vectors)
 
 
-def adam_kernel(norm, *refs):
-    grads, states, results = refs[:4], refs[4:16], refs[16:28]
-    clip_factor = jnp.minimum(1.0, MAX_NORM / (norm[0:1, 0:1] + 1e-06))
+def adam_kernel(boundary, input_grads, norm, *refs):
+    grads, states, out_boundary, out_input, out_norm = refs[:4], refs[4:16], *refs[16:19]
+    results, held, passing = refs[19:31], refs[31], refs[32]
+    step = pl.program_id(0)
+    take = [
+        pltpu.make_async_copy(source, held.at[i], passing.at[i])
+        for i, source in enumerate((boundary, input_grads))
+    ]
+    hand_on = [
+        pltpu.make_async_copy(held.at[i], target, passing.at[i])
+        for i, target in enumerate((out_boundary, out_input))
+    ]
+
+    @pl.when(step == 0)
+    def _():
+        for copy in take:
+            copy.start()
+        out_norm[0, 0] = norm[0, 0]
+
+    @pl.when(step == 1)
+    def _():
+        for first, second in zip(take, hand_on):
+            first.wait()
+            second.start()
+
+    clip_factor = jnp.minimum(1.0, MAX_NORM / (jnp.full((1, 1), norm[0, 0]) + 1e-06))
     for index in range(4):
         master, moment_one, moment_two = (states[index + 4 * part] for part in range(3))
-        shape = master.shape[1:]
+        vectors = index == 3
+        shape = (master.shape[0], master.shape[2]) if vectors else master.shape[1:]
         gradient = grads[index][0 : shape[0], 0 : shape[1]] * clip_factor
-        decay, rate = (0.0, VECTOR_RATE) if index == 3 else (DECAY_RATE, RATE)
-        updated = adam_update(master[0], gradient, moment_one[0], moment_two[0], decay, rate)
+        old = [ref[:, 0, :] if vectors else ref[0] for ref in (master, moment_one, moment_two)]
+        decay, rate = (0.0, VECTOR_RATE) if vectors else (DECAY_RATE, RATE)
+        updated = adam_update(old[0], gradient, old[1], old[2], decay, rate)
         for part in range(3):
-            results[index + 4 * part][0] = updated[part]
-
-
-def run_adam(norm, grads, states):
-    steps = 3
+            if vectors:
+                results[index + 4 * part][:, 0, :] = updated[part]
+            else:
+                results[index + 4 * part][0] = updated[part]
+
+    @pl.when(step == pl.num_programs(0) - 1)
+    def _():
+        for copy in hand_on:
+            copy.wait()
+
+
+def run_adam(boundary, input_grads, attn, upward_w, downward_w, vectors, norm, states):
+    grads = (attn, upward_w, downward_w, vectors)
+    steps = 2
 
     def cut(shape):
         block = shape[:-2] + (shape[-2] // steps, shape[-1])
@@ -1022,16 +1049,24 @@
     def spec(index, array):
         return keep(array.shape) if index % 4 == 3 else cut(array.shape)
 
+    in_hbm = pl.BlockSpec(memory_space=pl.ANY)
+    scalar = pl.BlockSpec(memory_space=pltpu.SMEM)
     state_specs = [spec(i, a) for i, a in enumerate(states)]
     return pl.pallas_call(
         adam_kernel,
         grid=(steps,),
-        out_shape=[jax.ShapeDtypeStruct(a.shape, F32) for a in states],
-        in_specs=[keep(norm.shape)] + [spec(i, a) for i, a in enumerate(grads)] + state_specs,
-        out_specs=state_specs,
+        out_shape=[
+            jax.ShapeDtypeStruct(boundary.shape, BF16),
+            jax.ShapeDtypeStruct(input_grads.shape, BF16),
+            jax.ShapeDtypeStruct((1, 1), F32),
+        ]
+        + [jax.ShapeDtypeStruct(a.shape, F32) for a in states],
+        in_specs=[in_hbm, in_hbm, scalar] + [spec(i, a) for i, a in enumerate(grads)] + state_specs,
+        out_specs=[in_hbm, in_hbm, scalar] + state_specs,
+        scratch_shapes=[pltpu.VMEM((2,) + boundary.shape, BF16), pltpu.SemaphoreType.DMA((2,))],
         compiler_params=pltpu.CompilerParams(vmem_limit_bytes=VMEM_LIMIT),
         name="adam",
-    )(norm, *grads, *states)
+    )(boundary, input_grads, norm, *grads, *states)
 
 
 def layer_norm(features, gain_row, shift_row):
@@ -1171,11 +1206,11 @@
 
 
 def shards_by_kernels(devices, sections, tokens, cotangent, crop_ids, *states):
-    boundary, input_grads, attn, upward_w, downward_w, vectors, norm = run_layers(
-        devices, sections, tokens, cotangent, crop_ids, *states[:4]
-    )
-    updated = run_adam(norm, (attn, upward_w, downward_w, vectors), states)
-    return (boundary[None], input_grads[None], norm[0, 0]) + tuple(updated)
+    states = [state.transpose(1, 0, 2) if i % 4 == 3 else state for i, state in enumerate(states)]
+    sums = run_layers(devices, sections, tokens, cotangent, crop_ids, *states[:4])
+    boundary, input_grads, grad_norm, *updated = run_adam(*sums, states)
+    updated = [state.transpose(1, 0, 2) if i % 4 == 3 else state for i, state in enumerate(updated)]
+    return (boundary[None], input_grads[None], grad_norm.reshape(())) + tuple(updated)
 
 
 def shards_by_collectives(devices, sections, tokens, cotangent, crop_ids, *states):

time: 269 us -> 234 us (0.87)
  Pallas kernels: 258 us -> 233 us
  local copies, waits for them, and re-layouts: 9.26 us -> 0 us
    pallas_call x1, Pallas kernels: 251 us -> 226 us  [run_layers(): pl.pallas_call(partial(layer_kernel, devices, sections), out_shape=[jax.S...]
    unnamed x20 -> x0, local copies, waits for them, and re-layouts: 8.07 us -> none
where the time goes in v3:
time: 234 us
  Pallas kernels  233 us (100%)
    pallas_call x1, Pallas kernels, run_layers(): pl.pallas_call(partial(layer_kernel, devices, sections), out_shape=[jax.S...  226 us
    pallas_call x1, Pallas kernels, run_adam(): pl.pallas_call(adam_kernel, grid=(steps,), out_shape=[jax.ShapeDtypeStruc...  6.84 us

profile of v3, /device:TPU:0, one launch (start us, length us, event | category | flops | bytes accessed | tf_op | source)
XLA Modules:
  0.0 234.0 jit_solution(4235046449742465844)
XLA Ops:
  0.6 226.3 %two_layers.1 = (bf16[2,224,768]{2,1,0:T(8,128)(2,1)}, bf16[2,224,768]{2,1,0:T(8,128)(2,1)}, f32[48,3072]{1,0:T(8,128)}, f32[48,3072]{1,0:T(8,128)}, f32[192,768...) custom-call(bf16[2,224,768]{2,1,0:T(8,128)(2,1)} %tokens.1, bf16[2,224,768]{2,1,0:T(8,128)(2,1)} %cotangent.1, ...), custom_call_target="tpu_custom_call" | custom-call | tf_op jit(solution)/shard_map/two_layers/pallas_call | solution.py:969
  227.0 6.8 %adam.1 = (bf16[2,224,768]{2,1,0:T(8,128)(2,1)}, bf16[2,224,768]{2,1,0:T(8,128)(2,1)}, f32[1,1]{1,0:T(1,128)}, f32[1,48,3072]{2,1,0:T(8,128)}, f32[1,48,3072]{2,...) custom-call(bf16[2,224,768]{2,1,0:T(8,128)(2,1)} %get-tuple-element., ...), custom_call_target="tpu_custom_call" | custom-call | tf_op jit(solution)/shard_map/adam/pallas_call | solution.py:1055

commit v4 on v3

--- a/solution.py
+++ b/solution.py
@@ -148,6 +148,59 @@
         self.bytes_of(2 * self.ring.chips - 1).wait_send()
 
 
+class Relay(Gather):
+    def __init__(self, shards, home, away, sent, arrived, crossed):
+        super().__init__(shards, True, sent, None, arrived)
+        self.home, self.away, self.crossed = home, away, crossed
+
+    def across(self, source, target, semaphore):
+        section = lax.axis_index("section")
+        return remote(source, target, self.sent, semaphore, (1 - section, self.ring.me))
+
+    def lend(self):
+        core = self.ring.core
+        for home, away in zip(self.home, self.away):
+            self.across(home.view(0, core), away.view(0, core), self.crossed.at[0]).start()
+
+    def borrow(self):
+        view = self.shards.view(0, self.ring.core)
+        self.across(view, view, self.crossed.at[0]).wait_recv()
+
+    def share(self, distance):
+        if distance == 0:
+            return
+        core = self.ring.core
+        for index, (home, away) in enumerate(zip(self.home, self.away)):
+            self.across(
+                away.view(distance, core), home.view(distance, core), self.crossed.at[1 + index]
+            ).start()
+
+    def take(self, index):
+        view = self.home[index].of_bytes(self.ring.chips - 1)
+        self.across(view, view, self.crossed.at[1 + index]).wait_recv()
+
+    def drain(self):
+        view = self.shards.of_bytes(2 * self.ring.chips - 2)
+        self.across(view, view, self.crossed.at[0]).wait_send()
+
+    def drain_lent(self):
+        view = self.shards.of_bytes(1)
+        self.across(view, view, self.crossed.at[0]).wait_send()
+
+
+class Pieces(Gather):
+    def __init__(self, shards, sent, shared):
+        super().__init__(shards, True, sent, shared, None)
+
+    def share_rest(self):
+        for distance in range(1 - self.ring.reach, self.ring.reach + 1):
+            if distance != 0:
+                self.share(distance)
+
+    def drain(self):
+        self.bytes_of(self.ring.chips).wait_send()
+
+
 class Reduce:
     def __init__(self, shards, put, other, slots, halves, block, sent, swapped, arrived):
         self.ring, self.shards, self.put = shards.ring, shards, put
@@ -235,7 +288,7 @@
                 elif far < ring.reach or way == 0:
                     total = total + self.slots[way, far - 1, rows, :].astype(F32)
             if final:
-                self.put(rows, total)
+                self.put(index * block, total)
             else:
                 shards.whole[here, columns] = total.astype(shards.whole.dtype)
             return 0
@@ -368,6 +421,7 @@
     local,
     gather_sems,
     gather_ways,
+    relay_sems,
     reduce_sems,
     reduce_ways,
     across,
@@ -458,48 +512,95 @@
             gather_ways.at[index],
         )
 
-    down_rows = own_down.shape[1]
+    attn_rows, up_rows, down_rows = own_attn.shape[1], own_up.shape[1], own_down.shape[1]
+    reach = ring.reach
     get_vec = gather_of(0, Shards(ring, tiles, 16), False)
-    get_attn = gather_of(1, Shards(ring, w_attn, own_attn.shape[1]))
-    get_up = gather_of(2, Shards(ring, w_up, own_up.shape[1]))
-    get_down = [
-        gather_of(3 + part, Shards(ring, w_down, down_rows // 2, down_rows, part * down_rows // 2))
-        for part in range(2)
-    ]
-
-    def down_step(step):
-        for gather in get_down:
-            gather.step(step)
-
-    def down_finish():
-        for gather in get_down:
-            gather.finish()
-
-    reach = ring.reach
+    get_attn = gather_of(1, Shards(ring, w_attn, attn_rows))
+
+    lent_rows = up_rows
+    kept_up = hidden_units - width
+    kept_down = down_rows - lent_rows
+    home = (
+        Shards(ring, w_up, lent_rows, first=kept_up, columns=width),
+        Shards(ring, w_down, lent_rows, down_rows, kept_down),
+    )
+    relay = Relay(
+        Shards(ring, g_down, 2 * lent_rows),
+        home,
+        [Shards(ring, g_down, lent_rows, 2 * lent_rows, part * lent_rows) for part in range(2)],
+        gather_sems.at[5, 0],
+        gather_ways.at[5],
+        relay_sems,
+    )
+    pieces = [Pieces(home[part], gather_sems.at[6, part], gather_sems.at[7, part]) for part in range(2)]
+
+    def gathers_of(rows, columns):
+        cut = (rows // 2 + 15) // 16 * 16
+        up = gather_of(2, Shards(ring, w_up, up_rows, columns=columns))
+        down = [
+            gather_of(3, Shards(ring, w_down, cut, down_rows)),
+            gather_of(4, Shards(ring, w_down, rows - cut, down_rows, cut)),
+        ]
+        return up, down
+
+    first_up, first_down = gathers_of(kept_down, kept_up)
+    last_up, last_down = gathers_of(down_rows, hidden_units)
+
+    def each(gathers, call, *values):
+        for gather in gathers:
+            getattr(gather, call)(*values)
+
     get_vec.begin()
     get_attn.begin()
-    for step in range(1, reach + 1):
-        get_vec.step(step)
-        get_attn.step(step)
-        if step == reach // 2:
-            get_up.begin()
-    get_up.step(1)
-    for gather in get_down:
-        gather.begin()
+
+    @pl.when(first_section)
+    def _():
+        relay.lend()
+        first_up.begin()
+        for part in range(2):
+            pieces[part].share(0)
+        for step in range(1, reach + 1):
+            get_vec.step(step)
+            get_attn.step(step)
+            if step < reach:
+                first_up.step(step)
+            if step == reach - 1:
+                each(first_down, "begin")
+
+    @pl.when(last_section)
+    def _():
+        relay.borrow()
+        relay.begin()
+        for step in range(1, reach + 1):
+            get_vec.step(step)
+            get_attn.step(step)
+            if step == reach - 1:
+                last_up.begin()
+            relay.step(step)
+
     get_vec.finish()
     get_attn.finish()
 
-    late = []
-    for step in range(2, reach + 1):
-        late.append(partial(get_up.step, step))
-        late.append(partial(down_step, step - 1))
-    late.append(get_up.finish)
-    late_down = [partial(down_step, reach), down_finish]
-
     @pl.when(last_section)
     def _():
-        for call in late + late_down:
-            call()
+        last_up.step(1)
+        each(last_down, "begin")
+        for step in range(2, reach + 1):
+            last_up.step(step)
+            if step < reach:
+                each(last_down, "step", step - 1)
+        last_up.finish()
+
+    def first_up_done():
+        first_up.step(reach)
+        relay.take(0)
+        pieces[0].share_rest()
+        first_up.finish()
+        pieces[0].finish()
+
+    def first_pieces():
+        relay.take(1)
+        pieces[1].share_rest()
 
     for device in range(devices):
         params[:, device * vec_columns : (device + 1) * vec_columns] = tiles[
@@ -587,11 +688,35 @@
             load_tokens(micro).wait()
 
         def serve(point):
-            @pl.when(first_section & (micro == 0))
+            first_of, last_of = micro == 0, micro == micro_count - 1
+
+            @pl.when(first_section & first_of)
             def _():
-                split = [late[0:2], late[2:4], late[4:], []]
-                for call in split[point]:
-                    call()
+                if point == 0:
+                    first_up_done()
+                if point == 2:
+                    for step in range(1, reach - 2):
+                        each(first_down, "step", step)
+                    first_pieces()
+
+            @pl.when(first_section & last_of)
+            def _():
+                if point == 0:
+                    each(first_down, "step", reach - 2)
+                if point == 2:
+                    each(first_down, "step", reach - 1)
+                if point == 3:
+                    each(first_down, "step", reach)
+
+            @pl.when(last_section & first_of)
+            def _():
+                if point == 2:
+                    each(last_down, "step", reach - 1)
+
+            @pl.when(last_section & last_of)
+            def _():
+                if point == 0:
+                    each(last_down, "step", reach)
 
         forward_micro(micro, serve)
         return 0
@@ -600,8 +725,12 @@
 
     @pl.when(first_section)
     def _():
-        for call in late_down:
-            call()
+        each(first_down, "finish")
+        pieces[1].finish()
+
+    @pl.when(last_section)
+    def _():
+        each(last_down, "finish")
 
     def finish_step(micro, _):
         here = rows_of(micro)
@@ -615,13 +744,23 @@
         return 0
 
     lax.fori_loop(0, micro_count, finish_step, 0)
-    for gather in (get_vec, get_attn, get_up, *get_down):
-        gather.drain()
+    each((get_vec, get_attn), "drain")
+
+    @pl.when(first_section)
+    def _():
+        each((first_up, *first_down, *pieces), "drain")
+        relay.drain_lent()
+
+    @pl.when(last_section)
+    def _():
+        each((last_up, *last_down, relay), "drain")
+
     pltpu.make_async_copy(boundary, boundary_out, local.at[0]).start()
 
 
-    def into(ref, first):
-        def put(rows, value):
+    def into(ref, first=0, row=0):
+        def put(start, value):
+            rows = pl.ds(pl.multiple_of(row + start, 8), value.shape[0])
             ref[rows, pl.ds(first, value.shape[1])] = value
 
         return put
@@ -639,17 +778,33 @@
             reduce_ways.at[index],
         )
 
-    put_down = reduce_of(
-        0, Shards(ring, g_down, down_rows), into(sum_down, 0), other_down, slots_down, block=64
-    )
-    put_up = reduce_of(
-        1, Shards(ring, w_up, own_up.shape[1]), into(sum_up, 0), other_up, slots_up
-    )
-    half_attn = w_attn.shape[1] // 2
+    half_down = down_rows // 2
+    put_down = [
+        reduce_of(
+            part,
+            Shards(ring, g_down, half_down, down_rows, part * half_down),
+            into(sum_down, row=part * half_down),
+            other_down.at[part],
+            slots_down.at[part],
+            block=half_down // 2,
+        )
+        for part in range(2)
+    ]
+    half_up, half_attn = hidden_units // 2, w_attn.shape[1] // 2
+    put_up = [
+        reduce_of(
+            2 + part,
+            Shards(ring, w_up, up_rows, first=part * half_up, columns=half_up),
+            into(sum_up, part * half_up),
+            other_up.at[part],
+            slots_up.at[part],
+        )
+        for part in range(2)
+    ]
     put_attn = [
         reduce_of(
-            2 + part,
-            Shards(ring, w_attn, own_attn.shape[1], first=part * half_attn, columns=half_attn),
+            4 + part,
+            Shards(ring, w_attn, attn_rows, first=part * half_attn, columns=half_attn),
             into(sum_attn, part * half_attn),
             other_attn.at[part],
             slots_attn.at[part],
@@ -657,7 +812,7 @@
         for part in range(2)
     ]
     put_vec = reduce_of(
-        4, Shards(ring, vec_tiles, 16), into(sum_vec, 0), other_vec, slots_vec, False
+        6, Shards(ring, vec_tiles, 16), into(sum_vec), other_vec, slots_vec, False
     )
 
     chunk = 2 * down_rows
@@ -668,14 +823,14 @@
         g_down[pl.ds(pl.multiple_of(start, 16), chunk), :] = dot_tn(
             active[:, columns], dy_in[...]
         ).astype(BF16)
-        put_down.swap(distance)
+        each(put_down, "swap", distance)
 
     def start_down():
-        for index, (distance, _) in enumerate(put_down.keys()):
+        for index, (distance, _) in enumerate(put_down[0].keys()):
             weigh_down(distance)
             if index == 1:
-                put_down.first()
-        put_down.step(reach - 1)
+                each(put_down, "first")
+        each(put_down, "step", reach - 1)
 
     def add_vec(row, value):
         vec_sums[row : row + 1, :] += value
@@ -763,10 +918,10 @@
             @pl.when(first_section & is_last)
             def _():
                 if point == 1:
-                    put_down.step(reach - 2)
+                    each(put_down, "step", reach - 2)
                 if point == 3:
                     for distance in range(reach - 3, 0, -1):
-                        put_down.step(distance)
+                        each(put_down, "step", distance)
 
         @pl.when(first_section & is_last)
         def _():
@@ -788,6 +943,15 @@
     @pl.when(last_section)
     def _():
         start_down()
+
+    def squares(ref):
+        value = ref[...]
+        value = value * value
+        while value.shape[1] > 128:
+            value = sum(
+                value[:, start : start + 128] for start in range(0, value.shape[1], 128)
+            )
+        return sum(value[start : start + 8, :] for start in range(0, value.shape[0], 8))
 
     third = width // 3
 
@@ -802,13 +966,13 @@
         lax.fori_loop(0, 3, body, 0)
 
     weigh(hidden_two, grad_up, w_up, 0)
-    put_up.exchange()
+    each(put_up, "exchange")
 
     @pl.when(last_section)
     def _():
-        put_down.step(reach - 2)
-
-    put_up.first()
+        each(put_down, "step", reach - 2)
+
+    each(put_up, "first")
     vec_tiles[...] = jnp.zeros_like(vec_tiles)
     for device in range(devices):
         vec_tiles[device * 16 : (device + 1) * 16, 0:vec_columns] = vec_sums[
@@ -823,38 +987,26 @@
     @pl.when(last_section)
     def _():
         for distance in range(reach - 3, 0, -1):
-            put_down.step(distance)
+            each(put_down, "step", distance)
 
     put_vec.first()
-    put_up.step(reach - 1)
-    put_down.last()
-    for part in range(2):
-        put_attn[part].first()
-    put_up.step(reach - 2)
+    each(put_up, "step", reach - 1)
+    each(put_down, "last")
+    each(put_attn, "first")
     put_vec.step(reach - 1)
-    for part in range(2):
-        put_attn[part].step(reach - 1)
+    each(put_up, "step", reach - 2)
+    each(put_attn, "step", reach - 1)
     for distance in range(reach - 2, 0, -1):
+        put_vec.step(distance)
         if distance > 1:
-            put_up.step(distance - 1)
+            each(put_up, "step", distance - 1)
         else:
-            put_up.last()
-        put_vec.step(distance)
-        for part in range(2):
-            put_attn[part].step(distance)
+            each(put_up, "last")
+        each(put_attn, "step", distance)
     put_vec.last()
-    for part in range(2):
-        put_attn[part].last()
-
-
-    def squares(ref):
-        value = ref[...]
-        value = value * value
-        while value.shape[1] > 128:
-            value = sum(
-                value[:, start : start + 128] for start in range(0, value.shape[1], 128)
-            )
-        return sum(value[start : start + 8, :] for start in range(0, value.shape[0], 8))
+    norm_slots[0] = squares(sum_up) + squares(sum_down) + squares(sum_vec)
+    each(put_attn, "last")
+
 
     total_devices = sections * devices
     flat = section * devices + me
@@ -863,7 +1015,7 @@
         other = (flat + distance) % total_devices
         return (other // devices, other % devices)
 
-    norm_slots[0] = squares(sum_attn) + squares(sum_up) + squares(sum_down) + squares(sum_vec)
+    norm_slots[0] += squares(sum_attn)
 
     def tell(distance, _):
         remote(
@@ -889,8 +1041,7 @@
     heard.wait_send()
 
 
-    for reduce in (put_down, put_up, *put_attn, put_vec):
-        reduce.drain()
+    each((*put_down, *put_up, *put_attn, put_vec), "drain")
     pltpu.make_async_copy(boundary, boundary_out, local.at[0]).wait()
     copy_input_grads.wait()
     for micro in range(micro_count):
@@ -949,20 +1100,21 @@
         pltpu.VMEM((16, width), F32),
         pltpu.VMEM((devices * 16, 128), F32),
         pltpu.VMEM((hidden_units, width), BF16),
-        other(down_rows, width),
-        other(up_rows, hidden_units),
+        pltpu.VMEM((2, chips, down_rows // 2, width), BF16),
+        pltpu.VMEM((2, chips, up_rows, hidden_units // 2), BF16),
         pltpu.VMEM((2, chips, attn_rows, attn.shape[2] // 2), BF16),
         other(16, 128, F32),
-        slots(down_rows, width),
-        slots(up_rows, hidden_units),
+        pltpu.VMEM((2, 2, reach, down_rows // 2, width), BF16),
+        pltpu.VMEM((2, 2, reach, up_rows, hidden_units // 2), BF16),
         pltpu.VMEM((2, 2, reach, attn_rows, attn.shape[2] // 2), BF16),
         slots(16, 128, F32),
         pltpu.VMEM((sections * devices, 8, 128), F32),
         pltpu.SemaphoreType.DMA((5 + micro_count,)),
-        pltpu.SemaphoreType.DMA((5, 2)),
-        pltpu.SemaphoreType.DMA((5, 2, reach)),
-        pltpu.SemaphoreType.DMA((5, 3)),
-        pltpu.SemaphoreType.DMA((5, 2, reach)),
+        pltpu.SemaphoreType.DMA((8, 2)),
+        pltpu.SemaphoreType.DMA((6, 2, reach)),
+        pltpu.SemaphoreType.DMA((3,)),
+        pltpu.SemaphoreType.DMA((7, 3)),
+        pltpu.SemaphoreType.DMA((7, 2, reach)),
         pltpu.SemaphoreType.DMA((2, micro_count)),
         pltpu.SemaphoreType.DMA((2,)),
     ]

time: 234 us -> 216 us (0.923)
  Pallas kernels: 233 us -> 215 us
    pallas_call x1, Pallas kernels: 226 us -> 208 us  [run_layers(): pl.pallas_call(partial(layer_kernel, devices, sections), out_shape=[jax.S...]
where the time goes in v4:
time: 216 us
  Pallas kernels  215 us (100%)
    pallas_call x1, Pallas kernels, run_layers(): pl.pallas_call(partial(layer_kernel, devices, sections), out_shape=[jax.S...  208 us
    pallas_call x1, Pallas kernels, run_adam(): pl.pallas_call(adam_kernel, grid=(steps,), out_shape=[jax.ShapeDtypeStruc...  6.84 us

profile of v4, /device:TPU:0, one launch (start us, length us, event | category | flops | bytes accessed | tf_op | source)
XLA Modules:
  0.0 215.9 jit_solution(4493604048501557063)
XLA Ops:
  0.6 208.2 %two_layers.1 = (bf16[2,224,768]{2,1,0:T(8,128)(2,1)}, bf16[2,224,768]{2,1,0:T(8,128)(2,1)}, f32[48,3072]{1,0:T(8,128)}, f32[48,3072]{1,0:T(8,128)}, f32[192,768...) custom-call(bf16[2,224,768]{2,1,0:T(8,128)(2,1)} %tokens.1, bf16[2,224,768]{2,1,0:T(8,128)(2,1)} %cotangent.1, ...), custom_call_target="tpu_custom_call" | custom-call | tf_op jit(solution)/shard_map/two_layers/pallas_call | solution.py:1121
  208.8 6.8 %adam.1 = (bf16[2,224,768]{2,1,0:T(8,128)(2,1)}, bf16[2,224,768]{2,1,0:T(8,128)(2,1)}, f32[1,1]{1,0:T(1,128)}, f32[1,48,3072]{2,1,0:T(8,128)}, f32[1,48,3072]{2,...) custom-call(bf16[2,224,768]{2,1,0:T(8,128)(2,1)} %get-tuple-element., ...), custom_call_target="tpu_custom_call" | custom-call | tf_op jit(solution)/shard_map/adam/pallas_call | solution.py:1207

commit v5 on v4

--- a/solution.py
+++ b/solution.py
@@ -19,7 +19,7 @@
 ADAM_EPS = 1e-08
 MAX_NORM = 1.0
 MESH = pl.DeviceIdType.MESH
-VMEM_LIMIT = 60 * 2**20
+VMEM_LIMIT = 61 * 2**20
 F32 = jnp.float32
 BF16 = jnp.bfloat16
 
@@ -236,8 +236,12 @@
         semaphore = self.swapped.at[0 if first else 1]
         remote(slots, slots, self.sent, semaphore, self.ring.sibling()).wait_recv()
 
+    def slot_number(self, way, distance):
+        reach = self.ring.reach
+        return distance - 1 if way == 0 or distance == reach else reach + distance - 1
+
     def slot(self, way, distance):
-        ref = self.slots.at[way, distance - 1]
+        ref = self.slots.at[self.slot_number(way, distance)]
         if distance == self.ring.reach and self.halves:
             columns = ref.shape[1] // 2
             return ref.at[:, pl.ds(way * columns, columns)]
@@ -278,15 +282,16 @@
             rows = pl.ds(pl.multiple_of(index * block, block), block)
             total = shards.whole[here, columns].astype(F32) + self.other[key, rows, :].astype(F32)
             for way, far in arrivals:
+                slot = self.slot_number(way, far)
                 if far == ring.reach and self.halves:
                     low, high = total[:, :half], total[:, half:]
                     if way == 0:
-                        low = low + self.slots[way, far - 1, rows, :half].astype(F32)
+                        low = low + self.slots[slot, rows, :half].astype(F32)
                     else:
-                        high = high + self.slots[way, far - 1, rows, half:].astype(F32)
+                        high = high + self.slots[slot, rows, half:].astype(F32)
                     total = jnp.concatenate([low, high], axis=1)
                 elif far < ring.reach or way == 0:
-                    total = total + self.slots[way, far - 1, rows, :].astype(F32)
+                    total = total + self.slots[slot, rows, :].astype(F32)
             if final:
                 self.put(index * block, total)
             else:
@@ -375,11 +380,15 @@
     own_vec_in,
     boundary_out,
     input_grads_out,
+    sum_attn_out,
+    sum_up_out,
+    sum_down_out,
+    sum_vec_out,
+    norm,
     sum_attn,
     sum_up,
     sum_down,
     sum_vec,
-    norm,
     crops,
     own_vec,
     boundary,
@@ -437,8 +446,6 @@
     hidden_units = w_up.shape[1]
     tiles_up = hidden_units // width
     head_width = width // HEADS
-    pairs = HEADS // 2
-    unroll = 3
     pair_width = 2 * head_width
     head_scale = head_width ** (-0.5)
     vec_rows, vec_columns = own_vec.shape[0], own_vec.shape[2]
@@ -488,18 +495,13 @@
 
     vec_tiles[...] = jnp.zeros_like(vec_tiles)
     vec_sums[...] = jnp.zeros_like(vec_sums)
-    for load in loads:
-        load.wait()
+    load_attn, load_up, load_down, load_vec, load_crops = loads
+    load_vec.wait()
     vec_tiles[0:vec_rows, 0:vec_columns] = own_vec[:, 0, :]
     tiles[pl.ds(pl.multiple_of(me * 16, 16), 16), :] = vec_tiles[0:16, :].astype(BF16)
+    load_attn.wait()
     count = own_attn.shape[1]
-    here = pl.ds(pl.multiple_of(me * count, 16), count)
-    w_attn[here, :] = stage_attn[...].astype(BF16)
-    count = own_up.shape[1]
-    w_up[pl.ds(pl.multiple_of(me * count, 16), count), :] = stage_up[...].astype(BF16)
-    count = own_down.shape[1]
-    w_down[pl.ds(pl.multiple_of(me * count, 16), count), :] = stage_down[...].astype(BF16)
-
+    w_attn[pl.ds(pl.multiple_of(me * count, 16), count), :] = stage_attn[...].astype(BF16)
     pl.semaphore_wait(barrier, len(neighbours))
 
 
@@ -552,6 +554,13 @@
 
     get_vec.begin()
     get_attn.begin()
+    load_up.wait()
+    count = own_up.shape[1]
+    w_up[pl.ds(pl.multiple_of(me * count, 16), count), :] = stage_up[...].astype(BF16)
+    load_down.wait()
+    count = own_down.shape[1]
+    w_down[pl.ds(pl.multiple_of(me * count, 16), count), :] = stage_down[...].astype(BF16)
+    load_crops.wait()
 
     @pl.when(first_section)
     def _():
@@ -633,25 +642,24 @@
             qkv[here, part * width : (part + 1) * width] = value.astype(BF16)
         serve(0)
 
-        def pair(index, _):
-            at = index * pair_width
-            queries = qkv[here, lanes(at, pair_width)]
-            keys = qkv[here, lanes(width + at, pair_width)]
-            values = qkv[here, lanes(2 * width + at, pair_width)]
-            scores = [dot_nt(keys, of_head(queries, sub)) for sub in range(2)]
-            outs = []
-            for sub in range(2):
-                value = jnp.where(mask[micro] > 0.5, scores[sub] * head_scale, NEG_BIG)
-                peak = jnp.max(value, axis=0, keepdims=True)
-                exponent = jnp.exp(value - peak)
-                totals = jnp.sum(exponent, axis=0, keepdims=True)
-                probs = (exponent * (1.0 / totals)).astype(BF16)
-                log_total[pl.ds(micro * HEADS + 2 * index + sub, 1), :] = peak + jnp.log(totals)
-                outs.append(dot_tn(probs, values))
-            mixed[here, lanes(at, pair_width)] = jnp.where(in_low, outs[0], outs[1]).astype(BF16)
-            return 0
-
-        lax.fori_loop(0, pairs, pair, 0, unroll=unroll)
+        same = mask[micro] > 0.5
+        loaded, scores, probs, outs = [], [], [], []
+        for at in range(0, width, pair_width):
+            loaded.append([qkv[here, part * width + at : part * width + at + pair_width] for part in range(3)])
+        for queries, keys, _ in loaded:
+            scores.append([dot_nt(keys, of_head(queries, sub)) for sub in range(2)])
+        for head in range(HEADS):
+            value = jnp.where(same, scores[head // 2][head % 2] * head_scale, NEG_BIG)
+            peak = jnp.max(value, axis=0, keepdims=True)
+            exponent = jnp.exp(value - peak)
+            totals = jnp.sum(exponent, axis=0, keepdims=True)
+            probs.append((exponent * (1.0 / totals)).astype(BF16))
+            log_total[micro, head : head + 1, :] = peak + jnp.log(totals)
+        for index in range(HEADS // 2):
+            low, high = (dot_tn(probs[2 * index + sub], loaded[index][2]) for sub in range(2))
+            outs.append(jnp.where(in_low, low, high).astype(BF16))
+        for index, value in enumerate(outs):
+            mixed[here, index * pair_width : (index + 1) * pair_width] = value
         serve(1)
         middle_value = x_in[here, :].astype(F32) + (
             dot_nn(mixed[here, :], w_attn[:, 3 * width :]) + params[4:5, :]
@@ -862,45 +870,52 @@
         grad_heads[...] = dot_nt(back, w_attn[:, 3 * width :]).astype(BF16)
         serve(1)
 
-        def pair(index, _):
-            at = index * pair_width
-            queries = qkv[here, lanes(at, pair_width)]
-            keys = qkv[here, lanes(width + at, pair_width)]
-            values = qkv[here, lanes(2 * width + at, pair_width)]
-            back_out = grad_heads[:, lanes(at, pair_width)]
-            scores = [dot_nt(keys, of_head(queries, sub)) for sub in range(2)]
-            back_probs = [dot_nt(values, of_head(back_out, sub)) for sub in range(2)]
-            results = []
-            for sub in range(2):
-                value = jnp.where(mask[micro] > 0.5, scores[sub] * head_scale, NEG_BIG)
-                probs = jnp.exp(
-                    value - log_total[pl.ds(micro * HEADS + 2 * index + sub, 1), :]
+        same = mask[micro] > 0.5
+        loaded, scores, back_probs, mids, results = [], [], [], [], []
+        for at in range(0, width, pair_width):
+            loaded.append(
+                [qkv[here, part * width + at : part * width + at + pair_width] for part in range(3)]
+                + [grad_heads[:, at : at + pair_width]]
+            )
+        for queries, keys, values, back_out in loaded:
+            scores.append([dot_nt(keys, of_head(queries, sub)) for sub in range(2)])
+            back_probs.append([dot_nt(values, of_head(back_out, sub)) for sub in range(2)])
+        for head in range(HEADS):
+            value = jnp.where(same, scores[head // 2][head % 2] * head_scale, NEG_BIG)
+            probs = jnp.exp(value - log_total[micro, head : head + 1, :])
+            back = back_probs[head // 2][head % 2]
+            inner = jnp.sum(back * probs, axis=0, keepdims=True)
+            mids.append(((probs * (back - inner)).astype(BF16), probs.astype(BF16)))
+        for index, (queries, keys, _, back_out) in enumerate(loaded):
+            heads = [
+                (
+                    dot_tn(back_scores, keys) * head_scale,
+                    dot_nn(back_scores, queries) * head_scale,
+                    dot_nn(probs, back_out),
                 )
-                inner = jnp.sum(back_probs[sub] * probs, axis=0, keepdims=True)
-                back_scores = (probs * (back_probs[sub] - inner)).astype(BF16)
-                results.append(
-                    (
-                        dot_tn(back_scores, keys) * head_scale,
-                        dot_nn(back_scores, queries) * head_scale,
-                        dot_nn(probs.astype(BF16), back_out),
-                    )
-                )
+                for back_scores, probs in mids[2 * index : 2 * index + 2]
+            ]
+            results.append(
+                [jnp.where(in_low, heads[0][part], heads[1][part]).astype(BF16) for part in range(3)]
+            )
+        for index, values in enumerate(results):
             for part in range(3):
-                grad_qkv[here, lanes(part * width + at, pair_width)] = jnp.where(
-                    in_low, results[0][part], results[1][part]
-                ).astype(BF16)
-            return 0
-
-        lax.fori_loop(0, pairs, pair, 0, unroll=unroll)
+                at = part * width + index * pair_width
+                grad_qkv[here, at : at + pair_width] = values[part]
         serve(2)
         e = dot_nt(grad_qkv[here, :], w_attn[:, : 3 * width])
         z, scale = norm_parts(x_in[here, :].astype(F32))
+        back = flow_two[...] + norm_back(z, scale, e, params[0:1, :])
+        input_grads[micro] = back.astype(BF16)
+
+        @pl.when(last_section)
+        def _():
+            hand_over(input_grads, dy_in, micro).start()
+
         add_vec(0, column_sum(e * z))
         add_vec(1, column_sum(e))
         add_vec(2, column_sum(grad_qkv[here, 0:width].astype(F32)))
         add_vec(3, column_sum(grad_qkv[here, 2 * width : 3 * width].astype(F32)))
-        back = flow_two[...] + norm_back(z, scale, e, params[0:1, :])
-        input_grads[micro] = back.astype(BF16)
         serve(3)
 
     def backward_step(micro, _):
@@ -928,11 +943,6 @@
             start_down()
 
         backward_micro(micro, serve)
-
-        @pl.when(last_section)
-        def _():
-            hand_over(input_grads, dy_in, micro).start()
-
         return 0
 
     lax.fori_loop(0, micro_count, backward_step, 0)
@@ -1004,6 +1014,14 @@
             each(put_up, "last")
         each(put_attn, "step", distance)
     put_vec.last()
+    leaving = [
+        pltpu.make_async_copy(source, target, local.at[2 + index])
+        for index, (source, target) in enumerate(
+            ((sum_up, sum_up_out), (sum_down, sum_down_out), (sum_vec, sum_vec_out))
+        )
+    ]
+    for copy in leaving:
+        copy.start()
     norm_slots[0] = squares(sum_up) + squares(sum_down) + squares(sum_vec)
     each(put_attn, "last")
 
@@ -1028,6 +1046,8 @@
         return 0
 
     lax.fori_loop(1, total_devices, tell, 0)
+    leaving.append(pltpu.make_async_copy(sum_attn, sum_attn_out, local.at[5]))
+    leaving[-1].start()
     rest = norm_slots.at[pl.ds(1, total_devices - 1)]
     heard = remote(rest, rest, norm_sem.at[0], norm_sem.at[1], other_device(1))
     heard.wait_recv()
@@ -1044,6 +1064,8 @@
     each((*put_down, *put_up, *put_attn, put_vec), "drain")
     pltpu.make_async_copy(boundary, boundary_out, local.at[0]).wait()
     copy_input_grads.wait()
+    for copy in leaving:
+        copy.wait()
     for micro in range(micro_count):
 
         @pl.when(first_section)
@@ -1062,15 +1084,18 @@
     hidden_units = upward_w.shape[2]
     attn_rows, up_rows, down_rows = attn.shape[1], upward_w.shape[1], downward_w.shape[1]
     in_hbm = pl.BlockSpec(memory_space=pl.ANY)
-    in_vmem = pl.BlockSpec(memory_space=pltpu.VMEM)
 
     def other(rows_of_shard, columns, kind=BF16):
         return pltpu.VMEM((chips, rows_of_shard, columns), kind)
 
     def slots(rows_of_shard, columns, kind=BF16):
-        return pltpu.VMEM((2, reach, rows_of_shard, columns), kind)
+        return pltpu.VMEM((2 * reach - 1, rows_of_shard, columns), kind)
 
     scratch = [
+        pltpu.VMEM(attn.shape[1:], F32),
+        pltpu.VMEM(upward_w.shape[1:], F32),
+        pltpu.VMEM(downward_w.shape[1:], F32),
+        pltpu.VMEM((16, 128), F32),
         pltpu.VMEM(crop_ids.shape, jnp.int32),
         pltpu.VMEM(vectors.shape, F32),
         pltpu.VMEM(tokens.shape, BF16),
@@ -1083,7 +1108,7 @@
         pltpu.VMEM((rows, width), BF16),
         pltpu.VMEM((rows, width), BF16),
         pltpu.VMEM((rows, 3 * width), BF16),
-        pltpu.VMEM((micro_count * HEADS, pack), F32),
+        pltpu.VMEM((micro_count, HEADS, pack), F32),
         pltpu.VMEM((rows, width), BF16),
         pltpu.VMEM((rows, width), F32),
         pltpu.VMEM((rows, width), BF16),
@@ -1104,9 +1129,9 @@
         pltpu.VMEM((2, chips, up_rows, hidden_units // 2), BF16),
         pltpu.VMEM((2, chips, attn_rows, attn.shape[2] // 2), BF16),
         other(16, 128, F32),
-        pltpu.VMEM((2, 2, reach, down_rows // 2, width), BF16),
-        pltpu.VMEM((2, 2, reach, up_rows, hidden_units // 2), BF16),
-        pltpu.VMEM((2, 2, reach, attn_rows, attn.shape[2] // 2), BF16),
+        pltpu.VMEM((2, 2 * reach - 1, down_rows // 2, width), BF16),
+        pltpu.VMEM((2, 2 * reach - 1, up_rows, hidden_units // 2), BF16),
+        pltpu.VMEM((2, 2 * reach - 1, attn_rows, attn.shape[2] // 2), BF16),
         slots(16, 128, F32),
         pltpu.VMEM((sections * devices, 8, 128), F32),
         pltpu.SemaphoreType.DMA((5 + micro_count,)),
@@ -1130,7 +1155,7 @@
             jax.ShapeDtypeStruct((1, 1), F32),
         ],
         in_specs=[in_hbm] * 7,
-        out_specs=[in_hbm] * 2 + [in_vmem] * 4 + [pl.BlockSpec(memory_space=pltpu.SMEM)],
+        out_specs=[in_hbm] * 6 + [pl.BlockSpec(memory_space=pltpu.SMEM)],
         scratch_shapes=scratch,
         compiler_params=pltpu.CompilerParams(
             collective_id=0, has_side_effects=True, vmem_limit_bytes=VMEM_LIMIT
@@ -1141,81 +1166,79 @@
 
 def adam_kernel(boundary, input_grads, norm, *refs):
     grads, states, out_boundary, out_input, out_norm = refs[:4], refs[4:16], *refs[16:19]
-    results, held, passing = refs[19:31], refs[31], refs[32]
-    step = pl.program_id(0)
+    results, held, held_grads, held_states = refs[19:31], refs[31], refs[32:36], refs[36:48]
+    fetching, leaving = refs[48:]
     take = [
-        pltpu.make_async_copy(source, held.at[i], passing.at[i])
+        pltpu.make_async_copy(source, held.at[i], fetching.at[i])
         for i, source in enumerate((boundary, input_grads))
     ]
     hand_on = [
-        pltpu.make_async_copy(held.at[i], target, passing.at[i])
+        pltpu.make_async_copy(held.at[i], target, leaving.at[i])
         for i, target in enumerate((out_boundary, out_input))
     ]
-
-    @pl.when(step == 0)
-    def _():
-        for copy in take:
+    order = (0, 1, 2, 3)
+
+    def fetches(index):
+        copies = [pltpu.make_async_copy(grads[index], held_grads[index], fetching.at[2 + index])]
+        for part in range(3):
+            at = index + 4 * part
+            copies.append(pltpu.make_async_copy(states[at], held_states[at], fetching.at[6 + at]))
+        return copies
+
+    def leave(at):
+        return pltpu.make_async_copy(held_states[at], results[at], leaving.at[2 + at])
+
+    for index in order:
+        for copy in fetches(index):
             copy.start()
-        out_norm[0, 0] = norm[0, 0]
-
-    @pl.when(step == 1)
-    def _():
-        for first, second in zip(take, hand_on):
-            first.wait()
-            second.start()
-
+    for copy in take:
+        copy.start()
+    out_norm[0, 0] = norm[0, 0]
     clip_factor = jnp.minimum(1.0, MAX_NORM / (jnp.full((1, 1), norm[0, 0]) + 1e-06))
-    for index in range(4):
-        master, moment_one, moment_two = (states[index + 4 * part] for part in range(3))
+    for index in order:
+        for copy in fetches(index):
+            copy.wait()
+        master, moment_one, moment_two = (held_states[index + 4 * part] for part in range(3))
         vectors = index == 3
         shape = (master.shape[0], master.shape[2]) if vectors else master.shape[1:]
-        gradient = grads[index][0 : shape[0], 0 : shape[1]] * clip_factor
+        gradient = held_grads[index][0 : shape[0], 0 : shape[1]] * clip_factor
         old = [ref[:, 0, :] if vectors else ref[0] for ref in (master, moment_one, moment_two)]
         decay, rate = (0.0, VECTOR_RATE) if vectors else (DECAY_RATE, RATE)
         updated = adam_update(old[0], gradient, old[1], old[2], decay, rate)
         for part in range(3):
+            at = index + 4 * part
             if vectors:
-                results[index + 4 * part][:, 0, :] = updated[part]
+                held_states[at][:, 0, :] = updated[part]
             else:
-                results[index + 4 * part][0] = updated[part]
-
-    @pl.when(step == pl.num_programs(0) - 1)
-    def _():
-        for copy in hand_on:
-            copy.wait()
+                held_states[at][0] = updated[part]
+            leave(at).start()
+    for first, second in zip(take, hand_on):
+        first.wait()
+        second.start()
+    for at in range(12):
+        leave(at).wait()
+    for copy in hand_on:
+        copy.wait()
 
 
 def run_adam(boundary, input_grads, attn, upward_w, downward_w, vectors, norm, states):
     grads = (attn, upward_w, downward_w, vectors)
-    steps = 2
-
-    def cut(shape):
-        block = shape[:-2] + (shape[-2] // steps, shape[-1])
-        lead = (0,) * (len(shape) - 2)
-        return pl.BlockSpec(block, lambda i: lead + (i, 0))
-
-    def keep(shape):
-        lead = (0,) * len(shape)
-        return pl.BlockSpec(shape, lambda i: lead)
-
-    def spec(index, array):
-        return keep(array.shape) if index % 4 == 3 else cut(array.shape)
-
     in_hbm = pl.BlockSpec(memory_space=pl.ANY)
     scalar = pl.BlockSpec(memory_space=pltpu.SMEM)
-    state_specs = [spec(i, a) for i, a in enumerate(states)]
     return pl.pallas_call(
         adam_kernel,
-        grid=(steps,),
         out_shape=[
             jax.ShapeDtypeStruct(boundary.shape, BF16),
             jax.ShapeDtypeStruct(input_grads.shape, BF16),
             jax.ShapeDtypeStruct((1, 1), F32),
         ]
         + [jax.ShapeDtypeStruct(a.shape, F32) for a in states],
-        in_specs=[in_hbm, in_hbm, scalar] + [spec(i, a) for i, a in enumerate(grads)] + state_specs,
-        out_specs=[in_hbm, in_hbm, scalar] + state_specs,
-        scratch_shapes=[pltpu.VMEM((2,) + boundary.shape, BF16), pltpu.SemaphoreType.DMA((2,))],
+        in_specs=[in_hbm, in_hbm, scalar] + [in_hbm] * 16,
+        out_specs=[in_hbm, in_hbm, scalar] + [in_hbm] * 12,
+        scratch_shapes=[pltpu.VMEM((2,) + boundary.shape, BF16)]
+        + [pltpu.VMEM(a.shape, F32) for a in grads]
+        + [pltpu.VMEM(a.shape, F32) for a in states]
+        + [pltpu.SemaphoreType.DMA((18,)), pltpu.SemaphoreType.DMA((14,))],
         compiler_params=pltpu.CompilerParams(vmem_limit_bytes=VMEM_LIMIT),
         name="adam",
     )(boundary, input_grads, norm, *grads, *states)
@@ -1407,6 +1430,7 @@
 def shards(devices, sections, tokens, cotangent, crop_ids, *states):
     whole_tiles = (
         devices % 8 == 0
+        and tokens.shape[1] % 32 == 0
         and all(state.shape[1] % 16 == 0 for state in states[:3])
         and states[2].shape[1] % 64 == 0
         and states[3].shape[1] <= 16

time: 216 us -> 210 us (0.972)
  Pallas kernels: 215 us -> 209 us
    pallas_call x1, Pallas kernels: 208 us -> 202 us  [run_layers(): pl.pallas_call(partial(layer_kernel, devices, sections), out_shape=[jax.S...]
where the time goes in v5:
time: 210 us
  Pallas kernels  209 us (100%)
    pallas_call x1, Pallas kernels, run_layers(): pl.pallas_call(partial(layer_kernel, devices, sections), out_shape=[jax.S...  202 us
    pallas_call x1, Pallas kernels, run_adam(): pl.pallas_call(adam_kernel, out_shape=[jax.ShapeDtypeStruct(boundary.shap...  6.71 us

profile of v5, /device:TPU:0, one launch (start us, length us, event | category | flops | bytes accessed | tf_op | source)
XLA Modules:
  0.0 209.8 jit_solution(8538392664843043877)
XLA Ops:
  0.6 202.2 %two_layers.1 = (bf16[2,224,768]{2,1,0:T(8,128)(2,1)}, bf16[2,224,768]{2,1,0:T(8,128)(2,1)}, f32[48,3072]{1,0:T(8,128)}, f32[48,3072]{1,0:T(8,128)}, f32[192,768...) custom-call(bf16[2,224,768]{2,1,0:T(8,128)(2,1)} %tokens.1, bf16[2,224,768]{2,1,0:T(8,128)(2,1)} %cotangent.1, ...), custom_call_target="tpu_custom_call" | custom-call | tf_op jit(solution)/shard_map/two_layers/pallas_call | solution.py:1146
  202.9 6.7 %adam.1 = (bf16[2,224,768]{2,1,0:T(8,128)(2,1)}, bf16[2,224,768]{2,1,0:T(8,128)(2,1)}, f32[1,1]{1,0:T(1,128)}, f32[1,48,3072]{2,1,0:T(8,128)}, f32[1,48,3072]{2,...) custom-call(bf16[2,224,768]{2,1,0:T(8,128)(2,1)} %get-tuple-element., ...), custom_call_target="tpu_custom_call" | custom-call | tf_op jit(solution)/shard_map/adam/pallas_call | solution.py:1228

commit v6 on v5

--- a/solution.py
+++ b/solution.py
@@ -340,13 +340,8 @@
 
 
 def gelu_parts(value):
-    bell = jnp.exp(-0.5 * value * value)
-    t = 1.0 / (1.0 + (0.3275911 * 0.7071067811865476) * jnp.abs(value))
-    tail = 0.5 * 1.061405429
-    for factor in (-1.453152027, 1.421413741, -0.284496736, 0.254829592):
-        tail = tail * t + 0.5 * factor
-    tail = tail * t * bell
-    return jnp.where(value >= 0.0, 1.0 - tail, tail), bell * 0.3989422804014327
+    area = 0.5 + 0.5 * lax.erf(value * 0.7071067811865476)
+    return area, jnp.exp(-0.5 * value * value) * 0.3989422804014327
 
 
 def norm_parts(features):

time: 210 us -> 209 us (level)
  no operation moved by 1% of the time
where the time goes in v6:
time: 209 us
  Pallas kernels  208 us (100%)
    pallas_call x1, Pallas kernels, run_layers(): pl.pallas_call(partial(layer_kernel, devices, sections), out_shape=[jax.S...  201 us
    pallas_call x1, Pallas kernels, run_adam(): pl.pallas_call(adam_kernel, out_shape=[jax.ShapeDtypeStruct(boundary.shap...  6.71 us

profile of v6, /device:TPU:0, one launch (start us, length us, event | category | flops | bytes accessed | tf_op | source)
XLA Modules:
  0.0 208.5 jit_solution(3035844373398442379)
XLA Ops:
  0.6 201.0 %two_layers.1 = (bf16[2,224,768]{2,1,0:T(8,128)(2,1)}, bf16[2,224,768]{2,1,0:T(8,128)(2,1)}, f32[48,3072]{1,0:T(8,128)}, f32[48,3072]{1,0:T(8,128)}, f32[192,768...) custom-call(bf16[2,224,768]{2,1,0:T(8,128)(2,1)} %tokens.1, bf16[2,224,768]{2,1,0:T(8,128)(2,1)} %cotangent.1, ...), custom_call_target="tpu_custom_call" | custom-call | tf_op jit(solution)/shard_map/two_layers/pallas_call | solution.py:1141
  201.7 6.7 %adam.1 = (bf16[2,224,768]{2,1,0:T(8,128)(2,1)}, bf16[2,224,768]{2,1,0:T(8,128)(2,1)}, f32[1,1]{1,0:T(1,128)}, f32[1,48,3072]{2,1,0:T(8,128)}, f32[1,48,3072]{2,...) custom-call(bf16[2,224,768]{2,1,0:T(8,128)(2,1)} %get-tuple-element., ...), custom_call_target="tpu_custom_call" | custom-call | tf_op jit(solution)/shard_map/adam/pallas_call | solution.py:1223

commit v7 on v6

--- a/solution.py
+++ b/solution.py
@@ -740,13 +740,19 @@
         output = middle[here, :] + (dot_nn(active[here, :], w_down[...]) + params[7:8, :])
         boundary[micro] = output.astype(BF16)
 
-        @pl.when(first_section)
-        def _():
-            hand_over(boundary, x_in, micro).start()
-
+        hand_over(boundary, x_in, micro).start()
         return 0
 
-    lax.fori_loop(0, micro_count, finish_step, 0)
+    @pl.when(first_section)
+    def _():
+        lax.fori_loop(0, micro_count, finish_step, 0)
+
+    @pl.when(last_section)
+    def _():
+        output = middle[...] + (dot_nn(active[...], w_down[...]) + params[7:8, :])
+        for micro in range(micro_count):
+            boundary[micro] = output[micro * pack : (micro + 1) * pack, :].astype(BF16)
+
     each((get_vec, get_attn), "drain")
 
     @pl.when(first_section)

time: 209 us -> 209 us (level)
  no operation moved by 1% of the time
where the time goes in v7:
time: 209 us; the launch traced here: 208 us
  Pallas kernels  208 us (100%)
    pallas_call x1, Pallas kernels, run_layers(): pl.pallas_call(partial(layer_kernel, devices, sections), out_shape=[jax.S...  201 us
    pallas_call x1, Pallas kernels, run_adam(): pl.pallas_call(adam_kernel, out_shape=[jax.ShapeDtypeStruct(boundary.shap...  6.71 us

profile of v7, /device:TPU:0, one launch (start us, length us, event | category | flops | bytes accessed | tf_op | source)
XLA Modules:
  0.0 208.4 jit_solution(8897114397779292603)
XLA Ops:
  0.6 200.9 %two_layers.1 = (bf16[2,224,768]{2,1,0:T(8,128)(2,1)}, bf16[2,224,768]{2,1,0:T(8,128)(2,1)}, f32[48,3072]{1,0:T(8,128)}, f32[48,3072]{1,0:T(8,128)}, f32[192,768...) custom-call(bf16[2,224,768]{2,1,0:T(8,128)(2,1)} %tokens.1, bf16[2,224,768]{2,1,0:T(8,128)(2,1)} %cotangent.1, ...), custom_call_target="tpu_custom_call" | custom-call | tf_op jit(solution)/shard_map/two_layers/pallas_call | solution.py:1147
  201.5 6.7 %adam.1 = (bf16[2,224,768]{2,1,0:T(8,128)(2,1)}, bf16[2,224,768]{2,1,0:T(8,128)(2,1)}, f32[1,1]{1,0:T(1,128)}, f32[1,48,3072]{2,1,0:T(8,128)}, f32[1,48,3072]{2,...) custom-call(bf16[2,224,768]{2,1,0:T(8,128)(2,1)} %get-tuple-element., ...), custom_call_target="tpu_custom_call" | custom-call | tf_op jit(solution)/shard_map/adam/pallas_call | solution.py:1229
